TPU v7x, 32 devices: a whole 2x2x4 slice. The times are simulated.
32 devices in a mesh: wide: 8 (over z, y), narrow: 4 (over x, core).
Axes of the slice: x: 2, y: 2, z: 4, core: 2. Of those that a mesh axis runs over, the one named last changes fastest.
Arguments:
- residual_in: bfloat16 [16, 7168], P('wide', 'narrow'), may hold values from -2 to 2
- query_nope: bfloat16 [16, 64, 128], P('wide', 'narrow'), may hold values from -6 to 6
- query_rope: bfloat16 [16, 64, 64], P('wide', 'narrow'), may hold values from -8 to 8
- absorb_key: bfloat16 [64, 128, 512], P('narrow'), may hold values from -0.5 to 0.5
- absorb_value: bfloat16 [64, 512, 128], P('narrow'), may hold values from -0.25 to 0.25
- latent_cache: bfloat16 [16, 2048, 576], P('wide'), may hold values from -8 to 8
- cache_lengths: int32 [16], P('wide'), may hold values from 256 to 2048, as said below
- slot_rows: int32 [16], replicated, may hold values from 0 to 15, each once
- out_proj: bfloat16 [8192, 7168], P('wide', 'narrow'), may hold values from -0.0625 to 0.0625
- norm_gain: bfloat16 [7168], P('narrow'), may hold values from 0.25 to 1.75
- gate_weight: bfloat16 [7168, 18432], P('narrow', 'wide'), may hold values from -0.0625 to 0.0625
- up_weight: bfloat16 [7168, 18432], P('narrow', 'wide'), may hold values from -0.0625 to 0.0625
- down_weight: bfloat16 [18432, 7168], P('wide', 'narrow'), may hold values from -0.046875 to 0.046875
Outputs:
- residual_out: bfloat16 [16, 7168], P('wide', 'narrow')
Inputs may be any that keep to these rules, and one draw needn't show every extreme that they name: `cache_lengths`: every slot has at least 256 live positions; in every draw some slot is full. `slot_rows`: each batch row is named by exactly one slot.
All inputs are finite; a program needn't handle non-finite values.
Results may differ from a plain program's by a relative error of at most 0.009.
Values may be sent and summed in bfloat16 or wider, within the bound.
No kernel may reach another device: no remote copies, remote signals or barrier semaphores. Data moves between devices by JAX's collectives and lax.ppermute only.
A program may use at most 64 MiB of HBM per device.

v0:
```python
import math

import jax
import jax.numpy as jnp
from jax import lax
from jax.sharding import PartitionSpec as P

D = 7168


def shards(
    residual_in,
    query_nope,
    query_rope,
    absorb_key,
    absorb_value,
    latent_cache,
    cache_lengths,
    slot_rows,
    out_proj,
    norm_gain,
    gate_weight,
    up_weight,
    down_weight,
):
    slot_count = latent_cache.shape[0]
    head_size = query_nope.shape[2]
    latent_width = absorb_key.shape[2]
    group_index = lax.axis_index("wide")
    packed_queries = jnp.concatenate([query_nope, query_rope], axis=2)
    gathered = lax.all_gather(packed_queries, "wide", axis=0, tiled=True)
    my_rows = lax.dynamic_slice_in_dim(slot_rows, group_index * slot_count, slot_count)
    selected = jnp.take(gathered, my_rows, axis=0)
    query_latent = jnp.einsum(
        "rhd,hdc->rhc", selected[:, :, :head_size], absorb_key, preferred_element_type=jnp.float32
    ).astype(jnp.bfloat16)
    full_query = jnp.concatenate([query_latent, selected[:, :, head_size:]], axis=2)
    scale = 1.0 / math.sqrt(full_query.shape[2] - latent_width + head_size)
    scores = (
        jnp.einsum("rhc,rtc->rht", full_query, latent_cache, preferred_element_type=jnp.float32)
        * scale
    )
    positions = jnp.arange(latent_cache.shape[1], dtype=jnp.int32)
    live = positions[None, None, :] < cache_lengths[:, None, None]
    scores = jnp.where(live, scores, -jnp.inf)
    highest = jnp.max(scores, axis=2, keepdims=True)
    weights = jnp.where(live, jnp.exp(scores - highest), 0.0)
    probs = (weights / jnp.sum(weights, axis=2, keepdims=True)).astype(jnp.bfloat16)
    context = jnp.einsum("rht,rtc->rhc", probs, latent_cache, preferred_element_type=jnp.float32)
    context = context[:, :, :latent_width].astype(jnp.bfloat16)
    heads_out = jnp.einsum(
        "rhc,hcd->rhd", context, absorb_value, preferred_element_type=jnp.float32
    ).astype(jnp.bfloat16)
    every_head = lax.all_gather(heads_out, "narrow", axis=1, tiled=True)
    flat_heads = every_head.reshape(slot_count, -1)
    head_columns = lax.all_to_all(flat_heads, "wide", split_axis=1, concat_axis=0, tiled=True)
    inverse = jnp.argsort(slot_rows)
    attention = lax.psum_scatter(
        jnp.dot(
            jnp.take(head_columns, inverse, axis=0), out_proj, preferred_element_type=jnp.float32
        ),
        "wide",
        scatter_dimension=0,
        tiled=True,
    )
    middle = residual_in.astype(jnp.float32) + attention
    square_sum = lax.psum(jnp.sum(middle * middle, axis=1), "narrow")
    normed = (
        middle * lax.rsqrt(square_sum / D + 1e-06)[:, None] * norm_gain.astype(jnp.float32)
    ).astype(jnp.bfloat16)
    hidden_cols = gate_weight.shape[1]
    row_piece = lax.all_gather(normed, "wide", axis=0, tiled=True)
    local_terms = jnp.concatenate(
        [
            jnp.dot(row_piece, gate_weight, preferred_element_type=jnp.float32),
            jnp.dot(row_piece, up_weight, preferred_element_type=jnp.float32),
        ],
        axis=1,
    )
    summed = lax.psum(local_terms, "narrow")
    hidden = (jax.nn.silu(summed[:, :hidden_cols]) * summed[:, hidden_cols:]).astype(jnp.bfloat16)
    ffn_total = lax.psum_scatter(
        jnp.dot(hidden, down_weight, preferred_element_type=jnp.float32),
        "wide",
        scatter_dimension=0,
        tiled=True,
    )
    return (middle + ffn_total).astype(jnp.bfloat16)


def solution(mesh):
    in_specs = (
        P("wide", "narrow"),
        P("wide", "narrow", None),
        P("wide", "narrow", None),
        P("narrow", None, None),
        P("narrow", None, None),
        P("wide", None, None),
        P("wide"),
        P(),
        P("wide", "narrow"),
        P("narrow"),
        P("narrow", "wide"),
        P("narrow", "wide"),
        P("wide", "narrow"),
    )
    out_specs = P("wide", "narrow")
    return jax.shard_map(shards, mesh=mesh, in_specs=in_specs, out_specs=out_specs, check_vma=False)
```

profile of v0, /device:TPU:0, one launch (start us, length us, event | category | flops | bytes accessed | tf_op | source)
XLA Modules:
  0.0 302.9 jit_solution(1529226852834250976)
XLA Ops:
  6.5 0.0 copy-start
  6.5 0.9 compare_and_fusion
  7.4 0.7 pad_maximum_fusion.1
  8.2 32.3 %all_gather.9 = bf16[16,16,192]{2,1,0:T(8,128)(2,1)S(1)} all-gather(bf16[2,16,192]{2,1,0:T(8,128)(2,1)S(1)} %pad_maximum_fusion.1), channel_id=1, replica_groups=mesh['wide'=8,'narrow'=4] {'wide'}, dimensions={0}, use_global_device_ids=true | all-gather | bytes 110592 | tf_op jit(solution)/shard_map/all_gather | solution.py:31
  40.4 0.5 gather_fusion
  41.0 0.1 broadcast_select_fusion
  41.1 0.7 iota_compare_fusion
  41.8 0.0 copy-done
  41.8 0.4 fusion.21
  42.2 3.1 %fusion.4 = f32[2,16,2048]{2,1,0:T(8,128)S(1)} fusion(bf16[2,2048,576]{1,2,0:T(8,128)(2,1)} %param.18, pred[2,2048]{1,0:T(4,128)(4,1)S(1)} %iota_compare_fusion, bf16[2,16,64]{2,1,0:T(8,128)(2,1)S(1)} %slice.26, bf16[2,16,512]{2,1,0:T(8,128)(2,1)S(1)} %bitcast.23), kind=kOutput, calls=%fused_computation.7 | convolution fusion | flops 75702272 | bytes 5021696 | tf_op jit(solution)/shard_map/rhc,rtc->rht/dot_general | solution.py:40
  45.4 0.0 copy-start.3
  45.4 0.2 fusion.29
  45.6 0.0 copy-start.4
  45.6 0.0 copy-start.1
  45.6 0.0 copy-start.2
  45.6 3.7 %fusion.7 = bf16[2,16,576]{2,1,0:T(8,128)(2,1)S(1)} fusion(bf16[2,2048,576]{1,2,0:T(8,128)(2,1)} %param.18, f32[2,16]{1,0:T(2,128)S(1)} %fusion.29, f32[2,16,2048]{2,1,0:T(8,128)S(1)} %fusion.4, pred[2,2048]{1,0:T(4,128)(4,1)S(1)} %iota_compare_fusion), kind=kOutput, calls=%fused_computation.14 | convolution fusion | flops 75761696 | bytes 5021824 | tf_op jit(solution)/shard_map/rht,rtc->rhc/dot_general | solution.py:49
  49.3 2.0 fusion.5
  51.3 5.6 %all_gather.10 = bf16[2,64,128]{2,0,1:T(2,128)(2,1)} all-gather(bf16[2,16,128]{2,0,1:T(2,128)(2,1)S(1)} %fusion.5), channel_id=1, replica_groups=mesh['wide'=8,'narrow'=4] {'narrow'}, dimensions={1}, use_global_device_ids=true | all-gather | bytes 40960 | tf_op jit(solution)/shard_map/all_gather | solution.py:54
  57.0 5.5 %all-to-all-start = ((bf16[2,8,1024]{2,0,1:T(2,128)(2,1)}), bf16[2,8,1024]{2,0,1:T(2,128)(2,1)S(1)}, u32[]{:S(2)}, u32[]{:S(2)}) async-start(bf16[2,8,1024]{2,0,1:T(2,128)(2,1)} %bitcast.2), calls=%async_computation | async-start | bytes 65536 | tf_op jit(solution)/shard_map/all_to_all | solution.py:56
  62.5 0.0 all-reduce.8.cloned.1.call-start
  62.5 0.0 copy-done.3
  62.5 1.2 sort.17
  63.8 5.3 %all-to-all-done = bf16[2,8,1024]{2,0,1:T(2,128)(2,1)S(1)} async-done(((bf16[2,8,1024]{2,0,1:T(2,128)(2,1)}), bf16[2,8,1024]{2,0,1:T(2,128)(2,1)S(1)}, u32[]{:S(2)}, u32[]{:S(2)}) %all-to-all-start) | async-done | bytes 32800 | tf_op jit(solution)/shard_map/all_to_all | solution.py:56
  69.2 0.6 gather_fusion.1
  69.8 3.3 %fusion.16 = f32[16,1792]{1,0:T(8,128)} fusion(bf16[1024,1792]{1,0:T(8,128)(2,1)} %param.21, bf16[16,1024]{1,0:T(8,128)(2,1)S(1)} %gather_fusion.1, pred[16]{0:T(512)(128)(4,1)S(1)} %compare_and_fusion.1), kind=kOutput, calls=%fused_computation.24 | convolution fusion | flops 58736640 | bytes 3817488 | tf_op jit(solution)/shard_map/dot_general | solution.py:59
  73.1 0.0 all-reduce.8.cloned.1.call-update
  73.1 0.0 all-reduce.6.cloned.1.call-start
  73.2 0.0 copy-done.4
  73.2 0.6 dynamic-slice
  74.4 65.3 %all-reduce.8.cloned.1.call-done = f32[16,1792]{1,0:T(8,128)} async-done(((f32[16,1792]{1,0:T(8,128)}), f32[16,1792]{1,0:T(8,128)}) %all-reduce.8.cloned.1.call-update) | async-done | bytes 114704
  139.7 0.0 copy-done.1
  139.7 1.0 multiply_reduce_fusion
  140.7 0.0 copy-done.2
  140.7 5.7 %psum.14 = f32[2]{0:T(128)S(1)} all-reduce(f32[2]{0:T(128)S(1)} %multiply_reduce_fusion), channel_id=1, replica_groups=mesh['wide'=8,'narrow'=4] {'narrow'}, use_global_device_ids=true, to_apply=%region_5.6 | all-reduce | flops 2 | bytes 16 | tf_op jit(solution)/shard_map/psum | solution.py:67
  146.4 0.9 fusion.23
  147.3 30.6 %all-gather = bf16[8,2,1792]{2,1,0:T(2,128)(2,1)S(1)} all-gather(bf16[1,2,1792]{2,1,0:T(2,128)(2,1)S(1)} %fusion.23), channel_id=1, replica_groups=mesh['wide'=8,'narrow'=4] {'wide'}, dimensions={0}, use_global_device_ids=true | all-gather | bytes 64512 | tf_op jit(solution)/shard_map/all_gather | solution.py:72
  177.9 4.5 %fusion.31 = f32[16,2304]{1,0:T(8,128)S(1)} fusion(bf16[16,1792]{1,0:T(8,128)(2,1)S(1)} %reshape.59, bf16[1792,2304]{1,0:T(8,128)(2,1)} %param.24), kind=kOutput, calls=%fused_computation.53 | convolution fusion | flops 132120576 | bytes 8462336 | tf_op jit(solution)/shard_map/dot_general | solution.py:76
  182.4 4.5 %fusion.30 = f32[16,2304]{1,0:T(8,128)S(1)} fusion(bf16[16,1792]{1,0:T(8,128)(2,1)S(1)} %reshape.59, bf16[1792,2304]{1,0:T(8,128)(2,1)} %param.23), kind=kOutput, calls=%fused_computation.52 | convolution fusion | flops 132120576 | bytes 8462336 | tf_op jit(solution)/shard_map/dot_general | solution.py:75
  187.0 0.7 pad_maximum_fusion
  187.7 0.0 all-reduce.6.cloned.1.call-update
  187.8 0.0 all-reduce.10.cloned.1.call-start
  187.8 32.4 %all-reduce.6.cloned.1.call-done = f32[16,4608]{1,0:T(8,128)} async-done(((f32[16,4608]{1,0:T(8,128)}), f32[16,4608]{1,0:T(8,128)}) %all-reduce.6.cloned.1.call-update) | async-done | bytes 294928 | tf_op jit(solution)/shard_map/psum | solution.py:80
  220.2 5.4 %fusion.9 = f32[16,1792]{1,0:T(8,128)} fusion(bf16[2304,1792]{1,0:T(8,128)(2,1)} %param.25, f32[16,4608]{1,0:T(8,128)} %all-reduce.6.cloned.1.call-done), kind=kOutput, calls=%fused_computation.16 | convolution fusion | flops 132341760 | bytes 8667136 | tf_op jit(solution)/shard_map/dot_general | solution.py:83
  225.6 0.0 all-reduce.10.cloned.1.call-update
  225.6 69.3 %all-reduce.10.cloned.1.call-done = f32[16,1792]{1,0:T(8,128)} async-done(((f32[16,1792]{1,0:T(8,128)}), f32[16,1792]{1,0:T(8,128)}) %all-reduce.10.cloned.1.call-update) | async-done | bytes 114704
  294.9 1.5 fusion.20
  (13 shorter events, 0.1 us)
Async XLA Ops:
  6.5 35.3 %copy-start = (bf16[16,128,512]{2,1,0:T(8,128)(2,1)S(1)}, bf16[16,128,512]{2,1,0:T(8,128)(2,1)}, u32[]{:S(2)}) copy-start(bf16[16,128,512]{2,1,0:T(8,128)(2,1)} %param.16) | copy-start | bytes 6291460
  45.4 17.2 %copy-start.3 = (s32[16]{0:T(128)S(1)}, s32[16]{0:T(128)}, u32[]{:S(2)}) copy-start(s32[16]{0:T(128)} %param.20) | copy-start | bytes 196
  45.6 27.6 %copy-start.4 = (u32[32]{0:T(128)S(1)}, u32[32]{0:T(128)}, u32[]{:S(2)}) copy-start(u32[32]{0:T(128)} %constant.59) | copy-start | bytes 388
  45.6 94.2 %copy-start.1 = (bf16[2,1792]{1,0:T(2,128)(2,1)S(1)}, bf16[2,1792]{1,0:T(2,128)(2,1)}, u32[]{:S(2)}) copy-start(bf16[2,1792]{1,0:T(2,128)(2,1)} %param.13) | copy-start | bytes 21508
  45.6 95.1 %copy-start.2 = (bf16[1792]{0:T(1024)(128)(2,1)S(1)}, bf16[1792]{0:T(1024)(128)(2,1)}, u32[]{:S(2)}) copy-start(bf16[1792]{0:T(1024)(128)(2,1)} %param.22) | copy-start | bytes 10756
  57.0 12.2 %all-to-all-start = ((bf16[2,8,1024]{2,0,1:T(2,128)(2,1)}), bf16[2,8,1024]{2,0,1:T(2,128)(2,1)S(1)}, u32[]{:S(2)}, u32[]{:S(2)}) async-start(bf16[2,8,1024]{2,0,1:T(2,128)(2,1)} %bitcast.2), calls=%async_computation | async-start | bytes 65536 | tf_op jit(solution)/shard_map/all_to_all | solution.py:56
  62.5 77.2 %all-reduce.8.cloned.1.call-start = ((), (), s32[]{:S(2)}) async-start(), calls=%async_computation.2 | async-start | bytes 229376
  73.1 147.1 %all-reduce.6.cloned.1.call-start = ((), (), s32[]{:S(2)}) async-start(), calls=%async_computation.1 | async-start | bytes 589824 | tf_op jit(solution)/shard_map/psum | solution.py:80
  187.8 107.1 %all-reduce.10.cloned.1.call-start = ((), (), s32[]{:S(2)}) async-start(), calls=%async_computation.3 | async-start | bytes 229376
Sparse Core Ops, SparseCore 0:
  73.2 66.4 all-reduce.7
  187.9 32.2 all-reduce.5
  225.7 69.0 all-reduce.9
where the time goes:
time: 304 us; the launch traced here: 303 us
  waiting for transfers between devices  172 us (57%)
  blocking collectives  74.2 us (24%)
  matrix products  27 us (9%)
  between operations  13.9 us (5%)
  other arithmetic  7.97 us (3%)
  starting transfers between devices  5.64 us (2%)
    unnamed x5, waiting for transfers between devices  135 us
    psum x1, waiting for transfers between devices, shards(): summed = lax.psum(local_terms, 'narrow')  32.4 us
    all_gather x1, blocking collectives, shards(): gathered = lax.all_gather(packed_queries, 'wide', axis=0, tiled=True)  32.3 us
    all_gather x1, blocking collectives, shards(): row_piece = lax.all_gather(normed, 'wide', axis=0, tiled=True)  30.6 us
  transfers between devices with their start and end apart: 4, of which 4 were waited for; matrix products, arithmetic and copies ran while one was open for 1% of the time, Pallas kernels for 0%

commit v1 on v0

v1 whole, which is shorter than its diff:
```python
import functools
import math

import jax
import jax.numpy as jnp
from jax import lax
from jax.experimental import pallas as pl
from jax.experimental.pallas import tpu as pltpu
from jax.sharding import PartitionSpec as P

D = 7168
BF16 = jnp.bfloat16
F32 = jnp.float32
VMEM = pl.BlockSpec(memory_space=pltpu.VMEM)
SMEM = pl.BlockSpec(memory_space=pltpu.SMEM)
NT = (((1,), (1,)), ((), ()))


def near(array):
    return pltpu.with_memory_space_constraint(array, pltpu.VMEM)


def call(kernel, out_shape, in_specs, name):
    return pl.pallas_call(
        kernel,
        out_shape=out_shape,
        in_specs=in_specs,
        out_specs=jax.tree.map(lambda _: VMEM, out_shape),
        compiler_params=pltpu.CompilerParams(vmem_limit_bytes=16 * 1024 * 1024),
        name=name,
    )


def attend_kernel(
    narrow, blocks, scale, rows_ref, lengths_ref, query_ref, key_ref, cache_ref, value_ref, out_ref
):
    slots, latent = cache_ref.shape[0], value_ref.shape[1]
    heads, head_size = key_ref.shape[0], key_ref.shape[1]
    rope = cache_ref.shape[1] - latent
    span = cache_ref.shape[2]
    queries = []
    for slot in range(slots):
        row = rows_ref[slot]
        queries.append(query_ref[row // slots, row % slots])
    query = jnp.concatenate(queries, axis=0)
    own_head = lax.broadcasted_iota(jnp.int32, (slots * heads, 1), 0) % heads
    nope = query[:, :head_size]
    zero = jnp.zeros((), BF16)
    spread = jnp.concatenate(
        [jnp.where(own_head == head, nope, zero) for head in range(heads)], axis=1
    )
    query_latent = jnp.dot(
        spread, key_ref[...].reshape(heads * head_size, latent), preferred_element_type=F32
    ).astype(BF16)
    contexts = []
    for slot in range(slots):
        part = slice(slot * heads, (slot + 1) * heads)
        scores = jnp.dot(
            query_latent[part], cache_ref[slot, :latent, :], preferred_element_type=F32
        ) + jnp.dot(
            query[part, head_size : head_size + rope],
            cache_ref[slot, latent:, :],
            preferred_element_type=F32,
        )
        live = lax.broadcasted_iota(jnp.int32, (1, span), 1) < lengths_ref[slot]
        scores = jnp.where(live, scores * scale, -jnp.inf)
        weights = jnp.exp(scores - jnp.max(scores, axis=1, keepdims=True))
        probs = (weights / jnp.sum(weights, axis=1, keepdims=True)).astype(BF16)
        contexts.append(
            lax.dot_general(
                probs, cache_ref[slot, :latent, :], NT, preferred_element_type=F32
            ).astype(BF16)
        )
    context = jnp.concatenate(contexts, axis=0)
    spread = jnp.concatenate(
        [jnp.where(own_head == head, context, zero) for head in range(heads)], axis=1
    )
    heads_out = jnp.dot(
        spread, value_ref[...].reshape(heads * latent, head_size), preferred_element_type=F32
    ).astype(BF16)
    per_block = heads // blocks
    pieces = []
    for block in range(blocks):
        low = block * per_block
        pieces.append(
            jnp.concatenate(
                [
                    heads_out[slot * heads + low : slot * heads + low + per_block]
                    for slot in range(slots)
                ],
                axis=0,
            )
        )
    for target in range(out_ref.shape[0]):
        out_ref[target] = pieces[(target // narrow) % blocks]


def project_kernel(narrow, blocks, rows_ref, group_ref, heads_ref, residual_ref, weight_ref, out_ref):
    wide = heads_ref.shape[0] // narrow
    slots = residual_ref.shape[0]
    rows = wide * slots
    per_block = heads_ref.shape[1] // slots
    head_size = heads_ref.shape[2]
    group = group_ref[0]
    holder = group // blocks
    received = jnp.concatenate(
        [heads_ref[source * narrow + holder] for source in range(wide)], axis=0
    )
    count = rows * per_block
    column = lax.broadcasted_iota(jnp.int32, (1, count), 1)
    column_row = jnp.zeros((1, count), jnp.int32)
    for slot in range(rows):
        column_row = jnp.where(column // per_block == slot, rows_ref[slot], column_row)
    wanted = column_row + rows * (column % per_block)
    position = lax.broadcasted_iota(jnp.int32, (count, count), 0)
    select = jnp.where(position == wanted, 1.0, 0.0).astype(BF16)
    ordered = jnp.dot(select, received, preferred_element_type=F32).astype(BF16)
    flat = jnp.concatenate(
        [ordered[head * rows : (head + 1) * rows] for head in range(per_block)], axis=1
    )
    total = jnp.dot(flat, weight_ref[...], preferred_element_type=F32)
    row = lax.broadcasted_iota(jnp.int32, (rows, 1), 0)
    for slot in range(slots):
        own = residual_ref[slot : slot + 1, :].astype(F32)
        total = total + jnp.where(row == group * slots + slot, own, 0.0)
    out_ref[...] = total.astype(BF16)


def split_sum(value):
    high = value.astype(BF16)
    low = (value - high.astype(F32)).astype(BF16)
    return high, low


def put_sums(out_ref, start, value):
    high, low = split_sum(value)
    shape = (value.shape[0], 128)
    out_ref[:, start : start + 128] = jnp.broadcast_to(high, shape)
    out_ref[:, start + 128 : start + 256] = jnp.broadcast_to(low, shape)


def get_sums(ref, start):
    return ref[:, start : start + 1].astype(F32) + ref[:, start + 128 : start + 129].astype(F32)


def expand_kernel(first_ref, second_ref, gain_ref, gate_ref, up_ref, middle_ref, out_ref):
    middle = first_ref[...].astype(F32) + second_ref[...].astype(F32)
    middle_ref[...] = middle
    columns = gate_ref.shape[1]
    padded = (out_ref.shape[1] - 256) // 2
    scaled = (middle * gain_ref[...].astype(F32)).astype(BF16)
    out_ref[:, :columns] = jnp.dot(scaled, gate_ref[...], preferred_element_type=F32).astype(BF16)
    out_ref[:, padded : padded + columns] = jnp.dot(
        scaled, up_ref[...], preferred_element_type=F32
    ).astype(BF16)
    put_sums(out_ref, 2 * padded, jnp.sum(middle * middle, axis=1, keepdims=True))


def merge_kernel(first_ref, second_ref, out_ref):
    end = out_ref.shape[1] - 256
    out_ref[:, :end] = (
        first_ref[:, :end].astype(F32) + second_ref[:, :end].astype(F32)
    ).astype(BF16)
    put_sums(out_ref, end, get_sums(first_ref, end) + get_sums(second_ref, end))


def contract_kernel(first_ref, second_ref, weight_ref, out_ref):
    padded = (first_ref.shape[1] - 256) // 2
    columns = weight_ref.shape[0]
    square = get_sums(first_ref, 2 * padded) + get_sums(second_ref, 2 * padded)
    factor = lax.rsqrt(square / D + 1e-06)
    gate = (first_ref[:, :columns].astype(F32) + second_ref[:, :columns].astype(F32)) * factor
    up = (
        first_ref[:, padded : padded + columns].astype(F32)
        + second_ref[:, padded : padded + columns].astype(F32)
    ) * factor
    hidden = (gate / (1.0 + jnp.exp(-gate)) * up).astype(BF16)
    total = jnp.dot(hidden, weight_ref[...], preferred_element_type=F32)
    slots = out_ref.shape[1]
    for owner in range(out_ref.shape[0]):
        out_ref[owner] = total[owner * slots : (owner + 1) * slots]


def swap(array, axis, distance, size):
    return lax.ppermute(array, axis, [(i, i ^ distance) for i in range(size)])


def shards(
    wide,
    narrow,
    residual_in,
    query_nope,
    query_rope,
    absorb_key,
    absorb_value,
    latent_cache,
    cache_lengths,
    slot_rows,
    out_proj,
    norm_gain,
    gate_weight,
    up_weight,
    down_weight,
):
    slots, heads, head_size = query_nope.shape
    rope = query_rope.shape[2]
    features = out_proj.shape[1]
    rows = slot_rows.shape[0]
    per_block = out_proj.shape[0] // head_size
    blocks = heads // per_block
    group = lax.axis_index("wide").astype(jnp.int32)
    scale = 1.0 / math.sqrt(head_size + rope)

    padding = jnp.zeros((slots, heads, 128 - rope), BF16)
    packed = jnp.concatenate([query_nope, query_rope, padding], axis=2)
    queries = lax.all_to_all(
        jnp.broadcast_to(packed[None], (wide,) + packed.shape), "wide", 0, 0, tiled=True
    )
    my_rows = lax.dynamic_slice_in_dim(slot_rows, group * slots, slots)
    heads_out = call(
        functools.partial(attend_kernel, narrow, blocks, scale),
        jax.ShapeDtypeStruct((wide * narrow, slots * per_block, head_size), BF16),
        [SMEM, SMEM, VMEM, VMEM, VMEM, VMEM],
        "attend",
    )(
        my_rows,
        cache_lengths,
        queries,
        near(absorb_key),
        near(jnp.swapaxes(latent_cache, 1, 2)),
        near(absorb_value),
    )
    received = lax.all_to_all(heads_out, ("wide", "narrow"), 0, 0, tiled=True)
    summed = call(
        functools.partial(project_kernel, narrow, blocks),
        jax.ShapeDtypeStruct((rows, features), BF16),
        [SMEM, SMEM, VMEM, VMEM, VMEM],
        "project",
    )(slot_rows, group[None], received, residual_in, near(out_proj))
    distance = 1
    while distance < wide:
        other = swap(summed, "wide", distance, wide)
        distance *= 2
        if distance < wide:
            summed = (summed.astype(F32) + other.astype(F32)).astype(BF16)
    columns = gate_weight.shape[1]
    padded = -(-columns // 128) * 128
    middle, terms = call(
        expand_kernel,
        (
            jax.ShapeDtypeStruct((rows, features), F32),
            jax.ShapeDtypeStruct((rows, 2 * padded + 256), BF16),
        ),
        [VMEM] * 5,
        "expand",
    )(summed, other, norm_gain[None, :], near(gate_weight), near(up_weight))
    distance = 1
    while distance < narrow:
        other = swap(terms, "narrow", distance, narrow)
        distance *= 2
        if distance < narrow:
            terms = call(merge_kernel, terms_like(terms), [VMEM] * 2, "merge")(terms, other)
    down = call(
        contract_kernel,
        jax.ShapeDtypeStruct((wide, slots, features), F32),
        [VMEM] * 3,
        "contract",
    )(terms, other, near(down_weight))
    total = jnp.sum(lax.all_to_all(down, "wide", 0, 0, tiled=True), axis=0)
    return (lax.dynamic_slice_in_dim(middle, group * slots, slots) + total).astype(BF16)


def terms_like(array):
    return jax.ShapeDtypeStruct(array.shape, array.dtype)


def solution(mesh):
    in_specs = (
        P("wide", "narrow"),
        P("wide", "narrow", None),
        P("wide", "narrow", None),
        P("narrow", None, None),
        P("narrow", None, None),
        P("wide", None, None),
        P("wide"),
        P(),
        P("wide", "narrow"),
        P("narrow"),
        P("narrow", "wide"),
        P("narrow", "wide"),
        P("wide", "narrow"),
    )
    out_specs = P("wide", "narrow")
    body = functools.partial(shards, mesh.shape["wide"], mesh.shape["narrow"])
    return jax.shard_map(body, mesh=mesh, in_specs=in_specs, out_specs=out_specs, check_vma=False)
```

time: 304 us -> 79.3 us (0.26)
  waiting for transfers between devices: 172 us -> 25.7 us
  blocking collectives: 74.2 us -> 20.2 us
  matrix products: 27 us -> 0 us
  between operations: 13.9 us -> 0.06 us
  local copies, waits for them, and re-layouts: 1.81 us -> 13.1 us
  Pallas kernels: 0 us -> 8.47 us
  other arithmetic: 7.97 us -> 1.41 us
  starting transfers between devices: 5.64 us -> 9.93 us
    unnamed x5 -> x0, waiting for transfers between devices: 135 us -> none
    all_gather x3 -> x0, blocking collectives: 68.5 us -> none  [the longest x1 32.3 us: shards(): gathered = lax.all_gather(packed_queries, 'wide', axis=0, tiled=True)]
    psum x1 -> x0, waiting for transfers between devices: 32.4 us -> none  [shards(): summed = lax.psum(local_terms, 'narrow')]
    dot_general x8 -> x0, matrix products: 27 us -> none  [the longest x1 5.37 us: shards(): jnp.dot(hidden, down_weight, preferred_element_type=jnp.float32)]
    all_to_all x0 -> x2, blocking collectives: none -> 20.2 us  [the longest x1 10.4 us: shards(): received = lax.all_to_all(heads_out, ('wide', 'narrow'), 0, 0, tiled=True)]
    ppermute x0 -> x5, waiting for transfers between devices: none -> 19.1 us  [swap(): return lax.ppermute(array, axis, [(i, i ^ distance) for i in range(size)])]
    unnamed x12 -> x24, local copies, waits for them, and re-layouts: 0.63 us -> 11.6 us
    pallas_call x0 -> x5, Pallas kernels: none -> 8.47 us  [the longest x1 3.64 us: shards(): call(functools.partial(attend_kernel, narrow, blocks, scale), jax.ShapeDt...]
  transfers between devices with their start and end apart: 4 -> 6, of which waited for: 4 -> 6; matrix products, arithmetic and copies ran while one was open for 1% -> 1% of each run, Pallas kernels for 0% -> 0%
where the time goes in v1:
time: 79.3 us; the launch traced here: 78.8 us
  waiting for transfers between devices  25.7 us (32%)
  blocking collectives  20.2 us (25%)
  local copies, waits for them, and re-layouts  13.1 us (17%)
  starting transfers between devices  9.93 us (13%)
  Pallas kernels  8.47 us (11%)
  other arithmetic  1.41 us (2%)
    ppermute x5, waiting for transfers between devices, swap(): return lax.ppermute(array, axis, [(i, i ^ distance) for i in range(size)])  19.1 us
    unnamed x24, local copies, waits for them, and re-layouts  11.6 us
    all_to_all x1, blocking collectives, shards(): received = lax.all_to_all(heads_out, ('wide', 'narrow'), 0, 0, tiled=True)  10.4 us
    all_to_all x1, blocking collectives, shards(): total = jnp.sum(lax.all_to_all(down, 'wide', 0, 0, tiled=True), axis=0)  9.74 us
    all_to_all x1, starting transfers between devices, shards(): lax.all_to_all(jnp.broadcast_to(packed[None], (wide,) + packed.shape), 'w...  7.28 us
    all_to_all x1, waiting for transfers between devices, shards(): lax.all_to_all(jnp.broadcast_to(packed[None], (wide,) + packed.shape), 'w...  6.62 us
    pallas_call x1, Pallas kernels, shards(): call(functools.partial(attend_kernel, narrow, blocks, scale), jax.ShapeDt...  3.64 us
    ppermute x5, starting transfers between devices, swap(): return lax.ppermute(array, axis, [(i, i ^ distance) for i in range(size)])  2.65 us
  transfers between devices with their start and end apart: 6, of which 6 were waited for; matrix products, arithmetic and copies ran while one was open for 1% of the time, Pallas kernels for 0%

profile of v1, /device:TPU:0, one launch (start us, length us, event | category | flops | bytes accessed | tf_op | source)
XLA Modules:
  0.0 78.8 jit_solution(17776416006623257586)
XLA Ops:
  0.0 0.1 pad.2.clone
  0.1 0.7 maximum_maximum_fusion
  0.8 0.7 broadcast_in_dim.17
  1.5 7.3 %all-to-all-start = ((bf16[8,2,16,256]{3,2,1,0:T(8,128)(2,1)}), bf16[8,2,16,256]{3,2,1,0:T(8,128)(2,1)S(1)}, u32[]{:S(2)}, u32[]{:S(2)}) async-start(bf16[8,2,16,256]{3,2,1,0:T(8,128)(2,1)} %broadcast_in_dim.17), calls=%async_computation | async-start | bytes 262144 | tf_op jit(solution)/shard_map/all_to_all | solution.py:216
  8.8 0.7 dynamic_slice.6.rows_ref
  9.5 6.6 %all-to-all-done.query_ref = bf16[8,2,16,256]{3,2,1,0:T(8,128)(2,1)S(1)} async-done(((bf16[8,2,16,256]{3,2,1,0:T(8,128)(2,1)}), bf16[8,2,16,256]{3,2,1,0:T(8,128)(2,1)S(1)}, u32[]{:S(2)}, u32[]{:S(2)}) %all-to-all-start) | async-done | bytes 131104 | tf_op jit(solution)/shard_map/all_to_all | solution.py:216
  16.1 0.0 copy-start.2
  16.1 2.3 %copy-done.2 = bf16[2,2048,576]{1,2,0:T(8,128)(2,1)S(1)} copy-done((bf16[2,2048,576]{1,2,0:T(8,128)(2,1)S(1)}, bf16[2,2048,576]{1,2,0:T(8,128)(2,1)}, u32[]{:S(2)}) %copy-start.2) | copy-done | bytes 4718616
  18.4 0.0 copy-start.4
  18.4 1.6 %copy-done.4 = bf16[16,128,512]{2,1,0:T(8,128)(2,1)S(1)} copy-done((bf16[16,128,512]{2,1,0:T(8,128)(2,1)S(1)}, bf16[16,128,512]{2,1,0:T(8,128)(2,1)}, u32[]{:S(2)}) %copy-start.4) | copy-done | bytes 2097176
  20.0 0.0 copy-start.5
  20.0 1.6 %copy-done.5 = bf16[16,512,128]{2,1,0:T(8,128)(2,1)S(1)} copy-done((bf16[16,512,128]{2,1,0:T(8,128)(2,1)S(1)}, bf16[16,512,128]{2,1,0:T(8,128)(2,1)}, u32[]{:S(2)}) %copy-start.5) | copy-done | bytes 2097176
  21.6 0.0 copy-start.7
  21.6 0.7 copy-done.7
  22.3 0.0 copy-start.6
  22.3 0.0 copy-start.8
  22.3 0.0 copy-start.9
  22.3 0.0 copy-start
  22.3 3.6 %attend.1 = bf16[32,16,128]{2,1,0:T(8,128)(2,1)S(1)} custom-call(s32[2]{0:T(128)S(1)} %dynamic_slice.6.rows_ref, s32[2]{0:T(128)S(1)} %copy-done.7, bf16[8,2,16,256]{3,2,1,0:T(8,128)(2,1)S(1)} %all-to-all-done.query_ref, bf16[16,128,512]{2,1,0:T(8,128)(2,1)S(1)} %copy-done.4, bf16[2,576,2048]{2,1,0:T(8,128)(2,1)S(1)} %bitcast.4, ...), custom_call_target="tpu_custom_call" | custom-call | tf_op jit(solution)/shard_map/attend/pallas_call | solution.py:220
  25.9 10.4 %all_to_all.15.heads_ref = bf16[32,16,128]{2,1,0:T(8,128)(2,1)S(1)} all-to-all(bf16[32,16,128]{2,1,0:T(8,128)(2,1)S(1)} %attend.1), channel_id=1, replica_groups=mesh['wide'=8,'narrow'=4] {'wide','narrow'}, dimensions={0} | all-to-all | bytes 262144 | tf_op jit(solution)/shard_map/all_to_all | solution.py:233
  36.3 0.0 copy-done.6
  36.3 0.0 copy-done.8
  36.4 0.0 copy-start.3
  36.4 2.0 %copy-done.3 = bf16[1024,1792]{1,0:T(8,128)(2,1)S(1)} copy-done((bf16[1024,1792]{1,0:T(8,128)(2,1)S(1)}, bf16[1024,1792]{1,0:T(8,128)(2,1)}, u32[]{:S(2)}) %copy-start.3) | copy-done | bytes 3670040
  38.4 1.2 %project.1 = bf16[16,1792]{1,0:T(8,128)(2,1)S(1)} custom-call(s32[16]{0:T(128)S(1)} %copy-done.8, s32[1]{0:T(128)} %bitcast.group_ref, bf16[32,16,128]{2,1,0:T(8,128)(2,1)S(1)} %all_to_all.15.heads_ref, bf16[2,1792]{1,0:T(2,128)(2,1)S(1)} %copy-done.6, bf16[1024,1792]{1,0:T(8,128)(2,1)S(1)} %copy-done.3), custom_call_target="tpu_custom_call" | custom-call | tf_op jit(solution)/shard_map/project/pallas_call | solution.py:234
  39.6 0.7 collective-permute-start
  40.4 3.5 %collective-permute-done = bf16[16,1792]{1,0:T(8,128)(2,1)S(1)} collective-permute-done((bf16[16,1792]{1,0:T(8,128)(2,1)S(1)}, bf16[16,1792]{1,0:T(8,128)(2,1)S(1)}, u32[]{:S(2)}, u32[]{:S(2)}) %collective-permute-start) | collective-permute-done | bytes 57376 | tf_op jit(solution)/shard_map/ppermute | solution.py:185
  43.9 0.7 collective-permute-start.1
  44.6 3.5 %collective-permute-done.1 = bf16[16,1792]{1,0:T(8,128)(2,1)S(1)} collective-permute-done((bf16[16,1792]{1,0:T(8,128)(2,1)S(1)}, bf16[16,1792]{1,0:T(8,128)(2,1)S(1)}, u32[]{:S(2)}, u32[]{:S(2)}) %collective-permute-start.1) | collective-permute-done | bytes 57376 | tf_op jit(solution)/shard_map/ppermute | solution.py:185
  48.2 0.8 %collective-permute-start.2 = (bf16[16,1792]{1,0:T(8,128)(2,1)S(1)}, bf16[16,1792]{1,0:T(8,128)(2,1)S(1)}, u32[]{:S(2)}, u32[]{:S(2)}) collective-permute-start(bf16[16,1792]{1,0:T(8,128)(2,1)S(1)} %add_convert_fusion.first_ref), channel_id=1, source_target_pairs={{0,16},{4,20},{8,24},{12,28},{16,0},{20,4},{24,8},{28,12},{1,17},{... | collective-permute-start | bytes 172040 | tf_op jit(solution)/shard_map/ppermute | solution.py:185
  49.0 0.0 copy-done.9
  49.0 0.0 slice-start
  49.0 0.0 slice-start.1
  49.0 4.9 %collective-permute-done.2.second_ref = bf16[16,1792]{1,0:T(8,128)(2,1)S(1)} collective-permute-done((bf16[16,1792]{1,0:T(8,128)(2,1)S(1)}, bf16[16,1792]{1,0:T(8,128)(2,1)S(1)}, u32[]{:S(2)}, u32[]{:S(2)}) %collective-permute-start.2) | collective-permute-done | bytes 57376 | tf_op jit(solution)/shard_map/ppermute | solution.py:185
  53.9 0.0 copy-done
  53.9 0.0 copy-start.1
  53.9 3.3 %copy-done.1 = bf16[1792,2304]{1,0:T(8,128)(2,1)S(1)} copy-done((bf16[1792,2304]{1,0:T(8,128)(2,1)S(1)}, bf16[1792,2304]{1,0:T(8,128)(2,1)}, u32[]{:S(2)}) %copy-start.1) | copy-done | bytes 8257560
  57.3 2.2 %expand.1 = (f32[16,1792]{1,0:T(8,128)S(1)}, bf16[16,4864]{1,0:T(8,128)(2,1)S(1)}) custom-call(bf16[16,1792]{1,0:T(8,128)(2,1)S(1)} %add_convert_fusion.first_ref, bf16[16,1792]{1,0:T(8,128)(2,1)S(1)} %collective-permute-done.2.second_ref, bf16[1,1792]{1,0:T(2,128)(2,1)S(1)} %broadcast_in_dim.18.gain_ref, bf16[1792,2304]{1,0:T(8,128)(2,1)S(1)} %copy-done, ...), custom_call_target="tpu_custom_call" | custom-call | tf_op jit(solution)/shard_map/expand/pallas_call | solution.py:248
  59.5 0.0 collective-permute-start.3
  59.5 1.4 %collective-permute-done.3.second_ref = bf16[16,4864]{1,0:T(8,128)(2,1)S(1)} collective-permute-done((bf16[16,4864]{1,0:T(8,128)(2,1)S(1)}, bf16[16,4864]{1,0:T(8,128)(2,1)S(1)}, u32[]{:S(2)}, u32[]{:S(2)}) %collective-permute-start.3) | collective-permute-done | bytes 155680 | tf_op jit(solution)/shard_map/ppermute | solution.py:185
  60.9 0.1 merge.1.first_ref
  61.0 0.4 collective-permute-start.4
  61.4 5.8 %collective-permute-done.4.second_ref = bf16[16,4864]{1,0:T(8,128)(2,1)S(1)} collective-permute-done((bf16[16,4864]{1,0:T(8,128)(2,1)S(1)}, bf16[16,4864]{1,0:T(8,128)(2,1)S(1)}, u32[]{:S(2)}, u32[]{:S(2)}) %collective-permute-start.4) | collective-permute-done | bytes 155680 | tf_op jit(solution)/shard_map/ppermute | solution.py:185
  67.1 0.0 slice-done
  67.1 0.0 slice-done.1
  67.1 1.3 %contract.1 = f32[8,2,1792]{2,1,0:T(2,128)S(1)} custom-call(bf16[16,4864]{1,0:T(8,128)(2,1)S(1)} %merge.1.first_ref, bf16[16,4864]{1,0:T(8,128)(2,1)S(1)} %collective-permute-done.4.second_ref, bf16[2304,1792]{1,0:T(8,128)(2,1)S(1)} %bitcast.3), custom_call_target="tpu_custom_call" | custom-call | tf_op jit(solution)/shard_map/contract/pallas_call | solution.py:263
  68.4 9.7 %all_to_all.16 = f32[8,2,1792]{2,1,0:T(2,128)S(1)} all-to-all(f32[8,2,1792]{2,1,0:T(2,128)S(1)} %contract.1), channel_id=1, replica_groups=mesh['wide'=8,'narrow'=4] {'wide'}, dimensions={0} | all-to-all | bytes 229376 | tf_op jit(solution)/shard_map/all_to_all | solution.py:269
  78.2 0.6 add_convert_fusion.2
  (6 shorter events, 0.1 us)
Async XLA Ops:
  1.5 14.6 %all-to-all-start = ((bf16[8,2,16,256]{3,2,1,0:T(8,128)(2,1)}), bf16[8,2,16,256]{3,2,1,0:T(8,128)(2,1)S(1)}, u32[]{:S(2)}, u32[]{:S(2)}) async-start(bf16[8,2,16,256]{3,2,1,0:T(8,128)(2,1)} %broadcast_in_dim.17), calls=%async_computation | async-start | bytes 262144 | tf_op jit(solution)/shard_map/all_to_all | solution.py:216
  16.1 2.3 %copy-start.2 = (bf16[2,2048,576]{1,2,0:T(8,128)(2,1)S(1)}, bf16[2,2048,576]{1,2,0:T(8,128)(2,1)}, u32[]{:S(2)}) copy-start(bf16[2,2048,576]{1,2,0:T(8,128)(2,1)} %param.18) | copy-start | bytes 14155780
  18.4 1.6 %copy-start.4 = (bf16[16,128,512]{2,1,0:T(8,128)(2,1)S(1)}, bf16[16,128,512]{2,1,0:T(8,128)(2,1)}, u32[]{:S(2)}) copy-start(bf16[16,128,512]{2,1,0:T(8,128)(2,1)} %key_ref.1) | copy-start | bytes 6291460
  20.0 1.6 %copy-start.5 = (bf16[16,512,128]{2,1,0:T(8,128)(2,1)S(1)}, bf16[16,512,128]{2,1,0:T(8,128)(2,1)}, u32[]{:S(2)}) copy-start(bf16[16,512,128]{2,1,0:T(8,128)(2,1)} %value_ref.1) | copy-start | bytes 6291460
  21.6 0.7 copy-start.7
  22.3 14.1 %copy-start.6 = (bf16[2,1792]{1,0:T(2,128)(2,1)S(1)}, bf16[2,1792]{1,0:T(2,128)(2,1)}, u32[]{:S(2)}) copy-start(bf16[2,1792]{1,0:T(2,128)(2,1)} %residual_ref.1) | copy-start | bytes 21508
  22.3 14.1 %copy-start.8 = (s32[16]{0:T(128)S(1)}, s32[16]{0:T(128)}, u32[]{:S(2)}) copy-start(s32[16]{0:T(128)} %rows_ref.1) | copy-start | bytes 196
  22.3 26.7 %copy-start.9 = (bf16[1792]{0:T(1024)(128)(2,1)S(1)}, bf16[1792]{0:T(1024)(128)(2,1)}, u32[]{:S(2)}) copy-start(bf16[1792]{0:T(1024)(128)(2,1)} %param.22) | copy-start | bytes 10756
  22.3 31.6 %copy-start = (bf16[1792,2304]{1,0:T(8,128)(2,1)S(1)}, bf16[1792,2304]{1,0:T(8,128)(2,1)}, u32[]{:S(2)}) copy-start(bf16[1792,2304]{1,0:T(8,128)(2,1)} %gate_ref.1) | copy-start | bytes 24772612
  36.4 2.0 %copy-start.3 = (bf16[1024,1792]{1,0:T(8,128)(2,1)S(1)}, bf16[1024,1792]{1,0:T(8,128)(2,1)}, u32[]{:S(2)}) copy-start(bf16[1024,1792]{1,0:T(8,128)(2,1)} %weight_ref.2) | copy-start | bytes 11010052
  39.6 4.2 %collective-permute-start = (bf16[16,1792]{1,0:T(8,128)(2,1)S(1)}, bf16[16,1792]{1,0:T(8,128)(2,1)S(1)}, u32[]{:S(2)}, u32[]{:S(2)}) collective-permute-start(bf16[16,1792]{1,0:T(8,128)(2,1)S(1)} %project.1), channel_id=1, source_target_pairs={{0,4},{4,0},{8,12},{12,8},{16,20},{20,16},{24,28},{28,24},{1,5},{5... | collective-permute-start | bytes 172040 | tf_op jit(solution)/shard_map/ppermute | solution.py:185
  43.9 4.2 %collective-permute-start.1 = (bf16[16,1792]{1,0:T(8,128)(2,1)S(1)}, bf16[16,1792]{1,0:T(8,128)(2,1)S(1)}, u32[]{:S(2)}, u32[]{:S(2)}) collective-permute-start(bf16[16,1792]{1,0:T(8,128)(2,1)S(1)} %add_convert_fusion.1), channel_id=1, source_target_pairs={{0,8},{4,12},{8,0},{12,4},{16,24},{20,28},{24,16},{28,20},{1,9},{5... | collective-permute-start | bytes 172040 | tf_op jit(solution)/shard_map/ppermute | solution.py:185
  48.2 5.8 %collective-permute-start.2 = (bf16[16,1792]{1,0:T(8,128)(2,1)S(1)}, bf16[16,1792]{1,0:T(8,128)(2,1)S(1)}, u32[]{:S(2)}, u32[]{:S(2)}) collective-permute-start(bf16[16,1792]{1,0:T(8,128)(2,1)S(1)} %add_convert_fusion.first_ref), channel_id=1, source_target_pairs={{0,16},{4,20},{8,24},{12,28},{16,0},{20,4},{24,8},{28,12},{1,17},{... | collective-permute-start | bytes 172040 | tf_op jit(solution)/shard_map/ppermute | solution.py:185
  49.0 18.1 %slice-start = ((s8[8257536]{0:T(1024)(128)(4,1)}), s8[4194304]{0:T(1024)(128)(4,1)S(1)}, s32[]{:S(2)}) async-start(s8[8257536]{0:T(1024)(128)(4,1)} %bitcast.2), calls=%async_computation.3 | async-start | bytes 8388608
  49.0 18.1 %slice-start.1 = ((s8[8257536]{0:T(1024)(128)(4,1)}), s8[4063232]{0:T(1024)(128)(4,1)S(1)}, s32[]{:S(2)}) async-start(s8[8257536]{0:T(1024)(128)(4,1)} %bitcast.2), calls=%async_computation.4 | async-start | bytes 8126464
  53.9 3.3 %copy-start.1 = (bf16[1792,2304]{1,0:T(8,128)(2,1)S(1)}, bf16[1792,2304]{1,0:T(8,128)(2,1)}, u32[]{:S(2)}) copy-start(bf16[1792,2304]{1,0:T(8,128)(2,1)} %up_ref.1) | copy-start | bytes 24772612
  59.5 1.4 %collective-permute-start.3 = (bf16[16,4864]{1,0:T(8,128)(2,1)S(1)}, bf16[16,4864]{1,0:T(8,128)(2,1)S(1)}, u32[]{:S(2)}, u32[]{:S(2)}) collective-permute-start(bf16[16,4864]{1,0:T(8,128)(2,1)S(1)} %get-tuple-element.8.first_ref), channel_id=1, source_target_pairs={{0,1},{1,0},{2,3},{3,2},{4,5},{5,4},{6,7},{7,6},{8,9},{9,8},{10,11... | collective-permute-start | bytes 466952 | tf_op jit(solution)/shard_map/ppermute | solution.py:185
  61.0 6.1 %collective-permute-start.4 = (bf16[16,4864]{1,0:T(8,128)(2,1)S(1)}, bf16[16,4864]{1,0:T(8,128)(2,1)S(1)}, u32[]{:S(2)}, u32[]{:S(2)}) collective-permute-start(bf16[16,4864]{1,0:T(8,128)(2,1)S(1)} %merge.1.first_ref), channel_id=1, source_target_pairs={{0,2},{1,3},{2,0},{3,1},{4,6},{5,7},{6,4},{7,5},{8,10},{9,11},{10,... | collective-permute-start | bytes 466952 | tf_op jit(solution)/shard_map/ppermute | solution.py:185

commit v2 on v1

--- a/solution.py
+++ b/solution.py
@@ -13,17 +13,19 @@
 F32 = jnp.float32
 VMEM = pl.BlockSpec(memory_space=pltpu.VMEM)
 SMEM = pl.BlockSpec(memory_space=pltpu.SMEM)
+HBM = pl.BlockSpec(memory_space=pltpu.HBM)
 NT = (((1,), (1,)), ((), ()))
 
 
-def near(array):
-    return pltpu.with_memory_space_constraint(array, pltpu.VMEM)
-
-
-def call(kernel, out_shape, in_specs, name):
+def far(array):
+    return pltpu.with_memory_space_constraint(array, pltpu.HBM)
+
+
+def call(kernel, out_shape, in_specs, name, scratch=()):
     return pl.pallas_call(
         kernel,
         out_shape=out_shape,
+        scratch_shapes=scratch,
         in_specs=in_specs,
         out_specs=jax.tree.map(lambda _: VMEM, out_shape),
         compiler_params=pltpu.CompilerParams(vmem_limit_bytes=16 * 1024 * 1024),
@@ -31,16 +33,91 @@
     )
 
 
+def pack_kernel(nope_hbm, rope_hbm, out_ref, nope_ref, rope_ref, sems):
+    copies = [
+        pltpu.make_async_copy(nope_hbm, nope_ref, sems.at[0]),
+        pltpu.make_async_copy(rope_hbm, rope_ref, sems.at[1]),
+    ]
+    for copy in copies:
+        copy.start()
+    head_size, width = nope_ref.shape[2], rope_ref.shape[2]
+    empty = jnp.zeros(rope_ref.shape[:2] + (out_ref.shape[3] - head_size - width,), BF16)
+    for copy in copies:
+        copy.wait()
+    row = jnp.concatenate([nope_ref[...], rope_ref[...], empty], axis=2)
+    for target in range(out_ref.shape[0]):
+        out_ref[target] = row
+
+
+class Fetch:
+    def __init__(self, source, target, sems, first, parts):
+        self.copies = [
+            pltpu.make_async_copy(source.at[part], target.at[part], sems.at[first + index])
+            for index, part in enumerate(parts)
+        ]
+
+    def start(self):
+        for copy in self.copies:
+            copy.start()
+        return self
+
+    def wait(self, first=0, last=None):
+        for copy in self.copies[first:last]:
+            copy.wait()
+
+
+def halves(size):
+    if size % 32:
+        return [pl.ds(0, size)]
+    return [pl.ds(0, size // 2), pl.ds(size // 2, size // 2)]
+
+
 def attend_kernel(
-    narrow, blocks, scale, rows_ref, lengths_ref, query_ref, key_ref, cache_ref, value_ref, out_ref
+    narrow,
+    blocks,
+    scale,
+    group_ref,
+    rows_hbm,
+    lengths_hbm,
+    query_ref,
+    key_hbm,
+    cache_hbm,
+    value_hbm,
+    weight_hbm,
+    out_ref,
+    weight_ref,
+    rows_ref,
+    lengths_ref,
+    key_ref,
+    cache_ref,
+    value_ref,
+    sems,
 ):
     slots, latent = cache_ref.shape[0], value_ref.shape[1]
     heads, head_size = key_ref.shape[0], key_ref.shape[1]
     rope = cache_ref.shape[1] - latent
     span = cache_ref.shape[2]
+    small = [
+        pltpu.make_async_copy(rows_hbm, rows_ref, sems.at[0]),
+        pltpu.make_async_copy(lengths_hbm, lengths_ref, sems.at[1]),
+    ]
+    for copy in small:
+        copy.start()
+    key = Fetch(key_hbm, key_ref, sems, 2, [pl.ds(0, heads // 2), pl.ds(heads // 2, heads // 2)]).start()
+    wide_cut = [(slot, part) for slot in range(slots) for part in halves(cache_ref.shape[1])]
+    cache = Fetch(cache_hbm, cache_ref, sems, 4, wide_cut).start()
+    value = Fetch(
+        value_hbm, value_ref, sems, 4 + 2 * slots, [pl.ds(0, heads // 2), pl.ds(heads // 2, heads // 2)]
+    ).start()
+    weight = Fetch(
+        weight_hbm, weight_ref, sems, 6 + 2 * slots, halves(weight_ref.shape[0])
+    ).start()
+    for copy in small:
+        copy.wait()
+    group = group_ref[0]
     queries = []
     for slot in range(slots):
-        row = rows_ref[slot]
+        row = rows_ref[group * slots + slot]
         queries.append(query_ref[row // slots, row % slots])
     query = jnp.concatenate(queries, axis=0)
     own_head = lax.broadcasted_iota(jnp.int32, (slots * heads, 1), 0) % heads
@@ -49,12 +126,15 @@
     spread = jnp.concatenate(
         [jnp.where(own_head == head, nope, zero) for head in range(heads)], axis=1
     )
+    key.wait()
     query_latent = jnp.dot(
         spread, key_ref[...].reshape(heads * head_size, latent), preferred_element_type=F32
     ).astype(BF16)
     contexts = []
     for slot in range(slots):
         part = slice(slot * heads, (slot + 1) * heads)
+        per_slot = len(wide_cut) // slots
+        cache.wait(slot * per_slot, (slot + 1) * per_slot)
         scores = jnp.dot(
             query_latent[part], cache_ref[slot, :latent, :], preferred_element_type=F32
         ) + jnp.dot(
@@ -75,6 +155,7 @@
     spread = jnp.concatenate(
         [jnp.where(own_head == head, context, zero) for head in range(heads)], axis=1
     )
+    value.wait()
     heads_out = jnp.dot(
         spread, value_ref[...].reshape(heads * latent, head_size), preferred_element_type=F32
     ).astype(BF16)
@@ -93,6 +174,7 @@
         )
     for target in range(out_ref.shape[0]):
         out_ref[target] = pieces[(target // narrow) % blocks]
+    weight.wait()
 
 
 def project_kernel(narrow, blocks, rows_ref, group_ref, heads_ref, residual_ref, weight_ref, out_ref):
@@ -211,32 +293,52 @@
     group = lax.axis_index("wide").astype(jnp.int32)
     scale = 1.0 / math.sqrt(head_size + rope)
 
-    padding = jnp.zeros((slots, heads, 128 - rope), BF16)
-    packed = jnp.concatenate([query_nope, query_rope, padding], axis=2)
-    queries = lax.all_to_all(
-        jnp.broadcast_to(packed[None], (wide,) + packed.shape), "wide", 0, 0, tiled=True
-    )
-    my_rows = lax.dynamic_slice_in_dim(slot_rows, group * slots, slots)
-    heads_out = call(
+    packed = call(
+        pack_kernel,
+        pltpu.VMEM((wide, slots, heads, head_size + 128), BF16),
+        [HBM] * 2,
+        "pack",
+        [
+            pltpu.VMEM(query_nope.shape, BF16),
+            pltpu.VMEM(query_rope.shape, BF16),
+            pltpu.SemaphoreType.DMA((2,)),
+        ],
+    )(far(query_nope), far(query_rope))
+    queries = lax.all_to_all(packed, "wide", 0, 0, tiled=True)
+    cache = jnp.swapaxes(latent_cache, 1, 2)
+    heads_out, out_weight = call(
         functools.partial(attend_kernel, narrow, blocks, scale),
-        jax.ShapeDtypeStruct((wide * narrow, slots * per_block, head_size), BF16),
-        [SMEM, SMEM, VMEM, VMEM, VMEM, VMEM],
+        (
+            pltpu.VMEM((wide * narrow, slots * per_block, head_size), BF16),
+            pltpu.VMEM(out_proj.shape, BF16),
+        ),
+        [SMEM, HBM, HBM, VMEM, HBM, HBM, HBM, HBM],
         "attend",
+        [
+            pltpu.SMEM(slot_rows.shape, jnp.int32),
+            pltpu.SMEM(cache_lengths.shape, jnp.int32),
+            pltpu.VMEM(absorb_key.shape, BF16),
+            pltpu.VMEM(cache.shape, BF16),
+            pltpu.VMEM(absorb_value.shape, BF16),
+            pltpu.SemaphoreType.DMA((8 + 2 * slots,)),
+        ],
     )(
-        my_rows,
-        cache_lengths,
+        group[None],
+        far(slot_rows),
+        far(cache_lengths),
         queries,
-        near(absorb_key),
-        near(jnp.swapaxes(latent_cache, 1, 2)),
-        near(absorb_value),
+        far(absorb_key),
+        far(cache),
+        far(absorb_value),
+        far(out_proj),
     )
     received = lax.all_to_all(heads_out, ("wide", "narrow"), 0, 0, tiled=True)
     summed = call(
         functools.partial(project_kernel, narrow, blocks),
-        jax.ShapeDtypeStruct((rows, features), BF16),
+        pltpu.VMEM((rows, features), BF16),
         [SMEM, SMEM, VMEM, VMEM, VMEM],
         "project",
-    )(slot_rows, group[None], received, residual_in, near(out_proj))
+    )(slot_rows, group[None], received, residual_in, out_weight)
     distance = 1
     while distance < wide:
         other = swap(summed, "wide", distance, wide)
@@ -248,12 +350,12 @@
     middle, terms = call(
         expand_kernel,
         (
-            jax.ShapeDtypeStruct((rows, features), F32),
-            jax.ShapeDtypeStruct((rows, 2 * padded + 256), BF16),
+            pltpu.VMEM((rows, features), F32),
+            pltpu.VMEM((rows, 2 * padded + 256), BF16),
         ),
         [VMEM] * 5,
         "expand",
-    )(summed, other, norm_gain[None, :], near(gate_weight), near(up_weight))
+    )(summed, other, norm_gain[None, :], gate_weight, up_weight)
     distance = 1
     while distance < narrow:
         other = swap(terms, "narrow", distance, narrow)
@@ -262,16 +364,16 @@
             terms = call(merge_kernel, terms_like(terms), [VMEM] * 2, "merge")(terms, other)
     down = call(
         contract_kernel,
-        jax.ShapeDtypeStruct((wide, slots, features), F32),
+        pltpu.VMEM((wide, slots, features), F32),
         [VMEM] * 3,
         "contract",
-    )(terms, other, near(down_weight))
+    )(terms, other, down_weight)
     total = jnp.sum(lax.all_to_all(down, "wide", 0, 0, tiled=True), axis=0)
     return (lax.dynamic_slice_in_dim(middle, group * slots, slots) + total).astype(BF16)
 
 
 def terms_like(array):
-    return jax.ShapeDtypeStruct(array.shape, array.dtype)
+    return pltpu.VMEM(array.shape, array.dtype)
 
 
 def solution(mesh):

time: 79.3 us -> 70.9 us (0.89)
  local copies, waits for them, and re-layouts: 13.1 us -> 0.05 us
  blocking collectives: 20.2 us -> 10.4 us
  waiting for transfers between devices: 25.7 us -> 33.6 us
  Pallas kernels: 8.47 us -> 12.3 us
  starting transfers between devices: 9.93 us -> 13.3 us
    unnamed x24 -> x16, local copies, waits for them, and re-layouts: 11.6 us -> 0.04 us
    all_to_all x1 -> x0, blocking collectives: 9.74 us -> none  [shards(): total = jnp.sum(lax.all_to_all(down, 'wide', 0, 0, tiled=True), axis=0)]
    all_to_all x1 -> x2, waiting for transfers between devices: 6.62 us -> 14.5 us  [the longest x1 7.34 us: shards(): queries = lax.all_to_all(packed, 'wide', 0, 0, tiled=True)]
    pallas_call x4 -> x5, Pallas kernels: 8.39 us -> 12.2 us  [the longest x1 5.38 us: shards(): call(functools.partial(attend_kernel, narrow, blocks, scale), (pltpu.VMEM...]
    all_to_all x1 -> x2, starting transfers between devices: 7.28 us -> 10.7 us  [the longest x1 7.29 us: shards(): queries = lax.all_to_all(packed, 'wide', 0, 0, tiled=True)]
  transfers between devices with their start and end apart: 6 -> 7, of which waited for: 6 -> 7; matrix products, arithmetic and copies ran while one was open for 1% -> 0% of each run, Pallas kernels for 0% -> 0%
where the time goes in v2:
time: 70.9 us; the launch traced here: 70.4 us
  waiting for transfers between devices  33.6 us (47%)
  starting transfers between devices  13.3 us (19%)
  Pallas kernels  12.3 us (17%)
  blocking collectives  10.4 us (15%)
    ppermute x5, waiting for transfers between devices, swap(): return lax.ppermute(array, axis, [(i, i ^ distance) for i in range(size)])  19.1 us
    all_to_all x1, blocking collectives, shards(): received = lax.all_to_all(heads_out, ('wide', 'narrow'), 0, 0, tiled=True)  10.4 us
    all_to_all x1, waiting for transfers between devices, shards(): queries = lax.all_to_all(packed, 'wide', 0, 0, tiled=True)  7.34 us
    all_to_all x1, starting transfers between devices, shards(): queries = lax.all_to_all(packed, 'wide', 0, 0, tiled=True)  7.29 us
    all_to_all x1, waiting for transfers between devices, shards(): total = jnp.sum(lax.all_to_all(down, 'wide', 0, 0, tiled=True), axis=0)  7.17 us
    pallas_call x1, Pallas kernels, shards(): call(functools.partial(attend_kernel, narrow, blocks, scale), (pltpu.VMEM...  5.38 us
    all_to_all x1, starting transfers between devices, shards(): total = jnp.sum(lax.all_to_all(down, 'wide', 0, 0, tiled=True), axis=0)  3.37 us
    ppermute x5, starting transfers between devices, swap(): return lax.ppermute(array, axis, [(i, i ^ distance) for i in range(size)])  2.66 us
  transfers between devices with their start and end apart: 7, of which 7 were waited for; matrix products, arithmetic and copies ran while one was open for 0% of the time, Pallas kernels for 0%

profile of v2, /device:TPU:0, one launch (start us, length us, event | category | flops | bytes accessed | tf_op | source)
XLA Modules:
  0.0 70.4 jit_solution(15104541370461146528)
XLA Ops:
  0.0 1.4 %pack.1 = bf16[8,2,16,256]{3,2,1,0:T(8,128)(2,1)} custom-call(bf16[2,16,128]{2,1,0:T(8,128)(2,1)} %nope_hbm.1, bf16[2,16,64]{2,1,0:T(8,128)(2,1)} %rope_hbm.1), custom_call_target="tpu_custom_call" | custom-call | tf_op jit(solution)/shard_map/pack/pallas_call | solution.py:296
  1.4 0.0 copy-start.1
  1.4 0.0 copy-start.2
  1.4 7.3 %all-to-all-start = ((bf16[8,2,16,256]{3,2,1,0:T(8,128)(2,1)}), bf16[8,2,16,256]{3,2,1,0:T(8,128)(2,1)S(1)}, u32[]{:S(2)}, u32[]{:S(2)}) async-start(bf16[8,2,16,256]{3,2,1,0:T(8,128)(2,1)} %pack.1), calls=%async_computation | async-start | bytes 262144 | tf_op jit(solution)/shard_map/all_to_all | solution.py:307
  8.7 7.3 %all-to-all-done.query_ref = bf16[8,2,16,256]{3,2,1,0:T(8,128)(2,1)S(1)} async-done(((bf16[8,2,16,256]{3,2,1,0:T(8,128)(2,1)}), bf16[8,2,16,256]{3,2,1,0:T(8,128)(2,1)S(1)}, u32[]{:S(2)}, u32[]{:S(2)}) %all-to-all-start) | async-done | bytes 131104 | tf_op jit(solution)/shard_map/all_to_all | solution.py:307
  16.1 0.0 slice-start.2
  16.1 0.0 copy-start.3
  16.1 0.0 slice-start.3
  16.1 0.0 copy-start
  16.1 5.4 %attend.1 = (bf16[32,16,128]{2,1,0:T(8,128)(2,1)S(1)}, bf16[1024,1792]{1,0:T(8,128)(2,1)S(1)}) custom-call(s32[1]{0:T(128)} %bitcast.group_ref, s32[16]{0:T(128)} %rows_ref.1, s32[2]{0:T(128)} %lengths_hbm.1, bf16[8,2,16,256]{3,2,1,0:T(8,128)(2,1)S(1)} %all-to-all-done.query_ref, bf16[16,128,512]{2,1,0:T(8,128)(2,1)} %key_hbm.1, ...), custom_call_target="tpu_custom_call" | custom-call | tf_op jit(solution)/shard_map/attend/pallas_call | solution.py:309
  21.5 10.4 %all_to_all.15.heads_ref = bf16[32,16,128]{2,1,0:T(8,128)(2,1)S(1)} all-to-all(bf16[32,16,128]{2,1,0:T(8,128)(2,1)S(1)} %get-tuple-element.9), channel_id=1, replica_groups=mesh['wide'=8,'narrow'=4] {'wide','narrow'}, dimensions={0} | all-to-all | bytes 262144 | tf_op jit(solution)/shard_map/all_to_all | solution.py:335
  31.9 0.0 copy-done.1
  31.9 0.0 copy-done.2
  31.9 1.2 %project.1 = bf16[16,1792]{1,0:T(8,128)(2,1)S(1)} custom-call(s32[16]{0:T(128)S(1)} %copy-done.2, s32[1]{0:T(128)} %bitcast.group_ref, bf16[32,16,128]{2,1,0:T(8,128)(2,1)S(1)} %all_to_all.15.heads_ref, bf16[2,1792]{1,0:T(2,128)(2,1)S(1)} %copy-done.1, bf16[1024,1792]{1,0:T(8,128)(2,1)S(1)} %get-tuple-element.10.weight_ref), custom_call_target="tpu_custom_call" | custom-call | tf_op jit(solution)/shard_map/project/pallas_call | solution.py:336
  33.1 0.7 %collective-permute-start = (bf16[16,1792]{1,0:T(8,128)(2,1)S(1)}, bf16[16,1792]{1,0:T(8,128)(2,1)S(1)}, u32[]{:S(2)}, u32[]{:S(2)}) collective-permute-start(bf16[16,1792]{1,0:T(8,128)(2,1)S(1)} %project.1), channel_id=1, source_target_pairs={{0,4},{4,0},{8,12},{12,8},{16,20},{20,16},{24,28},{28,24},{1,5},{5... | collective-permute-start | bytes 172040 | tf_op jit(solution)/shard_map/ppermute | solution.py:267
  33.9 3.5 %collective-permute-done = bf16[16,1792]{1,0:T(8,128)(2,1)S(1)} collective-permute-done((bf16[16,1792]{1,0:T(8,128)(2,1)S(1)}, bf16[16,1792]{1,0:T(8,128)(2,1)S(1)}, u32[]{:S(2)}, u32[]{:S(2)}) %collective-permute-start) | collective-permute-done | bytes 57376 | tf_op jit(solution)/shard_map/ppermute | solution.py:267
  37.4 0.7 %collective-permute-start.1 = (bf16[16,1792]{1,0:T(8,128)(2,1)S(1)}, bf16[16,1792]{1,0:T(8,128)(2,1)S(1)}, u32[]{:S(2)}, u32[]{:S(2)}) collective-permute-start(bf16[16,1792]{1,0:T(8,128)(2,1)S(1)} %add_convert_fusion.1), channel_id=1, source_target_pairs={{0,8},{4,12},{8,0},{12,4},{16,24},{20,28},{24,16},{28,20},{1,9},{5... | collective-permute-start | bytes 172040 | tf_op jit(solution)/shard_map/ppermute | solution.py:267
  38.1 3.5 %collective-permute-done.1 = bf16[16,1792]{1,0:T(8,128)(2,1)S(1)} collective-permute-done((bf16[16,1792]{1,0:T(8,128)(2,1)S(1)}, bf16[16,1792]{1,0:T(8,128)(2,1)S(1)}, u32[]{:S(2)}, u32[]{:S(2)}) %collective-permute-start.1) | collective-permute-done | bytes 57376 | tf_op jit(solution)/shard_map/ppermute | solution.py:267
  41.7 0.8 %collective-permute-start.2 = (bf16[16,1792]{1,0:T(8,128)(2,1)S(1)}, bf16[16,1792]{1,0:T(8,128)(2,1)S(1)}, u32[]{:S(2)}, u32[]{:S(2)}) collective-permute-start(bf16[16,1792]{1,0:T(8,128)(2,1)S(1)} %add_convert_fusion.first_ref), channel_id=1, source_target_pairs={{0,16},{4,20},{8,24},{12,28},{16,0},{20,4},{24,8},{28,12},{1,17},{... | collective-permute-start | bytes 172040 | tf_op jit(solution)/shard_map/ppermute | solution.py:267
  42.5 0.0 copy-done.3
  42.5 0.0 slice-start
  42.5 0.0 slice-start.1
  42.5 4.9 %collective-permute-done.2.second_ref = bf16[16,1792]{1,0:T(8,128)(2,1)S(1)} collective-permute-done((bf16[16,1792]{1,0:T(8,128)(2,1)S(1)}, bf16[16,1792]{1,0:T(8,128)(2,1)S(1)}, u32[]{:S(2)}, u32[]{:S(2)}) %collective-permute-start.2) | collective-permute-done | bytes 57376 | tf_op jit(solution)/shard_map/ppermute | solution.py:267
  47.4 0.0 slice-done.2
  47.4 0.0 slice-done.3
  47.4 0.0 copy-done
  47.4 2.2 %expand.1 = (f32[16,1792]{1,0:T(8,128)S(1)}, bf16[16,4864]{1,0:T(8,128)(2,1)S(1)}) custom-call(bf16[16,1792]{1,0:T(8,128)(2,1)S(1)} %add_convert_fusion.first_ref, bf16[16,1792]{1,0:T(8,128)(2,1)S(1)} %collective-permute-done.2.second_ref, bf16[1,1792]{1,0:T(2,128)(2,1)S(1)} %broadcast_in_dim.8.gain_ref, bf16[1792,2304]{1,0:T(8,128)(2,1)S(1)} %bitcast.5, ...), custom_call_target="tpu_custom_call" | custom-call | tf_op jit(solution)/shard_map/expand/pallas_call | solution.py:350
  49.7 0.0 collective-permute-start.3
  49.7 1.4 %collective-permute-done.3.second_ref = bf16[16,4864]{1,0:T(8,128)(2,1)S(1)} collective-permute-done((bf16[16,4864]{1,0:T(8,128)(2,1)S(1)}, bf16[16,4864]{1,0:T(8,128)(2,1)S(1)}, u32[]{:S(2)}, u32[]{:S(2)}) %collective-permute-start.3) | collective-permute-done | bytes 155680 | tf_op jit(solution)/shard_map/ppermute | solution.py:267
  51.1 0.1 merge.1.first_ref
  51.2 0.4 collective-permute-start.4
  51.5 5.8 %collective-permute-done.4.second_ref = bf16[16,4864]{1,0:T(8,128)(2,1)S(1)} collective-permute-done((bf16[16,4864]{1,0:T(8,128)(2,1)S(1)}, bf16[16,4864]{1,0:T(8,128)(2,1)S(1)}, u32[]{:S(2)}, u32[]{:S(2)}) %collective-permute-start.4) | collective-permute-done | bytes 155680 | tf_op jit(solution)/shard_map/ppermute | solution.py:267
  57.3 0.0 slice-done
  57.3 0.0 slice-done.1
  57.3 1.9 %contract.1 = f32[8,2,1792]{2,1,0:T(2,128)} custom-call(bf16[16,4864]{1,0:T(8,128)(2,1)S(1)} %merge.1.first_ref, bf16[16,4864]{1,0:T(8,128)(2,1)S(1)} %collective-permute-done.4.second_ref, bf16[2304,1792]{1,0:T(8,128)(2,1)S(1)} %bitcast.3), custom_call_target="tpu_custom_call" | custom-call | tf_op jit(solution)/shard_map/contract/pallas_call | solution.py:365
  59.2 3.4 %all-to-all-start.2 = ((f32[8,2,1792]{2,1,0:T(2,128)}), f32[8,2,1792]{2,1,0:T(2,128)S(1)}, u32[]{:S(2)}, u32[]{:S(2)}) async-start(f32[8,2,1792]{2,1,0:T(2,128)} %contract.1), calls=%async_computation.2 | async-start | bytes 229376 | tf_op jit(solution)/shard_map/all_to_all | solution.py:371
  62.6 7.2 %all-to-all-done.2 = f32[8,2,1792]{2,1,0:T(2,128)S(1)} async-done(((f32[8,2,1792]{2,1,0:T(2,128)}), f32[8,2,1792]{2,1,0:T(2,128)S(1)}, u32[]{:S(2)}, u32[]{:S(2)}) %all-to-all-start.2) | async-done | bytes 114720 | tf_op jit(solution)/shard_map/all_to_all | solution.py:371
  69.8 0.6 add_convert_fusion.2
  (6 shorter events, 0.1 us)
Async XLA Ops:
  1.4 30.5 %copy-start.1 = (bf16[2,1792]{1,0:T(2,128)(2,1)S(1)}, bf16[2,1792]{1,0:T(2,128)(2,1)}, u32[]{:S(2)}) copy-start(bf16[2,1792]{1,0:T(2,128)(2,1)} %residual_ref.1) | copy-start | bytes 21508
  1.4 30.5 %copy-start.2 = (s32[16]{0:T(128)S(1)}, s32[16]{0:T(128)}, u32[]{:S(2)}) copy-start(s32[16]{0:T(128)} %rows_ref.1) | copy-start | bytes 196
  1.4 14.6 %all-to-all-start = ((bf16[8,2,16,256]{3,2,1,0:T(8,128)(2,1)}), bf16[8,2,16,256]{3,2,1,0:T(8,128)(2,1)S(1)}, u32[]{:S(2)}, u32[]{:S(2)}) async-start(bf16[8,2,16,256]{3,2,1,0:T(8,128)(2,1)} %pack.1), calls=%async_computation | async-start | bytes 262144 | tf_op jit(solution)/shard_map/all_to_all | solution.py:307
  16.1 31.4 %slice-start.2 = ((s8[8257536]{0:T(1024)(128)(4,1)}), s8[4194304]{0:T(1024)(128)(4,1)S(1)}, s32[]{:S(2)}) async-start(s8[8257536]{0:T(1024)(128)(4,1)} %bitcast.4), calls=%async_computation.5 | async-start | bytes 8388608
  16.1 26.4 %copy-start.3 = (bf16[1792]{0:T(1024)(128)(2,1)S(1)}, bf16[1792]{0:T(1024)(128)(2,1)}, u32[]{:S(2)}) copy-start(bf16[1792]{0:T(1024)(128)(2,1)} %param.22) | copy-start | bytes 10756
  16.1 31.4 %slice-start.3 = ((s8[8257536]{0:T(1024)(128)(4,1)}), s8[4063232]{0:T(1024)(128)(4,1)S(1)}, s32[]{:S(2)}) async-start(s8[8257536]{0:T(1024)(128)(4,1)} %bitcast.4), calls=%async_computation.6 | async-start | bytes 8126464
  16.1 31.4 %copy-start = (bf16[1792,2304]{1,0:T(8,128)(2,1)S(1)}, bf16[1792,2304]{1,0:T(8,128)(2,1)}, u32[]{:S(2)}) copy-start(bf16[1792,2304]{1,0:T(8,128)(2,1)} %up_ref.1) | copy-start | bytes 24772612
  33.1 4.2 %collective-permute-start = (bf16[16,1792]{1,0:T(8,128)(2,1)S(1)}, bf16[16,1792]{1,0:T(8,128)(2,1)S(1)}, u32[]{:S(2)}, u32[]{:S(2)}) collective-permute-start(bf16[16,1792]{1,0:T(8,128)(2,1)S(1)} %project.1), channel_id=1, source_target_pairs={{0,4},{4,0},{8,12},{12,8},{16,20},{20,16},{24,28},{28,24},{1,5},{5... | collective-permute-start | bytes 172040 | tf_op jit(solution)/shard_map/ppermute | solution.py:267
  37.4 4.2 %collective-permute-start.1 = (bf16[16,1792]{1,0:T(8,128)(2,1)S(1)}, bf16[16,1792]{1,0:T(8,128)(2,1)S(1)}, u32[]{:S(2)}, u32[]{:S(2)}) collective-permute-start(bf16[16,1792]{1,0:T(8,128)(2,1)S(1)} %add_convert_fusion.1), channel_id=1, source_target_pairs={{0,8},{4,12},{8,0},{12,4},{16,24},{20,28},{24,16},{28,20},{1,9},{5... | collective-permute-start | bytes 172040 | tf_op jit(solution)/shard_map/ppermute | solution.py:267
  41.7 5.8 %collective-permute-start.2 = (bf16[16,1792]{1,0:T(8,128)(2,1)S(1)}, bf16[16,1792]{1,0:T(8,128)(2,1)S(1)}, u32[]{:S(2)}, u32[]{:S(2)}) collective-permute-start(bf16[16,1792]{1,0:T(8,128)(2,1)S(1)} %add_convert_fusion.first_ref), channel_id=1, source_target_pairs={{0,16},{4,20},{8,24},{12,28},{16,0},{20,4},{24,8},{28,12},{1,17},{... | collective-permute-start | bytes 172040 | tf_op jit(solution)/shard_map/ppermute | solution.py:267
  42.5 14.8 %slice-start = ((s8[8257536]{0:T(1024)(128)(4,1)}), s8[4194304]{0:T(1024)(128)(4,1)S(1)}, s32[]{:S(2)}) async-start(s8[8257536]{0:T(1024)(128)(4,1)} %bitcast.2), calls=%async_computation.3 | async-start | bytes 8388608
  42.5 14.8 %slice-start.1 = ((s8[8257536]{0:T(1024)(128)(4,1)}), s8[4063232]{0:T(1024)(128)(4,1)S(1)}, s32[]{:S(2)}) async-start(s8[8257536]{0:T(1024)(128)(4,1)} %bitcast.2), calls=%async_computation.4 | async-start | bytes 8126464
  49.7 1.4 %collective-permute-start.3 = (bf16[16,4864]{1,0:T(8,128)(2,1)S(1)}, bf16[16,4864]{1,0:T(8,128)(2,1)S(1)}, u32[]{:S(2)}, u32[]{:S(2)}) collective-permute-start(bf16[16,4864]{1,0:T(8,128)(2,1)S(1)} %get-tuple-element.12.first_ref), channel_id=1, source_target_pairs={{0,1},{1,0},{2,3},{3,2},{4,5},{5,4},{6,7},{7,6},{8,9},{9,8},{10,11... | collective-permute-start | bytes 466952 | tf_op jit(solution)/shard_map/ppermute | solution.py:267
  51.2 6.1 %collective-permute-start.4 = (bf16[16,4864]{1,0:T(8,128)(2,1)S(1)}, bf16[16,4864]{1,0:T(8,128)(2,1)S(1)}, u32[]{:S(2)}, u32[]{:S(2)}) collective-permute-start(bf16[16,4864]{1,0:T(8,128)(2,1)S(1)} %merge.1.first_ref), channel_id=1, source_target_pairs={{0,2},{1,3},{2,0},{3,1},{4,6},{5,7},{6,4},{7,5},{8,10},{9,11},{10,... | collective-permute-start | bytes 466952 | tf_op jit(solution)/shard_map/ppermute | solution.py:267
  59.2 10.5 %all-to-all-start.2 = ((f32[8,2,1792]{2,1,0:T(2,128)}), f32[8,2,1792]{2,1,0:T(2,128)S(1)}, u32[]{:S(2)}, u32[]{:S(2)}) async-start(f32[8,2,1792]{2,1,0:T(2,128)} %contract.1), calls=%async_computation.2 | async-start | bytes 229376 | tf_op jit(solution)/shard_map/all_to_all | solution.py:371

commit v3 on v2

--- a/solution.py
+++ b/solution.py
@@ -33,7 +33,7 @@
     )
 
 
-def pack_kernel(nope_hbm, rope_hbm, out_ref, nope_ref, rope_ref, sems):
+def pack_kernel(group_ref, nope_hbm, rope_hbm, out_ref, nope_ref, rope_ref, sems):
     copies = [
         pltpu.make_async_copy(nope_hbm, nope_ref, sems.at[0]),
         pltpu.make_async_copy(rope_hbm, rope_ref, sems.at[1]),
@@ -225,9 +225,15 @@
     return ref[:, start : start + 1].astype(F32) + ref[:, start + 128 : start + 129].astype(F32)
 
 
-def expand_kernel(first_ref, second_ref, gain_ref, gate_ref, up_ref, middle_ref, out_ref):
+def expand_kernel(
+    group_ref, first_ref, second_ref, gain_ref, gate_ref, up_ref, middle_ref, out_ref
+):
     middle = first_ref[...].astype(F32) + second_ref[...].astype(F32)
-    middle_ref[...] = middle
+    slots = middle_ref.shape[0]
+    row = lax.broadcasted_iota(jnp.int32, (middle.shape[0], 1), 0)
+    for slot in range(slots):
+        own = jnp.where(row == group_ref[0] * slots + slot, middle, 0.0)
+        middle_ref[slot : slot + 1] = jnp.sum(own, axis=0, keepdims=True)
     columns = gate_ref.shape[1]
     padded = (out_ref.shape[1] - 256) // 2
     scaled = (middle * gain_ref[...].astype(F32)).astype(BF16)
@@ -296,14 +302,14 @@
     packed = call(
         pack_kernel,
         pltpu.VMEM((wide, slots, heads, head_size + 128), BF16),
-        [HBM] * 2,
+        [SMEM, HBM, HBM],
         "pack",
         [
             pltpu.VMEM(query_nope.shape, BF16),
             pltpu.VMEM(query_rope.shape, BF16),
             pltpu.SemaphoreType.DMA((2,)),
         ],
-    )(far(query_nope), far(query_rope))
+    )(group[None], far(query_nope), far(query_rope))
     queries = lax.all_to_all(packed, "wide", 0, 0, tiled=True)
     cache = jnp.swapaxes(latent_cache, 1, 2)
     heads_out, out_weight = call(
@@ -350,12 +356,12 @@
     middle, terms = call(
         expand_kernel,
         (
-            pltpu.VMEM((rows, features), F32),
+            pltpu.VMEM((slots, features), F32),
             pltpu.VMEM((rows, 2 * padded + 256), BF16),
         ),
-        [VMEM] * 5,
+        [SMEM] + [VMEM] * 5,
         "expand",
-    )(summed, other, norm_gain[None, :], gate_weight, up_weight)
+    )(group[None], summed, other, norm_gain[None, :], gate_weight, up_weight)
     distance = 1
     while distance < narrow:
         other = swap(terms, "narrow", distance, narrow)
@@ -369,7 +375,7 @@
         "contract",
     )(terms, other, down_weight)
     total = jnp.sum(lax.all_to_all(down, "wide", 0, 0, tiled=True), axis=0)
-    return (lax.dynamic_slice_in_dim(middle, group * slots, slots) + total).astype(BF16)
+    return (middle + total).astype(BF16)
 
 
 def terms_like(array):

time: 70.9 us -> 68.4 us (0.965)
  blocking collectives: 10.4 us -> 34.6 us
  waiting for transfers between devices: 33.6 us -> 19.1 us
  starting transfers between devices: 13.3 us -> 2.67 us
  Pallas kernels: 12.3 us -> 10.9 us
    all_to_all x0 -> x2, blocking collectives: none -> 24.2 us  [the longest x1 14.4 us: shards(): queries = lax.all_to_all(packed, 'wide', 0, 0, tiled=True)]
    all_to_all x2 -> x0, waiting for transfers between devices: 14.5 us -> none  [the longest x1 7.34 us: shards(): queries = lax.all_to_all(packed, 'wide', 0, 0, tiled=True)]
    all_to_all x2 -> x0, starting transfers between devices: 10.7 us -> none  [the longest x1 7.29 us: shards(): queries = lax.all_to_all(packed, 'wide', 0, 0, tiled=True)]
  transfers between devices with their start and end apart: 7 -> 5, of which waited for: 7 -> 5; matrix products, arithmetic and copies ran while one was open for 0% -> 0% of each run, Pallas kernels for 0% -> 0%
where the time goes in v3:
time: 68.4 us; the launch traced here: 68.1 us
  blocking collectives  34.6 us (51%)
  waiting for transfers between devices  19.1 us (28%)
  Pallas kernels  10.9 us (16%)
  starting transfers between devices  2.67 us (4%)
    ppermute x5, waiting for transfers between devices, swap(): return lax.ppermute(array, axis, [(i, i ^ distance) for i in range(size)])  19.1 us
    all_to_all x1, blocking collectives, shards(): queries = lax.all_to_all(packed, 'wide', 0, 0, tiled=True)  14.4 us
    all_to_all x1, blocking collectives, shards(): received = lax.all_to_all(heads_out, ('wide', 'narrow'), 0, 0, tiled=True)  10.4 us
    all_to_all x1, blocking collectives, shards(): total = jnp.sum(lax.all_to_all(down, 'wide', 0, 0, tiled=True), axis=0)  9.74 us
    pallas_call x1, Pallas kernels, shards(): call(functools.partial(attend_kernel, narrow, blocks, scale), (pltpu.VMEM...  5.38 us
    ppermute x5, starting transfers between devices, swap(): return lax.ppermute(array, axis, [(i, i ^ distance) for i in range(size)])  2.67 us
    pallas_call x1, Pallas kernels, shards(): call(expand_kernel, (pltpu.VMEM((slots, features), F32), pltpu.VMEM((rows...  2.25 us
  transfers between devices with their start and end apart: 5, of which 5 were waited for; matrix products, arithmetic and copies ran while one was open for 0% of the time, Pallas kernels for 0%

profile of v3, /device:TPU:0, one launch (start us, length us, event | category | flops | bytes accessed | tf_op | source)
XLA Modules:
  0.0 68.1 jit_solution(14908662327430981655)
XLA Ops:
  0.0 0.7 %pack.1 = bf16[8,2,16,256]{3,2,1,0:T(8,128)(2,1)S(1)} custom-call(s32[1]{0:T(128)} %bitcast.group_ref, bf16[2,16,128]{2,1,0:T(8,128)(2,1)} %nope_hbm.1, bf16[2,16,64]{2,1,0:T(8,128)(2,1)} %rope_hbm.1), custom_call_target="tpu_custom_call" | custom-call | tf_op jit(solution)/shard_map/pack/pallas_call | solution.py:302
  0.7 0.0 copy-start.1
  0.8 0.0 copy-start.2
  0.8 14.4 %all_to_all.15.query_ref = bf16[8,2,16,256]{3,2,1,0:T(8,128)(2,1)S(1)} all-to-all(bf16[8,2,16,256]{3,2,1,0:T(8,128)(2,1)S(1)} %pack.1), channel_id=1, replica_groups=mesh['wide'=8,'narrow'=4] {'wide'}, dimensions={0} | all-to-all | bytes 262144 | tf_op jit(solution)/shard_map/all_to_all | solution.py:313
  15.2 0.0 slice-start
  15.2 0.0 copy-start.3
  15.2 0.0 slice-start.1
  15.2 0.0 copy-start
  15.2 5.4 %attend.1 = (bf16[32,16,128]{2,1,0:T(8,128)(2,1)S(1)}, bf16[1024,1792]{1,0:T(8,128)(2,1)S(1)}) custom-call(s32[1]{0:T(128)} %bitcast.group_ref, s32[16]{0:T(128)} %rows_ref.1, s32[2]{0:T(128)} %lengths_hbm.1, bf16[8,2,16,256]{3,2,1,0:T(8,128)(2,1)S(1)} %all_to_all.15.query_ref, bf16[16,128,512]{2,1,0:T(8,128)(2,1)} %key_hbm.1, ...), custom_call_target="tpu_custom_call" | custom-call | tf_op jit(solution)/shard_map/attend/pallas_call | solution.py:315
  20.6 10.4 %all_to_all.16.heads_ref = bf16[32,16,128]{2,1,0:T(8,128)(2,1)S(1)} all-to-all(bf16[32,16,128]{2,1,0:T(8,128)(2,1)S(1)} %get-tuple-element.9), channel_id=1, replica_groups=mesh['wide'=8,'narrow'=4] {'wide','narrow'}, dimensions={0} | all-to-all | bytes 262144 | tf_op jit(solution)/shard_map/all_to_all | solution.py:341
  31.0 0.0 copy-done.1
  31.0 0.0 copy-done.2
  31.0 1.2 %project.1 = bf16[16,1792]{1,0:T(8,128)(2,1)S(1)} custom-call(s32[16]{0:T(128)S(1)} %copy-done.2, s32[1]{0:T(128)} %bitcast.group_ref, bf16[32,16,128]{2,1,0:T(8,128)(2,1)S(1)} %all_to_all.16.heads_ref, bf16[2,1792]{1,0:T(2,128)(2,1)S(1)} %copy-done.1, bf16[1024,1792]{1,0:T(8,128)(2,1)S(1)} %get-tuple-element.10.weight_ref), custom_call_target="tpu_custom_call" | custom-call | tf_op jit(solution)/shard_map/project/pallas_call | solution.py:342
  32.3 0.7 %collective-permute-start = (bf16[16,1792]{1,0:T(8,128)(2,1)S(1)}, bf16[16,1792]{1,0:T(8,128)(2,1)S(1)}, u32[]{:S(2)}, u32[]{:S(2)}) collective-permute-start(bf16[16,1792]{1,0:T(8,128)(2,1)S(1)} %project.1), channel_id=1, source_target_pairs={{0,4},{4,0},{8,12},{12,8},{16,20},{20,16},{24,28},{28,24},{1,5},{5... | collective-permute-start | bytes 172040 | tf_op jit(solution)/shard_map/ppermute | solution.py:273
  33.0 3.5 %collective-permute-done = bf16[16,1792]{1,0:T(8,128)(2,1)S(1)} collective-permute-done((bf16[16,1792]{1,0:T(8,128)(2,1)S(1)}, bf16[16,1792]{1,0:T(8,128)(2,1)S(1)}, u32[]{:S(2)}, u32[]{:S(2)}) %collective-permute-start) | collective-permute-done | bytes 57376 | tf_op jit(solution)/shard_map/ppermute | solution.py:273
  36.5 0.7 %collective-permute-start.1 = (bf16[16,1792]{1,0:T(8,128)(2,1)S(1)}, bf16[16,1792]{1,0:T(8,128)(2,1)S(1)}, u32[]{:S(2)}, u32[]{:S(2)}) collective-permute-start(bf16[16,1792]{1,0:T(8,128)(2,1)S(1)} %add_convert_fusion.1), channel_id=1, source_target_pairs={{0,8},{4,12},{8,0},{12,4},{16,24},{20,28},{24,16},{28,20},{1,9},{5... | collective-permute-start | bytes 172040 | tf_op jit(solution)/shard_map/ppermute | solution.py:273
  37.2 3.5 %collective-permute-done.1 = bf16[16,1792]{1,0:T(8,128)(2,1)S(1)} collective-permute-done((bf16[16,1792]{1,0:T(8,128)(2,1)S(1)}, bf16[16,1792]{1,0:T(8,128)(2,1)S(1)}, u32[]{:S(2)}, u32[]{:S(2)}) %collective-permute-start.1) | collective-permute-done | bytes 57376 | tf_op jit(solution)/shard_map/ppermute | solution.py:273
  40.8 0.9 %collective-permute-start.2 = (bf16[16,1792]{1,0:T(8,128)(2,1)S(1)}, bf16[16,1792]{1,0:T(8,128)(2,1)S(1)}, u32[]{:S(2)}, u32[]{:S(2)}) collective-permute-start(bf16[16,1792]{1,0:T(8,128)(2,1)S(1)} %add_convert_fusion.first_ref), channel_id=1, source_target_pairs={{0,16},{4,20},{8,24},{12,28},{16,0},{20,4},{24,8},{28,12},{1,17},{... | collective-permute-start | bytes 172040 | tf_op jit(solution)/shard_map/ppermute | solution.py:273
  41.6 0.0 copy-done.3
  41.6 0.0 slice-start.2
  41.7 0.0 slice-start.3
  41.7 4.9 %collective-permute-done.2.second_ref = bf16[16,1792]{1,0:T(8,128)(2,1)S(1)} collective-permute-done((bf16[16,1792]{1,0:T(8,128)(2,1)S(1)}, bf16[16,1792]{1,0:T(8,128)(2,1)S(1)}, u32[]{:S(2)}, u32[]{:S(2)}) %collective-permute-start.2) | collective-permute-done | bytes 57376 | tf_op jit(solution)/shard_map/ppermute | solution.py:273
  46.5 0.0 slice-done
  46.5 0.0 slice-done.1
  46.6 0.0 copy-done
  46.6 2.2 %expand.1 = (f32[2,1792]{1,0:T(2,128)S(1)}, bf16[16,4864]{1,0:T(8,128)(2,1)S(1)}) custom-call(s32[1]{0:T(128)} %bitcast.group_ref, bf16[16,1792]{1,0:T(8,128)(2,1)S(1)} %add_convert_fusion.first_ref, bf16[16,1792]{1,0:T(8,128)(2,1)S(1)} %collective-permute-done.2.second_ref, bf16[1,1792]{1,0:T(2,128)(2,1)S(1)} %broadcast_in_dim.10.gain_ref, ...), custom_call_target="tpu_custom_call" | custom-call | tf_op jit(solution)/shard_map/expand/pallas_call | solution.py:356
  48.8 0.0 collective-permute-start.3
  48.8 1.4 %collective-permute-done.3.second_ref = bf16[16,4864]{1,0:T(8,128)(2,1)S(1)} collective-permute-done((bf16[16,4864]{1,0:T(8,128)(2,1)S(1)}, bf16[16,4864]{1,0:T(8,128)(2,1)S(1)}, u32[]{:S(2)}, u32[]{:S(2)}) %collective-permute-start.3) | collective-permute-done | bytes 155680 | tf_op jit(solution)/shard_map/ppermute | solution.py:273
  50.2 0.1 merge.1.first_ref
  50.3 0.4 collective-permute-start.4
  50.7 5.8 %collective-permute-done.4.second_ref = bf16[16,4864]{1,0:T(8,128)(2,1)S(1)} collective-permute-done((bf16[16,4864]{1,0:T(8,128)(2,1)S(1)}, bf16[16,4864]{1,0:T(8,128)(2,1)S(1)}, u32[]{:S(2)}, u32[]{:S(2)}) %collective-permute-start.4) | collective-permute-done | bytes 155680 | tf_op jit(solution)/shard_map/ppermute | solution.py:273
  56.4 0.0 slice-done.2
  56.4 0.0 slice-done.3
  56.4 1.3 %contract.1 = f32[8,2,1792]{2,1,0:T(2,128)S(1)} custom-call(bf16[16,4864]{1,0:T(8,128)(2,1)S(1)} %merge.1.first_ref, bf16[16,4864]{1,0:T(8,128)(2,1)S(1)} %collective-permute-done.4.second_ref, bf16[2304,1792]{1,0:T(8,128)(2,1)S(1)} %bitcast.5), custom_call_target="tpu_custom_call" | custom-call | tf_op jit(solution)/shard_map/contract/pallas_call | solution.py:371
  57.7 9.7 %all_to_all.17 = f32[8,2,1792]{2,1,0:T(2,128)S(1)} all-to-all(f32[8,2,1792]{2,1,0:T(2,128)S(1)} %contract.1), channel_id=1, replica_groups=mesh['wide'=8,'narrow'=4] {'wide'}, dimensions={0} | all-to-all | bytes 229376 | tf_op jit(solution)/shard_map/all_to_all | solution.py:377
  67.5 0.6 add_convert_fusion.2
  (6 shorter events, 0.1 us)
Async XLA Ops:
  0.7 30.3 %copy-start.1 = (bf16[2,1792]{1,0:T(2,128)(2,1)S(1)}, bf16[2,1792]{1,0:T(2,128)(2,1)}, u32[]{:S(2)}) copy-start(bf16[2,1792]{1,0:T(2,128)(2,1)} %residual_ref.1) | copy-start | bytes 21508
  0.8 30.3 %copy-start.2 = (s32[16]{0:T(128)S(1)}, s32[16]{0:T(128)}, u32[]{:S(2)}) copy-start(s32[16]{0:T(128)} %rows_ref.1) | copy-start | bytes 196
  15.2 31.4 %slice-start = ((s8[8257536]{0:T(1024)(128)(4,1)}), s8[4194304]{0:T(1024)(128)(4,1)S(1)}, s32[]{:S(2)}) async-start(s8[8257536]{0:T(1024)(128)(4,1)} %bitcast.2), calls=%async_computation.3 | async-start | bytes 8388608
  15.2 26.4 %copy-start.3 = (bf16[1792]{0:T(1024)(128)(2,1)S(1)}, bf16[1792]{0:T(1024)(128)(2,1)}, u32[]{:S(2)}) copy-start(bf16[1792]{0:T(1024)(128)(2,1)} %param.22) | copy-start | bytes 10756
  15.2 31.4 %slice-start.1 = ((s8[8257536]{0:T(1024)(128)(4,1)}), s8[4063232]{0:T(1024)(128)(4,1)S(1)}, s32[]{:S(2)}) async-start(s8[8257536]{0:T(1024)(128)(4,1)} %bitcast.2), calls=%async_computation.4 | async-start | bytes 8126464
  15.2 31.4 %copy-start = (bf16[1792,2304]{1,0:T(8,128)(2,1)S(1)}, bf16[1792,2304]{1,0:T(8,128)(2,1)}, u32[]{:S(2)}) copy-start(bf16[1792,2304]{1,0:T(8,128)(2,1)} %up_ref.1) | copy-start | bytes 24772612
  32.3 4.2 %collective-permute-start = (bf16[16,1792]{1,0:T(8,128)(2,1)S(1)}, bf16[16,1792]{1,0:T(8,128)(2,1)S(1)}, u32[]{:S(2)}, u32[]{:S(2)}) collective-permute-start(bf16[16,1792]{1,0:T(8,128)(2,1)S(1)} %project.1), channel_id=1, source_target_pairs={{0,4},{4,0},{8,12},{12,8},{16,20},{20,16},{24,28},{28,24},{1,5},{5... | collective-permute-start | bytes 172040 | tf_op jit(solution)/shard_map/ppermute | solution.py:273
  36.5 4.2 %collective-permute-start.1 = (bf16[16,1792]{1,0:T(8,128)(2,1)S(1)}, bf16[16,1792]{1,0:T(8,128)(2,1)S(1)}, u32[]{:S(2)}, u32[]{:S(2)}) collective-permute-start(bf16[16,1792]{1,0:T(8,128)(2,1)S(1)} %add_convert_fusion.1), channel_id=1, source_target_pairs={{0,8},{4,12},{8,0},{12,4},{16,24},{20,28},{24,16},{28,20},{1,9},{5... | collective-permute-start | bytes 172040 | tf_op jit(solution)/shard_map/ppermute | solution.py:273
  40.8 5.8 %collective-permute-start.2 = (bf16[16,1792]{1,0:T(8,128)(2,1)S(1)}, bf16[16,1792]{1,0:T(8,128)(2,1)S(1)}, u32[]{:S(2)}, u32[]{:S(2)}) collective-permute-start(bf16[16,1792]{1,0:T(8,128)(2,1)S(1)} %add_convert_fusion.first_ref), channel_id=1, source_target_pairs={{0,16},{4,20},{8,24},{12,28},{16,0},{20,4},{24,8},{28,12},{1,17},{... | collective-permute-start | bytes 172040 | tf_op jit(solution)/shard_map/ppermute | solution.py:273
  41.6 14.8 %slice-start.2 = ((s8[8257536]{0:T(1024)(128)(4,1)}), s8[4194304]{0:T(1024)(128)(4,1)S(1)}, s32[]{:S(2)}) async-start(s8[8257536]{0:T(1024)(128)(4,1)} %bitcast.4), calls=%async_computation.5 | async-start | bytes 8388608
  41.7 14.8 %slice-start.3 = ((s8[8257536]{0:T(1024)(128)(4,1)}), s8[4063232]{0:T(1024)(128)(4,1)S(1)}, s32[]{:S(2)}) async-start(s8[8257536]{0:T(1024)(128)(4,1)} %bitcast.4), calls=%async_computation.6 | async-start | bytes 8126464
  48.8 1.4 %collective-permute-start.3 = (bf16[16,4864]{1,0:T(8,128)(2,1)S(1)}, bf16[16,4864]{1,0:T(8,128)(2,1)S(1)}, u32[]{:S(2)}, u32[]{:S(2)}) collective-permute-start(bf16[16,4864]{1,0:T(8,128)(2,1)S(1)} %get-tuple-element.12.first_ref), channel_id=1, source_target_pairs={{0,1},{1,0},{2,3},{3,2},{4,5},{5,4},{6,7},{7,6},{8,9},{9,8},{10,11... | collective-permute-start | bytes 466952 | tf_op jit(solution)/shard_map/ppermute | solution.py:273
  50.3 6.1 %collective-permute-start.4 = (bf16[16,4864]{1,0:T(8,128)(2,1)S(1)}, bf16[16,4864]{1,0:T(8,128)(2,1)S(1)}, u32[]{:S(2)}, u32[]{:S(2)}) collective-permute-start(bf16[16,4864]{1,0:T(8,128)(2,1)S(1)} %merge.1.first_ref), channel_id=1, source_target_pairs={{0,2},{1,3},{2,0},{3,1},{4,6},{5,7},{6,4},{7,5},{8,10},{9,11},{10,... | collective-permute-start | bytes 466952 | tf_op jit(solution)/shard_map/ppermute | solution.py:273

commit v4 on v3

--- a/solution.py
+++ b/solution.py
@@ -17,15 +17,28 @@
 NT = (((1,), (1,)), ((), ()))
 
 
+PACK = 10 * 10**9
+ATTEND = 15 * 10**9
+PROJECT = 12 * 10**9
+EXPAND = 4 * 10**9
+MERGE = 4 * 10**9
+CONTRACT = 4 * 10**9
+
+
+def near(array):
+    return pltpu.with_memory_space_constraint(array, pltpu.VMEM)
+
+
 def far(array):
     return pltpu.with_memory_space_constraint(array, pltpu.HBM)
 
 
-def call(kernel, out_shape, in_specs, name, scratch=()):
+def call(kernel, out_shape, in_specs, name, scratch=(), flops=0):
     return pl.pallas_call(
         kernel,
         out_shape=out_shape,
         scratch_shapes=scratch,
+        cost_estimate=pl.CostEstimate(flops=flops, transcendentals=0, bytes_accessed=0),
         in_specs=in_specs,
         out_specs=jax.tree.map(lambda _: VMEM, out_shape),
         compiler_params=pltpu.CompilerParams(vmem_limit_bytes=16 * 1024 * 1024),
@@ -49,71 +62,23 @@
         out_ref[target] = row
 
 
-class Fetch:
-    def __init__(self, source, target, sems, first, parts):
-        self.copies = [
-            pltpu.make_async_copy(source.at[part], target.at[part], sems.at[first + index])
-            for index, part in enumerate(parts)
-        ]
-
-    def start(self):
-        for copy in self.copies:
-            copy.start()
-        return self
-
-    def wait(self, first=0, last=None):
-        for copy in self.copies[first:last]:
-            copy.wait()
-
-
-def halves(size):
-    if size % 32:
-        return [pl.ds(0, size)]
-    return [pl.ds(0, size // 2), pl.ds(size // 2, size // 2)]
-
-
 def attend_kernel(
     narrow,
     blocks,
     scale,
     group_ref,
-    rows_hbm,
-    lengths_hbm,
-    query_ref,
-    key_hbm,
-    cache_hbm,
-    value_hbm,
-    weight_hbm,
-    out_ref,
-    weight_ref,
     rows_ref,
     lengths_ref,
+    query_ref,
     key_ref,
     cache_ref,
     value_ref,
-    sems,
+    out_ref,
 ):
     slots, latent = cache_ref.shape[0], value_ref.shape[1]
     heads, head_size = key_ref.shape[0], key_ref.shape[1]
     rope = cache_ref.shape[1] - latent
     span = cache_ref.shape[2]
-    small = [
-        pltpu.make_async_copy(rows_hbm, rows_ref, sems.at[0]),
-        pltpu.make_async_copy(lengths_hbm, lengths_ref, sems.at[1]),
-    ]
-    for copy in small:
-        copy.start()
-    key = Fetch(key_hbm, key_ref, sems, 2, [pl.ds(0, heads // 2), pl.ds(heads // 2, heads // 2)]).start()
-    wide_cut = [(slot, part) for slot in range(slots) for part in halves(cache_ref.shape[1])]
-    cache = Fetch(cache_hbm, cache_ref, sems, 4, wide_cut).start()
-    value = Fetch(
-        value_hbm, value_ref, sems, 4 + 2 * slots, [pl.ds(0, heads // 2), pl.ds(heads // 2, heads // 2)]
-    ).start()
-    weight = Fetch(
-        weight_hbm, weight_ref, sems, 6 + 2 * slots, halves(weight_ref.shape[0])
-    ).start()
-    for copy in small:
-        copy.wait()
     group = group_ref[0]
     queries = []
     for slot in range(slots):
@@ -126,15 +91,12 @@
     spread = jnp.concatenate(
         [jnp.where(own_head == head, nope, zero) for head in range(heads)], axis=1
     )
-    key.wait()
     query_latent = jnp.dot(
         spread, key_ref[...].reshape(heads * head_size, latent), preferred_element_type=F32
     ).astype(BF16)
     contexts = []
     for slot in range(slots):
         part = slice(slot * heads, (slot + 1) * heads)
-        per_slot = len(wide_cut) // slots
-        cache.wait(slot * per_slot, (slot + 1) * per_slot)
         scores = jnp.dot(
             query_latent[part], cache_ref[slot, :latent, :], preferred_element_type=F32
         ) + jnp.dot(
@@ -155,7 +117,6 @@
     spread = jnp.concatenate(
         [jnp.where(own_head == head, context, zero) for head in range(heads)], axis=1
     )
-    value.wait()
     heads_out = jnp.dot(
         spread, value_ref[...].reshape(heads * latent, head_size), preferred_element_type=F32
     ).astype(BF16)
@@ -174,7 +135,6 @@
         )
     for target in range(out_ref.shape[0]):
         out_ref[target] = pieces[(target // narrow) % blocks]
-    weight.wait()
 
 
 def project_kernel(narrow, blocks, rows_ref, group_ref, heads_ref, residual_ref, weight_ref, out_ref):
@@ -309,34 +269,24 @@
             pltpu.VMEM(query_rope.shape, BF16),
             pltpu.SemaphoreType.DMA((2,)),
         ],
+        flops=PACK,
     )(group[None], far(query_nope), far(query_rope))
     queries = lax.all_to_all(packed, "wide", 0, 0, tiled=True)
     cache = jnp.swapaxes(latent_cache, 1, 2)
-    heads_out, out_weight = call(
+    heads_out = call(
         functools.partial(attend_kernel, narrow, blocks, scale),
-        (
-            pltpu.VMEM((wide * narrow, slots * per_block, head_size), BF16),
-            pltpu.VMEM(out_proj.shape, BF16),
-        ),
-        [SMEM, HBM, HBM, VMEM, HBM, HBM, HBM, HBM],
+        pltpu.VMEM((wide * narrow, slots * per_block, head_size), BF16),
+        [SMEM, SMEM, SMEM, VMEM, VMEM, VMEM, VMEM],
         "attend",
-        [
-            pltpu.SMEM(slot_rows.shape, jnp.int32),
-            pltpu.SMEM(cache_lengths.shape, jnp.int32),
-            pltpu.VMEM(absorb_key.shape, BF16),
-            pltpu.VMEM(cache.shape, BF16),
-            pltpu.VMEM(absorb_value.shape, BF16),
-            pltpu.SemaphoreType.DMA((8 + 2 * slots,)),
-        ],
+        flops=ATTEND,
     )(
         group[None],
-        far(slot_rows),
-        far(cache_lengths),
+        slot_rows,
+        cache_lengths,
         queries,
-        far(absorb_key),
-        far(cache),
-        far(absorb_value),
-        far(out_proj),
+        near(absorb_key),
+        near(cache),
+        near(absorb_value),
     )
     received = lax.all_to_all(heads_out, ("wide", "narrow"), 0, 0, tiled=True)
     summed = call(
@@ -344,7 +294,8 @@
         pltpu.VMEM((rows, features), BF16),
         [SMEM, SMEM, VMEM, VMEM, VMEM],
         "project",
-    )(slot_rows, group[None], received, residual_in, out_weight)
+        flops=PROJECT,
+    )(slot_rows, group[None], received, residual_in, out_proj)
     distance = 1
     while distance < wide:
         other = swap(summed, "wide", distance, wide)
@@ -361,18 +312,20 @@
         ),
         [SMEM] + [VMEM] * 5,
         "expand",
+        flops=EXPAND,
     )(group[None], summed, other, norm_gain[None, :], gate_weight, up_weight)
     distance = 1
     while distance < narrow:
         other = swap(terms, "narrow", distance, narrow)
         distance *= 2
         if distance < narrow:
-            terms = call(merge_kernel, terms_like(terms), [VMEM] * 2, "merge")(terms, other)
+            terms = call(merge_kernel, terms_like(terms), [VMEM] * 2, "merge", flops=MERGE)(terms, other)
     down = call(
         contract_kernel,
         pltpu.VMEM((wide, slots, features), F32),
         [VMEM] * 3,
         "contract",
+        flops=CONTRACT,
     )(terms, other, down_weight)
     total = jnp.sum(lax.all_to_all(down, "wide", 0, 0, tiled=True), axis=0)
     return (middle + total).astype(BF16)

time: 68.4 us -> 67.2 us (0.982)
  Pallas kernels: 10.9 us -> 9.37 us
    pallas_call x2, Pallas kernels: 5.46 us -> 3.72 us  [the longest x1 3.64 us: shards(): call(functools.partial(attend_kernel, narrow, blocks, scale), pltpu.VMEM(...]
where the time goes in v4:
time: 67.2 us; the launch traced here: 66.9 us
  blocking collectives  34.9 us (52%)
  waiting for transfers between devices  19.1 us (28%)
  Pallas kernels  9.37 us (14%)
  starting transfers between devices  2.67 us (4%)
  other arithmetic  0.68 us (1%)
    ppermute x5, waiting for transfers between devices, swap(): return lax.ppermute(array, axis, [(i, i ^ distance) for i in range(size)])  19.1 us
    all_to_all x1, blocking collectives, shards(): queries = lax.all_to_all(packed, 'wide', 0, 0, tiled=True)  14.7 us
    all_to_all x1, blocking collectives, shards(): received = lax.all_to_all(heads_out, ('wide', 'narrow'), 0, 0, tiled=True)  10.4 us
    all_to_all x1, blocking collectives, shards(): total = jnp.sum(lax.all_to_all(down, 'wide', 0, 0, tiled=True), axis=0)  9.75 us
    pallas_call x1, Pallas kernels, shards(): call(functools.partial(attend_kernel, narrow, blocks, scale), pltpu.VMEM(...  3.64 us
    ppermute x5, starting transfers between devices, swap(): return lax.ppermute(array, axis, [(i, i ^ distance) for i in range(size)])  2.67 us
    pallas_call x1, Pallas kernels, shards(): call(expand_kernel, (pltpu.VMEM((slots, features), F32), pltpu.VMEM((rows...  2.25 us
  transfers between devices with their start and end apart: 5, of which 5 were waited for; matrix products, arithmetic and copies ran while one was open for 0% of the time, Pallas kernels for 0%

profile of v4, /device:TPU:0, one launch (start us, length us, event | category | flops | bytes accessed | tf_op | source)
XLA Modules:
  0.0 66.9 jit_solution(9161565644775976532)
XLA Ops:
  0.0 0.0 copy-start
  0.0 0.0 copy-start.2
  0.0 0.0 copy-start.3
  0.0 0.0 copy-start.5
  0.0 0.0 copy-start.6
  0.0 0.0 slice-start
  0.0 0.0 slice-start.2
  0.0 0.9 %pack.1 = bf16[8,2,16,256]{3,2,1,0:T(8,128)(2,1)S(1)} custom-call(s32[1]{0:T(128)} %bitcast.group_ref, bf16[2,16,128]{2,1,0:T(8,128)(2,1)} %nope_hbm.1, bf16[2,16,64]{2,1,0:T(8,128)(2,1)} %rope_hbm.1), custom_call_target="tpu_custom_call" | custom-call | flops 10000000000 | tf_op jit(solution)/shard_map/pack/pallas_call | solution.py:262
  0.9 14.7 %all_to_all.15.query_ref = bf16[8,2,16,256]{3,2,1,0:T(8,128)(2,1)S(1)} all-to-all(bf16[8,2,16,256]{3,2,1,0:T(8,128)(2,1)S(1)} %pack.1), channel_id=1, replica_groups=mesh['wide'=8,'narrow'=4] {'wide'}, dimensions={0} | all-to-all | bytes 262144 | tf_op jit(solution)/shard_map/all_to_all | solution.py:274
  15.6 0.0 copy-done
  15.6 0.0 copy-done.2
  15.6 0.0 copy-done.3
  15.7 0.0 copy-done.5
  15.7 0.0 copy-done.6
  15.7 0.0 copy-start.1
  15.7 0.0 copy-start.4
  15.7 0.0 slice-start.1
  15.7 0.0 slice-start.3
  15.7 0.0 slice-start.4
  15.7 3.6 %attend.1 = bf16[32,16,128]{2,1,0:T(8,128)(2,1)S(1)} custom-call(s32[1]{0:T(128)} %bitcast.group_ref, s32[16]{0:T(128)S(1)} %copy-done.6, s32[2]{0:T(128)S(1)} %copy-done.5, bf16[8,2,16,256]{3,2,1,0:T(8,128)(2,1)S(1)} %all_to_all.15.query_ref, bf16[16,128,512]{2,1,0:T(8,128)(2,1)S(1)} %copy-done.2, bf16[2,576,2048]{2,1,0:T(8,128)(2,1)S(1)} %bitcast.8, ...), custom_call_target="tpu_custom_call" | custom-call | flops 15000000512 | tf_op jit(solution)/shard_map/attend/pallas_call | solution.py:276
  19.4 10.4 %all_to_all.16.heads_ref = bf16[32,16,128]{2,1,0:T(8,128)(2,1)S(1)} all-to-all(bf16[32,16,128]{2,1,0:T(8,128)(2,1)S(1)} %attend.1), channel_id=1, replica_groups=mesh['wide'=8,'narrow'=4] {'wide','narrow'}, dimensions={0} | all-to-all | bytes 262144 | tf_op jit(solution)/shard_map/all_to_all | solution.py:291
  29.8 0.0 copy-done.1
  29.8 0.0 copy-done.4
  29.8 0.0 copy-start.7
  29.8 0.0 slice-start.5
  29.8 1.2 %project.1 = bf16[16,1792]{1,0:T(8,128)(2,1)S(1)} custom-call(s32[16]{0:T(128)S(1)} %copy-done.6, s32[1]{0:T(128)} %bitcast.group_ref, bf16[32,16,128]{2,1,0:T(8,128)(2,1)S(1)} %all_to_all.16.heads_ref, bf16[2,1792]{1,0:T(2,128)(2,1)S(1)} %copy-done.4, bf16[1024,1792]{1,0:T(8,128)(2,1)S(1)} %copy-done.1), custom_call_target="tpu_custom_call" | custom-call | flops 12000000000 | tf_op jit(solution)/shard_map/project/pallas_call | solution.py:292
  31.1 0.7 %collective-permute-start = (bf16[16,1792]{1,0:T(8,128)(2,1)S(1)}, bf16[16,1792]{1,0:T(8,128)(2,1)S(1)}, u32[]{:S(2)}, u32[]{:S(2)}) collective-permute-start(bf16[16,1792]{1,0:T(8,128)(2,1)S(1)} %project.1), channel_id=1, source_target_pairs={{0,4},{4,0},{8,12},{12,8},{16,20},{20,16},{24,28},{28,24},{1,5},{5... | collective-permute-start | bytes 172040 | tf_op jit(solution)/shard_map/ppermute | solution.py:233
  31.8 3.5 %collective-permute-done = bf16[16,1792]{1,0:T(8,128)(2,1)S(1)} collective-permute-done((bf16[16,1792]{1,0:T(8,128)(2,1)S(1)}, bf16[16,1792]{1,0:T(8,128)(2,1)S(1)}, u32[]{:S(2)}, u32[]{:S(2)}) %collective-permute-start) | collective-permute-done | bytes 57376 | tf_op jit(solution)/shard_map/ppermute | solution.py:233
  35.3 0.7 %collective-permute-start.1 = (bf16[16,1792]{1,0:T(8,128)(2,1)S(1)}, bf16[16,1792]{1,0:T(8,128)(2,1)S(1)}, u32[]{:S(2)}, u32[]{:S(2)}) collective-permute-start(bf16[16,1792]{1,0:T(8,128)(2,1)S(1)} %add_convert_fusion.1), channel_id=1, source_target_pairs={{0,8},{4,12},{8,0},{12,4},{16,24},{20,28},{24,16},{28,20},{1,9},{5... | collective-permute-start | bytes 172040 | tf_op jit(solution)/shard_map/ppermute | solution.py:233
  36.0 3.5 %collective-permute-done.1 = bf16[16,1792]{1,0:T(8,128)(2,1)S(1)} collective-permute-done((bf16[16,1792]{1,0:T(8,128)(2,1)S(1)}, bf16[16,1792]{1,0:T(8,128)(2,1)S(1)}, u32[]{:S(2)}, u32[]{:S(2)}) %collective-permute-start.1) | collective-permute-done | bytes 57376 | tf_op jit(solution)/shard_map/ppermute | solution.py:233
  39.6 0.9 %collective-permute-start.2 = (bf16[16,1792]{1,0:T(8,128)(2,1)S(1)}, bf16[16,1792]{1,0:T(8,128)(2,1)S(1)}, u32[]{:S(2)}, u32[]{:S(2)}) collective-permute-start(bf16[16,1792]{1,0:T(8,128)(2,1)S(1)} %add_convert_fusion.first_ref), channel_id=1, source_target_pairs={{0,16},{4,20},{8,24},{12,28},{16,0},{20,4},{24,8},{28,12},{1,17},{... | collective-permute-start | bytes 172040 | tf_op jit(solution)/shard_map/ppermute | solution.py:233
  40.4 0.0 copy-done.7
  40.5 4.9 %collective-permute-done.2.second_ref = bf16[16,1792]{1,0:T(8,128)(2,1)S(1)} collective-permute-done((bf16[16,1792]{1,0:T(8,128)(2,1)S(1)}, bf16[16,1792]{1,0:T(8,128)(2,1)S(1)}, u32[]{:S(2)}, u32[]{:S(2)}) %collective-permute-start.2) | collective-permute-done | bytes 57376 | tf_op jit(solution)/shard_map/ppermute | solution.py:233
  45.3 0.0 slice-done
  45.4 0.0 slice-done.2
  45.4 0.0 slice-done.1
  45.4 0.0 slice-done.3
  45.4 2.2 %expand.1 = (f32[2,1792]{1,0:T(2,128)S(1)}, bf16[16,4864]{1,0:T(8,128)(2,1)S(1)}) custom-call(s32[1]{0:T(128)} %bitcast.group_ref, bf16[16,1792]{1,0:T(8,128)(2,1)S(1)} %add_convert_fusion.first_ref, bf16[16,1792]{1,0:T(8,128)(2,1)S(1)} %collective-permute-done.2.second_ref, bf16[1,1792]{1,0:T(2,128)(2,1)S(1)} %broadcast_in_dim.10.gain_ref, ...), custom_call_target="tpu_custom_call" | custom-call | flops 4000000000 | tf_op jit(solution)/shard_map/expand/pallas_call | solution.py:307
  47.6 0.0 collective-permute-start.3
  47.6 1.4 %collective-permute-done.3.second_ref = bf16[16,4864]{1,0:T(8,128)(2,1)S(1)} collective-permute-done((bf16[16,4864]{1,0:T(8,128)(2,1)S(1)}, bf16[16,4864]{1,0:T(8,128)(2,1)S(1)}, u32[]{:S(2)}, u32[]{:S(2)}) %collective-permute-start.3) | collective-permute-done | bytes 155680 | tf_op jit(solution)/shard_map/ppermute | solution.py:233
  49.0 0.1 merge.1.first_ref
  49.1 0.4 collective-permute-start.4
  49.5 5.8 %collective-permute-done.4.second_ref = bf16[16,4864]{1,0:T(8,128)(2,1)S(1)} collective-permute-done((bf16[16,4864]{1,0:T(8,128)(2,1)S(1)}, bf16[16,4864]{1,0:T(8,128)(2,1)S(1)}, u32[]{:S(2)}, u32[]{:S(2)}) %collective-permute-start.4) | collective-permute-done | bytes 155680 | tf_op jit(solution)/shard_map/ppermute | solution.py:233
  55.2 0.0 slice-done.4
  55.2 0.0 slice-done.5
  55.2 1.3 %contract.1 = f32[8,2,1792]{2,1,0:T(2,128)S(1)} custom-call(bf16[16,4864]{1,0:T(8,128)(2,1)S(1)} %merge.1.first_ref, bf16[16,4864]{1,0:T(8,128)(2,1)S(1)} %collective-permute-done.4.second_ref, bf16[2304,1792]{1,0:T(8,128)(2,1)S(1)} %bitcast.7), custom_call_target="tpu_custom_call" | custom-call | flops 4000000000 | tf_op jit(solution)/shard_map/contract/pallas_call | solution.py:323
  56.5 9.7 %all_to_all.17 = f32[8,2,1792]{2,1,0:T(2,128)S(1)} all-to-all(f32[8,2,1792]{2,1,0:T(2,128)S(1)} %contract.1), channel_id=1, replica_groups=mesh['wide'=8,'narrow'=4] {'wide'}, dimensions={0} | all-to-all | bytes 229376 | tf_op jit(solution)/shard_map/all_to_all | solution.py:330
  66.3 0.6 add_convert_fusion.2
  (7 shorter events, 0.1 us)
Async XLA Ops:
  0.0 15.6 %copy-start = (bf16[2,2048,576]{1,2,0:T(8,128)(2,1)S(1)}, bf16[2,2048,576]{1,2,0:T(8,128)(2,1)}, u32[]{:S(2)}) copy-start(bf16[2,2048,576]{1,2,0:T(8,128)(2,1)} %param.18) | copy-start | bytes 14155780
  0.0 15.6 %copy-start.2 = (bf16[16,128,512]{2,1,0:T(8,128)(2,1)S(1)}, bf16[16,128,512]{2,1,0:T(8,128)(2,1)}, u32[]{:S(2)}) copy-start(bf16[16,128,512]{2,1,0:T(8,128)(2,1)} %key_ref.1) | copy-start | bytes 6291460
  0.0 15.6 %copy-start.3 = (bf16[16,512,128]{2,1,0:T(8,128)(2,1)S(1)}, bf16[16,512,128]{2,1,0:T(8,128)(2,1)}, u32[]{:S(2)}) copy-start(bf16[16,512,128]{2,1,0:T(8,128)(2,1)} %value_ref.1) | copy-start | bytes 6291460
  0.0 15.6 %copy-start.5 = (s32[2]{0:T(128)S(1)}, s32[2]{0:T(128)}, u32[]{:S(2)}) copy-start(s32[2]{0:T(128)} %lengths_ref.1) | copy-start | bytes 28
  0.0 15.7 %copy-start.6 = (s32[16]{0:T(128)S(1)}, s32[16]{0:T(128)}, u32[]{:S(2)}) copy-start(s32[16]{0:T(128)} %rows_ref.3) | copy-start | bytes 196
  0.0 45.3 %slice-start = ((s8[8257536]{0:T(1024)(128)(4,1)}), s8[4194304]{0:T(1024)(128)(4,1)S(1)}, s32[]{:S(2)}) async-start(s8[8257536]{0:T(1024)(128)(4,1)} %bitcast.2), calls=%async_computation.3 | async-start | bytes 8388608
  0.0 45.3 %slice-start.2 = ((s8[8257536]{0:T(1024)(128)(4,1)}), s8[4194304]{0:T(1024)(128)(4,1)S(1)}, s32[]{:S(2)}) async-start(s8[8257536]{0:T(1024)(128)(4,1)} %bitcast.4), calls=%async_computation.5 | async-start | bytes 8388608
  15.7 14.1 %copy-start.1 = (bf16[1024,1792]{1,0:T(8,128)(2,1)S(1)}, bf16[1024,1792]{1,0:T(8,128)(2,1)}, u32[]{:S(2)}) copy-start(bf16[1024,1792]{1,0:T(8,128)(2,1)} %weight_ref.2) | copy-start | bytes 11010052
  15.7 14.1 %copy-start.4 = (bf16[2,1792]{1,0:T(2,128)(2,1)S(1)}, bf16[2,1792]{1,0:T(2,128)(2,1)}, u32[]{:S(2)}) copy-start(bf16[2,1792]{1,0:T(2,128)(2,1)} %residual_ref.1) | copy-start | bytes 21508
  15.7 29.7 %slice-start.1 = ((s8[8257536]{0:T(1024)(128)(4,1)}), s8[4063232]{0:T(1024)(128)(4,1)S(1)}, s32[]{:S(2)}) async-start(s8[8257536]{0:T(1024)(128)(4,1)} %bitcast.2), calls=%async_computation.4 | async-start | bytes 8126464
  15.7 29.7 %slice-start.3 = ((s8[8257536]{0:T(1024)(128)(4,1)}), s8[4063232]{0:T(1024)(128)(4,1)S(1)}, s32[]{:S(2)}) async-start(s8[8257536]{0:T(1024)(128)(4,1)} %bitcast.4), calls=%async_computation.6 | async-start | bytes 8126464
  15.7 39.5 %slice-start.4 = ((s8[8257536]{0:T(1024)(128)(4,1)}), s8[4194304]{0:T(1024)(128)(4,1)S(1)}, s32[]{:S(2)}) async-start(s8[8257536]{0:T(1024)(128)(4,1)} %bitcast.6), calls=%async_computation.7 | async-start | bytes 8388608
  29.8 10.6 %copy-start.7 = (bf16[1792]{0:T(1024)(128)(2,1)S(1)}, bf16[1792]{0:T(1024)(128)(2,1)}, u32[]{:S(2)}) copy-start(bf16[1792]{0:T(1024)(128)(2,1)} %param.22) | copy-start | bytes 10756
  29.8 25.4 %slice-start.5 = ((s8[8257536]{0:T(1024)(128)(4,1)}), s8[4063232]{0:T(1024)(128)(4,1)S(1)}, s32[]{:S(2)}) async-start(s8[8257536]{0:T(1024)(128)(4,1)} %bitcast.6), calls=%async_computation.8 | async-start | bytes 8126464
  31.1 4.2 %collective-permute-start = (bf16[16,1792]{1,0:T(8,128)(2,1)S(1)}, bf16[16,1792]{1,0:T(8,128)(2,1)S(1)}, u32[]{:S(2)}, u32[]{:S(2)}) collective-permute-start(bf16[16,1792]{1,0:T(8,128)(2,1)S(1)} %project.1), channel_id=1, source_target_pairs={{0,4},{4,0},{8,12},{12,8},{16,20},{20,16},{24,28},{28,24},{1,5},{5... | collective-permute-start | bytes 172040 | tf_op jit(solution)/shard_map/ppermute | solution.py:233
  35.3 4.2 %collective-permute-start.1 = (bf16[16,1792]{1,0:T(8,128)(2,1)S(1)}, bf16[16,1792]{1,0:T(8,128)(2,1)S(1)}, u32[]{:S(2)}, u32[]{:S(2)}) collective-permute-start(bf16[16,1792]{1,0:T(8,128)(2,1)S(1)} %add_convert_fusion.1), channel_id=1, source_target_pairs={{0,8},{4,12},{8,0},{12,4},{16,24},{20,28},{24,16},{28,20},{1,9},{5... | collective-permute-start | bytes 172040 | tf_op jit(solution)/shard_map/ppermute | solution.py:233
  39.6 5.8 %collective-permute-start.2 = (bf16[16,1792]{1,0:T(8,128)(2,1)S(1)}, bf16[16,1792]{1,0:T(8,128)(2,1)S(1)}, u32[]{:S(2)}, u32[]{:S(2)}) collective-permute-start(bf16[16,1792]{1,0:T(8,128)(2,1)S(1)} %add_convert_fusion.first_ref), channel_id=1, source_target_pairs={{0,16},{4,20},{8,24},{12,28},{16,0},{20,4},{24,8},{28,12},{1,17},{... | collective-permute-start | bytes 172040 | tf_op jit(solution)/shard_map/ppermute | solution.py:233
  47.6 1.4 %collective-permute-start.3 = (bf16[16,4864]{1,0:T(8,128)(2,1)S(1)}, bf16[16,4864]{1,0:T(8,128)(2,1)S(1)}, u32[]{:S(2)}, u32[]{:S(2)}) collective-permute-start(bf16[16,4864]{1,0:T(8,128)(2,1)S(1)} %get-tuple-element.8.first_ref), channel_id=1, source_target_pairs={{0,1},{1,0},{2,3},{3,2},{4,5},{5,4},{6,7},{7,6},{8,9},{9,8},{10,11... | collective-permute-start | bytes 466952 | tf_op jit(solution)/shard_map/ppermute | solution.py:233
  49.1 6.1 %collective-permute-start.4 = (bf16[16,4864]{1,0:T(8,128)(2,1)S(1)}, bf16[16,4864]{1,0:T(8,128)(2,1)S(1)}, u32[]{:S(2)}, u32[]{:S(2)}) collective-permute-start(bf16[16,4864]{1,0:T(8,128)(2,1)S(1)} %merge.1.first_ref), channel_id=1, source_target_pairs={{0,2},{1,3},{2,0},{3,1},{4,6},{5,7},{6,4},{7,5},{8,10},{9,11},{10,... | collective-permute-start | bytes 466952 | tf_op jit(solution)/shard_map/ppermute | solution.py:233

commit v5 on v4

--- a/solution.py
+++ b/solution.py
@@ -185,8 +185,8 @@
     return ref[:, start : start + 1].astype(F32) + ref[:, start + 128 : start + 129].astype(F32)
 
 
-def expand_kernel(
-    group_ref, first_ref, second_ref, gain_ref, gate_ref, up_ref, middle_ref, out_ref
+def gate_kernel(
+    group_ref, first_ref, second_ref, gain_ref, weight_ref, middle_ref, scaled_ref, out_ref
 ):
     middle = first_ref[...].astype(F32) + second_ref[...].astype(F32)
     slots = middle_ref.shape[0]
@@ -194,17 +194,24 @@
     for slot in range(slots):
         own = jnp.where(row == group_ref[0] * slots + slot, middle, 0.0)
         middle_ref[slot : slot + 1] = jnp.sum(own, axis=0, keepdims=True)
-    columns = gate_ref.shape[1]
-    padded = (out_ref.shape[1] - 256) // 2
     scaled = (middle * gain_ref[...].astype(F32)).astype(BF16)
-    out_ref[:, :columns] = jnp.dot(scaled, gate_ref[...], preferred_element_type=F32).astype(BF16)
-    out_ref[:, padded : padded + columns] = jnp.dot(
-        scaled, up_ref[...], preferred_element_type=F32
-    ).astype(BF16)
-    put_sums(out_ref, 2 * padded, jnp.sum(middle * middle, axis=1, keepdims=True))
+    scaled_ref[...] = scaled
+    columns = weight_ref.shape[1]
+    out_ref[:, :columns] = jnp.dot(scaled, weight_ref[...], preferred_element_type=F32).astype(BF16)
+    put_sums(out_ref, out_ref.shape[1] - 256, jnp.sum(middle * middle, axis=1, keepdims=True))
+
+
+def up_kernel(scaled_ref, weight_ref, out_ref):
+    out_ref[...] = jnp.dot(scaled_ref[...], weight_ref[...], preferred_element_type=F32).astype(
+        BF16
+    )
 
 
 def merge_kernel(first_ref, second_ref, out_ref):
+    out_ref[...] = (first_ref[...].astype(F32) + second_ref[...].astype(F32)).astype(BF16)
+
+
+def merge_sums_kernel(first_ref, second_ref, out_ref):
     end = out_ref.shape[1] - 256
     out_ref[:, :end] = (
         first_ref[:, :end].astype(F32) + second_ref[:, :end].astype(F32)
@@ -212,16 +219,16 @@
     put_sums(out_ref, end, get_sums(first_ref, end) + get_sums(second_ref, end))
 
 
-def contract_kernel(first_ref, second_ref, weight_ref, out_ref):
-    padded = (first_ref.shape[1] - 256) // 2
+def contract_kernel(
+    first_gate_ref, second_gate_ref, first_up_ref, second_up_ref, weight_ref, out_ref
+):
+    end = first_gate_ref.shape[1] - 256
     columns = weight_ref.shape[0]
-    square = get_sums(first_ref, 2 * padded) + get_sums(second_ref, 2 * padded)
+    square = get_sums(first_gate_ref, end) + get_sums(second_gate_ref, end)
     factor = lax.rsqrt(square / D + 1e-06)
-    gate = (first_ref[:, :columns].astype(F32) + second_ref[:, :columns].astype(F32)) * factor
-    up = (
-        first_ref[:, padded : padded + columns].astype(F32)
-        + second_ref[:, padded : padded + columns].astype(F32)
-    ) * factor
+    gate = first_gate_ref[:, :columns].astype(F32) + second_gate_ref[:, :columns].astype(F32)
+    gate = gate * factor
+    up = (first_up_ref[...].astype(F32) + second_up_ref[...].astype(F32)) * factor
     hidden = (gate / (1.0 + jnp.exp(-gate)) * up).astype(BF16)
     total = jnp.dot(hidden, weight_ref[...], preferred_element_type=F32)
     slots = out_ref.shape[1]
@@ -304,35 +311,37 @@
             summed = (summed.astype(F32) + other.astype(F32)).astype(BF16)
     columns = gate_weight.shape[1]
     padded = -(-columns // 128) * 128
-    middle, terms = call(
-        expand_kernel,
-        (
-            pltpu.VMEM((slots, features), F32),
-            pltpu.VMEM((rows, 2 * padded + 256), BF16),
-        ),
-        [SMEM] + [VMEM] * 5,
-        "expand",
-        flops=EXPAND,
-    )(group[None], summed, other, norm_gain[None, :], gate_weight, up_weight)
+    gate_shape = pltpu.VMEM((rows, padded + 256), BF16)
+    up_shape = pltpu.VMEM((rows, columns), BF16)
+    middle, scaled, gate = call(
+        gate_kernel,
+        (pltpu.VMEM((slots, features), F32), pltpu.VMEM((rows, features), BF16), gate_shape),
+        [SMEM] + [VMEM] * 4,
+        "gate",
+        flops=EXPAND // 2,
+    )(group[None], summed, other, norm_gain[None, :], gate_weight)
+    up = call(up_kernel, up_shape, [VMEM] * 2, "up", flops=EXPAND // 2)(scaled, up_weight)
     distance = 1
     while distance < narrow:
-        other = swap(terms, "narrow", distance, narrow)
+        other_gate = swap(gate, "narrow", distance, narrow)
+        other_up = swap(up, "narrow", distance, narrow)
         distance *= 2
         if distance < narrow:
-            terms = call(merge_kernel, terms_like(terms), [VMEM] * 2, "merge", flops=MERGE)(terms, other)
+            gate = call(
+                merge_sums_kernel, gate_shape, [VMEM] * 2, "merge_gate", flops=MERGE // 4
+            )(gate, other_gate)
+            up = call(merge_kernel, up_shape, [VMEM] * 2, "merge_up", flops=MERGE // 4)(
+                up, other_up
+            )
     down = call(
         contract_kernel,
         pltpu.VMEM((wide, slots, features), F32),
-        [VMEM] * 3,
+        [VMEM] * 5,
         "contract",
         flops=CONTRACT,
-    )(terms, other, down_weight)
+    )(gate, other_gate, up, other_up, down_weight)
     total = jnp.sum(lax.all_to_all(down, "wide", 0, 0, tiled=True), axis=0)
     return (middle + total).astype(BF16)
-
-
-def terms_like(array):
-    return pltpu.VMEM(array.shape, array.dtype)
 
 
 def solution(mesh):

time: 67.2 us -> 66.3 us (0.987)
  waiting for transfers between devices: 19.1 us -> 16.3 us
  starting transfers between devices: 2.67 us -> 4.4 us
    ppermute x5 -> x7, waiting for transfers between devices: 19.1 us -> 16.3 us  [swap(): return lax.ppermute(array, axis, [(i, i ^ distance) for i in range(size)])]
    ppermute x5 -> x7, starting transfers between devices: 2.67 us -> 4.4 us  [swap(): return lax.ppermute(array, axis, [(i, i ^ distance) for i in range(size)])]
    pallas_call x2 -> x4, Pallas kernels: 2.33 us -> 2.5 us  [the longest x1 1.2 us: shards(): call(gate_kernel, (pltpu.VMEM((slots, features), F32), pltpu.VMEM((rows,...]
  transfers between devices with their start and end apart: 5 -> 7, of which waited for: 5 -> 5; matrix products, arithmetic and copies ran while one was open for 0% -> 0% of each run, Pallas kernels for 0% -> 2%
where the time goes in v5:
time: 66.3 us; the launch traced here: 66.1 us
  blocking collectives  34.9 us (53%)
  waiting for transfers between devices  16.3 us (25%)
  Pallas kernels  9.53 us (14%)
  starting transfers between devices  4.4 us (7%)
  other arithmetic  0.68 us (1%)
    ppermute x7, waiting for transfers between devices, swap(): return lax.ppermute(array, axis, [(i, i ^ distance) for i in range(size)])  16.3 us
    all_to_all x1, blocking collectives, shards(): queries = lax.all_to_all(packed, 'wide', 0, 0, tiled=True)  14.7 us
    all_to_all x1, blocking collectives, shards(): received = lax.all_to_all(heads_out, ('wide', 'narrow'), 0, 0, tiled=True)  10.4 us
    all_to_all x1, blocking collectives, shards(): total = jnp.sum(lax.all_to_all(down, 'wide', 0, 0, tiled=True), axis=0)  9.75 us
    ppermute x7, starting transfers between devices, swap(): return lax.ppermute(array, axis, [(i, i ^ distance) for i in range(size)])  4.4 us
    pallas_call x1, Pallas kernels, shards(): call(functools.partial(attend_kernel, narrow, blocks, scale), pltpu.VMEM(...  3.64 us
  transfers between devices with their start and end apart: 7, of which 5 were waited for; matrix products, arithmetic and copies ran while one was open for 0% of the time, Pallas kernels for 2%

profile of v5, /device:TPU:0, one launch (start us, length us, event | category | flops | bytes accessed | tf_op | source)
XLA Modules:
  0.0 66.1 jit_solution(18381405314655653368)
XLA Ops:
  0.0 0.0 copy-start.2
  0.0 0.0 copy-start.3
  0.0 0.0 slice-start
  0.0 0.9 %pack.1 = bf16[8,2,16,256]{3,2,1,0:T(8,128)(2,1)S(1)} custom-call(s32[1]{0:T(128)} %bitcast.group_ref, bf16[2,16,128]{2,1,0:T(8,128)(2,1)} %nope_hbm.1, bf16[2,16,64]{2,1,0:T(8,128)(2,1)} %rope_hbm.1), custom_call_target="tpu_custom_call" | custom-call | flops 10000000000 | tf_op jit(solution)/shard_map/pack/pallas_call | solution.py:269
  0.9 14.7 %all_to_all.15.query_ref = bf16[8,2,16,256]{3,2,1,0:T(8,128)(2,1)S(1)} all-to-all(bf16[8,2,16,256]{3,2,1,0:T(8,128)(2,1)S(1)} %pack.1), channel_id=1, replica_groups=mesh['wide'=8,'narrow'=4] {'wide'}, dimensions={0} | all-to-all | bytes 262144 | tf_op jit(solution)/shard_map/all_to_all | solution.py:281
  15.6 0.0 copy-done
  15.6 0.0 copy-done.2
  15.6 0.0 copy-done.3
  15.6 0.0 copy-done.5
  15.6 0.0 copy-done.6
  15.7 0.0 copy-start.1
  15.7 0.0 copy-start.4
  15.7 0.0 slice-start.1
  15.7 3.6 %attend.1 = bf16[32,16,128]{2,1,0:T(8,128)(2,1)S(1)} custom-call(s32[1]{0:T(128)} %bitcast.group_ref, s32[16]{0:T(128)S(1)} %copy-done.6, s32[2]{0:T(128)S(1)} %copy-done.5, bf16[8,2,16,256]{3,2,1,0:T(8,128)(2,1)S(1)} %all_to_all.15.query_ref, bf16[16,128,512]{2,1,0:T(8,128)(2,1)S(1)} %copy-done.2, bf16[2,576,2048]{2,1,0:T(8,128)(2,1)S(1)} %bitcast.8, ...), custom_call_target="tpu_custom_call" | custom-call | flops 15000000512 | tf_op jit(solution)/shard_map/attend/pallas_call | solution.py:283
  19.3 0.0 slice-start.2
  19.4 10.4 %all_to_all.16.heads_ref = bf16[32,16,128]{2,1,0:T(8,128)(2,1)S(1)} all-to-all(bf16[32,16,128]{2,1,0:T(8,128)(2,1)S(1)} %attend.1), channel_id=1, replica_groups=mesh['wide'=8,'narrow'=4] {'wide','narrow'}, dimensions={0} | all-to-all | bytes 262144 | tf_op jit(solution)/shard_map/all_to_all | solution.py:298
  29.8 0.0 copy-done.1
  29.8 0.0 copy-done.4
  29.8 1.2 %project.1 = bf16[16,1792]{1,0:T(8,128)(2,1)S(1)} custom-call(s32[16]{0:T(128)S(1)} %copy-done.6, s32[1]{0:T(128)} %bitcast.group_ref, bf16[32,16,128]{2,1,0:T(8,128)(2,1)S(1)} %all_to_all.16.heads_ref, bf16[2,1792]{1,0:T(2,128)(2,1)S(1)} %copy-done.4, bf16[1024,1792]{1,0:T(8,128)(2,1)S(1)} %copy-done.1), custom_call_target="tpu_custom_call" | custom-call | flops 12000000000 | tf_op jit(solution)/shard_map/project/pallas_call | solution.py:299
  31.0 0.7 %collective-permute-start = (bf16[16,1792]{1,0:T(8,128)(2,1)S(1)}, bf16[16,1792]{1,0:T(8,128)(2,1)S(1)}, u32[]{:S(2)}, u32[]{:S(2)}) collective-permute-start(bf16[16,1792]{1,0:T(8,128)(2,1)S(1)} %project.1), channel_id=1, source_target_pairs={{0,4},{4,0},{8,12},{12,8},{16,20},{20,16},{24,28},{28,24},{1,5},{5... | collective-permute-start | bytes 172040 | tf_op jit(solution)/shard_map/ppermute | solution.py:240
  31.8 3.5 %collective-permute-done = bf16[16,1792]{1,0:T(8,128)(2,1)S(1)} collective-permute-done((bf16[16,1792]{1,0:T(8,128)(2,1)S(1)}, bf16[16,1792]{1,0:T(8,128)(2,1)S(1)}, u32[]{:S(2)}, u32[]{:S(2)}) %collective-permute-start) | collective-permute-done | bytes 57376 | tf_op jit(solution)/shard_map/ppermute | solution.py:240
  35.3 0.7 %collective-permute-start.1 = (bf16[16,1792]{1,0:T(8,128)(2,1)S(1)}, bf16[16,1792]{1,0:T(8,128)(2,1)S(1)}, u32[]{:S(2)}, u32[]{:S(2)}) collective-permute-start(bf16[16,1792]{1,0:T(8,128)(2,1)S(1)} %add_convert_fusion.1), channel_id=1, source_target_pairs={{0,8},{4,12},{8,0},{12,4},{16,24},{20,28},{24,16},{28,20},{1,9},{5... | collective-permute-start | bytes 172040 | tf_op jit(solution)/shard_map/ppermute | solution.py:240
  36.0 3.5 %collective-permute-done.1 = bf16[16,1792]{1,0:T(8,128)(2,1)S(1)} collective-permute-done((bf16[16,1792]{1,0:T(8,128)(2,1)S(1)}, bf16[16,1792]{1,0:T(8,128)(2,1)S(1)}, u32[]{:S(2)}, u32[]{:S(2)}) %collective-permute-start.1) | collective-permute-done | bytes 57376 | tf_op jit(solution)/shard_map/ppermute | solution.py:240
  39.6 0.9 %collective-permute-start.2 = (bf16[16,1792]{1,0:T(8,128)(2,1)S(1)}, bf16[16,1792]{1,0:T(8,128)(2,1)S(1)}, u32[]{:S(2)}, u32[]{:S(2)}) collective-permute-start(bf16[16,1792]{1,0:T(8,128)(2,1)S(1)} %add_convert_fusion.first_ref), channel_id=1, source_target_pairs={{0,16},{4,20},{8,24},{12,28},{16,0},{20,4},{24,8},{28,12},{1,17},{... | collective-permute-start | bytes 172040 | tf_op jit(solution)/shard_map/ppermute | solution.py:240
  40.4 0.0 copy-done.7
  40.4 4.9 %collective-permute-done.2.second_ref = bf16[16,1792]{1,0:T(8,128)(2,1)S(1)} collective-permute-done((bf16[16,1792]{1,0:T(8,128)(2,1)S(1)}, bf16[16,1792]{1,0:T(8,128)(2,1)S(1)}, u32[]{:S(2)}, u32[]{:S(2)}) %collective-permute-start.2) | collective-permute-done | bytes 57376 | tf_op jit(solution)/shard_map/ppermute | solution.py:240
  45.3 0.0 slice-done
  45.3 0.0 slice-done.1
  45.3 1.2 %gate.1 = (f32[2,1792]{1,0:T(2,128)S(1)}, bf16[16,1792]{1,0:T(8,128)(2,1)S(1)}, bf16[16,2560]{1,0:T(8,128)(2,1)S(1)}) custom-call(s32[1]{0:T(128)} %bitcast.group_ref, bf16[16,1792]{1,0:T(8,128)(2,1)S(1)} %add_convert_fusion.first_ref, bf16[16,1792]{1,0:T(8,128)(2,1)S(1)} %collective-permute-done.2.second_ref, ...), custom_call_target="tpu_custom_call" | custom-call | flops 2000000000 | tf_op jit(solution)/shard_map/gate/pallas_call | solution.py:316
  46.5 0.0 collective-permute-start.3
  46.5 0.0 slice-start.4
  46.6 0.0 slice-done.2
  46.6 0.0 slice-done.3
  46.6 0.0 slice-start.5
  46.6 1.2 %up.1.first_ref = bf16[16,2304]{1,0:T(8,128)(2,1)S(1)} custom-call(bf16[16,1792]{1,0:T(8,128)(2,1)S(1)} %get-tuple-element.10.scaled_ref, bf16[1792,2304]{1,0:T(8,128)(2,1)S(1)} %bitcast.5), custom_call_target="tpu_custom_call" | custom-call | flops 2000000000 | tf_op jit(solution)/shard_map/up/pallas_call | solution.py:323
  47.8 0.5 collective-permute-start.5
  48.3 0.0 collective-permute-done.3.second_ref
  48.3 0.1 merge_gate.1.first_gate_ref
  48.4 0.3 collective-permute-start.4
  48.7 0.5 collective-permute-done.5.second_ref
  49.2 1.3 %collective-permute-start.6 = (bf16[16,2304]{1,0:T(8,128)(2,1)S(1)}, bf16[16,2304]{1,0:T(8,128)(2,1)S(1)}, u32[]{:S(2)}, u32[]{:S(2)}) collective-permute-start(bf16[16,2304]{1,0:T(8,128)(2,1)S(1)} %merge_up.1.first_up_ref), channel_id=1, source_target_pairs={{0,2},{1,3},{2,0},{3,1},{4,6},{5,7},{6,4},{7,5},{8,10},{9,11},{10,... | collective-permute-start | bytes 221192 | tf_op jit(solution)/shard_map/ppermute | solution.py:240
  50.5 3.9 %collective-permute-done.6.second_up_ref = bf16[16,2304]{1,0:T(8,128)(2,1)S(1)} collective-permute-done((bf16[16,2304]{1,0:T(8,128)(2,1)S(1)}, bf16[16,2304]{1,0:T(8,128)(2,1)S(1)}, u32[]{:S(2)}, u32[]{:S(2)}) %collective-permute-start.6) | collective-permute-done | bytes 73760 | tf_op jit(solution)/shard_map/ppermute | solution.py:240
  54.4 0.0 collective-permute-done.4.second_gate_ref
  54.4 0.0 slice-done.4
  54.4 0.0 slice-done.5
  54.4 1.3 %contract.1 = f32[8,2,1792]{2,1,0:T(2,128)S(1)} custom-call(bf16[16,2560]{1,0:T(8,128)(2,1)S(1)} %merge_gate.1.first_gate_ref, bf16[16,2560]{1,0:T(8,128)(2,1)S(1)} %collective-permute-done.4.second_gate_ref, bf16[16,2304]{1,0:T(8,128)(2,1)S(1)} %merge_up.1.first_up_ref, bf16[16,2304]{1,0:T(8,128)(2,1)S(1)} %collective-permute-done.6.second_up_ref, ...), custom_call_target="tpu_custom_call" | custom-call | flops 4000000000 | tf_op jit(solution)/shard_map/contract/pallas_call | solution.py:336
  55.7 9.7 %all_to_all.17 = f32[8,2,1792]{2,1,0:T(2,128)S(1)} all-to-all(f32[8,2,1792]{2,1,0:T(2,128)S(1)} %contract.1), channel_id=1, replica_groups=mesh['wide'=8,'narrow'=4] {'wide'}, dimensions={0} | all-to-all | bytes 229376 | tf_op jit(solution)/shard_map/all_to_all | solution.py:343
  65.5 0.6 add_convert_fusion.2
  (13 shorter events, 0.1 us)
Async XLA Ops:
  0.0 15.6 %copy-start = (bf16[2,2048,576]{1,2,0:T(8,128)(2,1)S(1)}, bf16[2,2048,576]{1,2,0:T(8,128)(2,1)}, u32[]{:S(2)}) copy-start(bf16[2,2048,576]{1,2,0:T(8,128)(2,1)} %param.18) | copy-start | bytes 14155780
  0.0 15.6 %copy-start.2 = (bf16[16,128,512]{2,1,0:T(8,128)(2,1)S(1)}, bf16[16,128,512]{2,1,0:T(8,128)(2,1)}, u32[]{:S(2)}) copy-start(bf16[16,128,512]{2,1,0:T(8,128)(2,1)} %key_ref.1) | copy-start | bytes 6291460
  0.0 15.6 %copy-start.3 = (bf16[16,512,128]{2,1,0:T(8,128)(2,1)S(1)}, bf16[16,512,128]{2,1,0:T(8,128)(2,1)}, u32[]{:S(2)}) copy-start(bf16[16,512,128]{2,1,0:T(8,128)(2,1)} %value_ref.1) | copy-start | bytes 6291460
  0.0 15.6 %copy-start.5 = (s32[2]{0:T(128)S(1)}, s32[2]{0:T(128)}, u32[]{:S(2)}) copy-start(s32[2]{0:T(128)} %lengths_ref.1) | copy-start | bytes 28
  0.0 15.6 %copy-start.6 = (s32[16]{0:T(128)S(1)}, s32[16]{0:T(128)}, u32[]{:S(2)}) copy-start(s32[16]{0:T(128)} %rows_ref.3) | copy-start | bytes 196
  0.0 45.3 %slice-start = ((s8[8257536]{0:T(1024)(128)(4,1)}), s8[4194304]{0:T(1024)(128)(4,1)S(1)}, s32[]{:S(2)}) async-start(s8[8257536]{0:T(1024)(128)(4,1)} %bitcast.2), calls=%async_computation.3 | async-start | bytes 8388608
  15.7 14.1 %copy-start.1 = (bf16[1024,1792]{1,0:T(8,128)(2,1)S(1)}, bf16[1024,1792]{1,0:T(8,128)(2,1)}, u32[]{:S(2)}) copy-start(bf16[1024,1792]{1,0:T(8,128)(2,1)} %weight_ref.4) | copy-start | bytes 11010052
  15.7 14.1 %copy-start.4 = (bf16[2,1792]{1,0:T(2,128)(2,1)S(1)}, bf16[2,1792]{1,0:T(2,128)(2,1)}, u32[]{:S(2)}) copy-start(bf16[2,1792]{1,0:T(2,128)(2,1)} %residual_ref.1) | copy-start | bytes 21508
  15.7 29.6 %slice-start.1 = ((s8[8257536]{0:T(1024)(128)(4,1)}), s8[4063232]{0:T(1024)(128)(4,1)S(1)}, s32[]{:S(2)}) async-start(s8[8257536]{0:T(1024)(128)(4,1)} %bitcast.2), calls=%async_computation.4 | async-start | bytes 8126464
  19.3 27.2 %slice-start.2 = ((s8[8257536]{0:T(1024)(128)(4,1)}), s8[4194304]{0:T(1024)(128)(4,1)S(1)}, s32[]{:S(2)}) async-start(s8[8257536]{0:T(1024)(128)(4,1)} %bitcast.4), calls=%async_computation.5 | async-start | bytes 8388608
  29.8 10.6 %copy-start.7 = (bf16[1792]{0:T(1024)(128)(2,1)S(1)}, bf16[1792]{0:T(1024)(128)(2,1)}, u32[]{:S(2)}) copy-start(bf16[1792]{0:T(1024)(128)(2,1)} %param.22) | copy-start | bytes 10756
  29.8 16.8 %slice-start.3 = ((s8[8257536]{0:T(1024)(128)(4,1)}), s8[4063232]{0:T(1024)(128)(4,1)S(1)}, s32[]{:S(2)}) async-start(s8[8257536]{0:T(1024)(128)(4,1)} %bitcast.4), calls=%async_computation.6 | async-start | bytes 8126464
  31.0 4.2 %collective-permute-start = (bf16[16,1792]{1,0:T(8,128)(2,1)S(1)}, bf16[16,1792]{1,0:T(8,128)(2,1)S(1)}, u32[]{:S(2)}, u32[]{:S(2)}) collective-permute-start(bf16[16,1792]{1,0:T(8,128)(2,1)S(1)} %project.1), channel_id=1, source_target_pairs={{0,4},{4,0},{8,12},{12,8},{16,20},{20,16},{24,28},{28,24},{1,5},{5... | collective-permute-start | bytes 172040 | tf_op jit(solution)/shard_map/ppermute | solution.py:240
  35.3 4.2 %collective-permute-start.1 = (bf16[16,1792]{1,0:T(8,128)(2,1)S(1)}, bf16[16,1792]{1,0:T(8,128)(2,1)S(1)}, u32[]{:S(2)}, u32[]{:S(2)}) collective-permute-start(bf16[16,1792]{1,0:T(8,128)(2,1)S(1)} %add_convert_fusion.1), channel_id=1, source_target_pairs={{0,8},{4,12},{8,0},{12,4},{16,24},{20,28},{24,16},{28,20},{1,9},{5... | collective-permute-start | bytes 172040 | tf_op jit(solution)/shard_map/ppermute | solution.py:240
  39.6 5.8 %collective-permute-start.2 = (bf16[16,1792]{1,0:T(8,128)(2,1)S(1)}, bf16[16,1792]{1,0:T(8,128)(2,1)S(1)}, u32[]{:S(2)}, u32[]{:S(2)}) collective-permute-start(bf16[16,1792]{1,0:T(8,128)(2,1)S(1)} %add_convert_fusion.first_ref), channel_id=1, source_target_pairs={{0,16},{4,20},{8,24},{12,28},{16,0},{20,4},{24,8},{28,12},{1,17},{... | collective-permute-start | bytes 172040 | tf_op jit(solution)/shard_map/ppermute | solution.py:240
  46.5 1.7 %collective-permute-start.3 = (bf16[16,2560]{1,0:T(8,128)(2,1)S(1)}, bf16[16,2560]{1,0:T(8,128)(2,1)S(1)}, u32[]{:S(2)}, u32[]{:S(2)}) collective-permute-start(bf16[16,2560]{1,0:T(8,128)(2,1)S(1)} %get-tuple-element.9.first_ref), channel_id=1, source_target_pairs={{0,1},{1,0},{2,3},{3,2},{4,5},{5,4},{6,7},{7,6},{8,9},{9,8},{10,11... | collective-permute-start | bytes 245768 | tf_op jit(solution)/shard_map/ppermute | solution.py:240
  46.5 7.9 %slice-start.4 = ((s8[8257536]{0:T(1024)(128)(4,1)}), s8[4194304]{0:T(1024)(128)(4,1)S(1)}, s32[]{:S(2)}) async-start(s8[8257536]{0:T(1024)(128)(4,1)} %bitcast.6), calls=%async_computation.7 | async-start | bytes 8388608
  46.6 7.8 %slice-start.5 = ((s8[8257536]{0:T(1024)(128)(4,1)}), s8[4063232]{0:T(1024)(128)(4,1)S(1)}, s32[]{:S(2)}) async-start(s8[8257536]{0:T(1024)(128)(4,1)} %bitcast.6), calls=%async_computation.8 | async-start | bytes 8126464
  47.8 1.4 %collective-permute-start.5 = (bf16[16,2304]{1,0:T(8,128)(2,1)S(1)}, bf16[16,2304]{1,0:T(8,128)(2,1)S(1)}, u32[]{:S(2)}, u32[]{:S(2)}) collective-permute-start(bf16[16,2304]{1,0:T(8,128)(2,1)S(1)} %up.1.first_ref), channel_id=1, source_target_pairs={{0,1},{1,0},{2,3},{3,2},{4,5},{5,4},{6,7},{7,6},{8,9},{9,8},{10,11... | collective-permute-start | bytes 221192 | tf_op jit(solution)/shard_map/ppermute | solution.py:240
  48.4 6.0 %collective-permute-start.4 = (bf16[16,2560]{1,0:T(8,128)(2,1)S(1)}, bf16[16,2560]{1,0:T(8,128)(2,1)S(1)}, u32[]{:S(2)}, u32[]{:S(2)}) collective-permute-start(bf16[16,2560]{1,0:T(8,128)(2,1)S(1)} %merge_gate.1.first_gate_ref), channel_id=1, source_target_pairs={{0,2},{1,3},{2,0},{3,1},{4,6},{5,7},{6,4},{7,5},{8,10},{9,11},{10,... | collective-permute-start | bytes 245768 | tf_op jit(solution)/shard_map/ppermute | solution.py:240
  49.2 5.2 %collective-permute-start.6 = (bf16[16,2304]{1,0:T(8,128)(2,1)S(1)}, bf16[16,2304]{1,0:T(8,128)(2,1)S(1)}, u32[]{:S(2)}, u32[]{:S(2)}) collective-permute-start(bf16[16,2304]{1,0:T(8,128)(2,1)S(1)} %merge_up.1.first_up_ref), channel_id=1, source_target_pairs={{0,2},{1,3},{2,0},{3,1},{4,6},{5,7},{6,4},{7,5},{8,10},{9,11},{10,... | collective-permute-start | bytes 221192 | tf_op jit(solution)/shard_map/ppermute | solution.py:240

commit v6 on v5

--- a/solution.py
+++ b/solution.py
@@ -53,11 +53,11 @@
     ]
     for copy in copies:
         copy.start()
-    head_size, width = nope_ref.shape[2], rope_ref.shape[2]
-    empty = jnp.zeros(rope_ref.shape[:2] + (out_ref.shape[3] - head_size - width,), BF16)
+    heads = nope_ref.shape[1]
     for copy in copies:
         copy.wait()
-    row = jnp.concatenate([nope_ref[...], rope_ref[...], empty], axis=2)
+    pairs = jnp.concatenate([rope_ref[:, : heads // 2], rope_ref[:, heads // 2 :]], axis=2)
+    row = jnp.concatenate([nope_ref[...], pairs], axis=1)
     for target in range(out_ref.shape[0]):
         out_ref[target] = row
 
@@ -84,42 +84,46 @@
     for slot in range(slots):
         row = rows_ref[group * slots + slot]
         queries.append(query_ref[row // slots, row % slots])
-    query = jnp.concatenate(queries, axis=0)
+    nope = jnp.concatenate([query[:heads] for query in queries], axis=0)
+    ropes = [
+        jnp.concatenate([query[heads:, :rope], query[heads:, rope:]], axis=0) for query in queries
+    ]
     own_head = lax.broadcasted_iota(jnp.int32, (slots * heads, 1), 0) % heads
-    nope = query[:, :head_size]
-    zero = jnp.zeros((), BF16)
-    spread = jnp.concatenate(
-        [jnp.where(own_head == head, nope, zero) for head in range(heads)], axis=1
-    )
-    query_latent = jnp.dot(
-        spread, key_ref[...].reshape(heads * head_size, latent), preferred_element_type=F32
-    ).astype(BF16)
-    contexts = []
-    for slot in range(slots):
-        part = slice(slot * heads, (slot + 1) * heads)
-        scores = jnp.dot(
-            query_latent[part], cache_ref[slot, :latent, :], preferred_element_type=F32
-        ) + jnp.dot(
-            query[part, head_size : head_size + rope],
+    total = jnp.zeros((slots * heads, latent), F32)
+    for head in range(heads):
+        term = jnp.dot(nope, key_ref[head], preferred_element_type=F32)
+        total = jnp.where(own_head == head, term, total)
+    query_latent = total.astype(BF16)
+    parts = [slice(slot * heads, (slot + 1) * heads) for slot in range(slots)]
+    scores = [
+        jnp.dot(query_latent[part], cache_ref[slot, :latent, :], preferred_element_type=F32)
+        + jnp.dot(
+            ropes[slot],
             cache_ref[slot, latent:, :],
             preferred_element_type=F32,
         )
+        for slot, part in enumerate(parts)
+    ]
+    probs = []
+    for slot in range(slots):
         live = lax.broadcasted_iota(jnp.int32, (1, span), 1) < lengths_ref[slot]
-        scores = jnp.where(live, scores * scale, -jnp.inf)
-        weights = jnp.exp(scores - jnp.max(scores, axis=1, keepdims=True))
-        probs = (weights / jnp.sum(weights, axis=1, keepdims=True)).astype(BF16)
-        contexts.append(
+        masked = jnp.where(live, scores[slot] * scale, -jnp.inf)
+        weights = jnp.exp(masked - jnp.max(masked, axis=1, keepdims=True))
+        probs.append((weights / jnp.sum(weights, axis=1, keepdims=True)).astype(BF16))
+    context = jnp.concatenate(
+        [
             lax.dot_general(
-                probs, cache_ref[slot, :latent, :], NT, preferred_element_type=F32
+                probs[slot], cache_ref[slot, :latent, :], NT, preferred_element_type=F32
             ).astype(BF16)
-        )
-    context = jnp.concatenate(contexts, axis=0)
-    spread = jnp.concatenate(
-        [jnp.where(own_head == head, context, zero) for head in range(heads)], axis=1
-    )
-    heads_out = jnp.dot(
-        spread, value_ref[...].reshape(heads * latent, head_size), preferred_element_type=F32
-    ).astype(BF16)
+            for slot in range(slots)
+        ],
+        axis=0,
+    )
+    total = jnp.zeros((slots * heads, head_size), F32)
+    for head in range(heads):
+        term = jnp.dot(context, value_ref[head], preferred_element_type=F32)
+        total = jnp.where(own_head == head, term, total)
+    heads_out = total.astype(BF16)
     per_block = heads // blocks
     pieces = []
     for block in range(blocks):
@@ -268,7 +272,7 @@
 
     packed = call(
         pack_kernel,
-        pltpu.VMEM((wide, slots, heads, head_size + 128), BF16),
+        pltpu.VMEM((wide, slots, heads + heads // 2, head_size), BF16),
         [SMEM, HBM, HBM],
         "pack",
         [

time: 66.3 us -> 65.5 us (0.988)
  no operation moved by 1% of the time
where the time goes in v6:
time: 65.5 us; the launch traced here: 65.3 us
  blocking collectives  34.5 us (53%)
  waiting for transfers between devices  16.3 us (25%)
  Pallas kernels  9.07 us (14%)
  starting transfers between devices  4.4 us (7%)
  other arithmetic  0.68 us (1%)
    ppermute x7, waiting for transfers between devices, swap(): return lax.ppermute(array, axis, [(i, i ^ distance) for i in range(size)])  16.3 us
    all_to_all x1, blocking collectives, shards(): queries = lax.all_to_all(packed, 'wide', 0, 0, tiled=True)  14.5 us
    all_to_all x1, blocking collectives, shards(): received = lax.all_to_all(heads_out, ('wide', 'narrow'), 0, 0, tiled=True)  10.3 us
    all_to_all x1, blocking collectives, shards(): total = jnp.sum(lax.all_to_all(down, 'wide', 0, 0, tiled=True), axis=0)  9.75 us
    ppermute x7, starting transfers between devices, swap(): return lax.ppermute(array, axis, [(i, i ^ distance) for i in range(size)])  4.4 us
    pallas_call x1, Pallas kernels, shards(): call(functools.partial(attend_kernel, narrow, blocks, scale), pltpu.VMEM(...  3.11 us
  transfers between devices with their start and end apart: 7, of which 5 were waited for; matrix products, arithmetic and copies ran while one was open for 0% of the time, Pallas kernels for 2%

profile of v6, /device:TPU:0, one launch (start us, length us, event | category | flops | bytes accessed | tf_op | source)
XLA Modules:
  0.0 65.3 jit_solution(7646936177353489840)
XLA Ops:
  0.0 0.0 copy-start.2
  0.0 0.0 copy-start.3
  0.0 0.0 slice-start
  0.0 1.0 %pack.1 = bf16[8,2,24,128]{3,2,1,0:T(8,128)(2,1)S(1)} custom-call(s32[1]{0:T(128)} %bitcast.group_ref, bf16[2,16,128]{2,1,0:T(8,128)(2,1)} %nope_hbm.1, bf16[2,16,64]{2,1,0:T(8,128)(2,1)} %rope_hbm.1), custom_call_target="tpu_custom_call" | custom-call | flops 10000000000 | tf_op jit(solution)/shard_map/pack/pallas_call | solution.py:273
  1.0 14.5 %all_to_all.15.query_ref = bf16[8,2,24,128]{3,2,1,0:T(8,128)(2,1)S(1)} all-to-all(bf16[8,2,24,128]{3,2,1,0:T(8,128)(2,1)S(1)} %pack.1), channel_id=1, replica_groups=mesh['wide'=8,'narrow'=4] {'wide'}, dimensions={0} | all-to-all | bytes 196608 | tf_op jit(solution)/shard_map/all_to_all | solution.py:285
  15.5 0.0 copy-done
  15.5 0.0 copy-done.2
  15.5 0.0 copy-done.3
  15.5 0.0 copy-done.5
  15.5 0.0 copy-done.6
  15.5 0.0 copy-start.1
  15.5 0.0 copy-start.4
  15.5 0.0 slice-start.1
  15.5 3.1 %attend.1 = bf16[32,16,128]{2,1,0:T(8,128)(2,1)S(1)} custom-call(s32[1]{0:T(128)} %bitcast.group_ref, s32[16]{0:T(128)S(1)} %copy-done.6, s32[2]{0:T(128)S(1)} %copy-done.5, bf16[8,2,24,128]{3,2,1,0:T(8,128)(2,1)S(1)} %all_to_all.15.query_ref, bf16[16,128,512]{2,1,0:T(8,128)(2,1)S(1)} %copy-done.2, bf16[2,576,2048]{2,1,0:T(8,128)(2,1)S(1)} %bitcast.8, ...), custom_call_target="tpu_custom_call" | custom-call | flops 15000000512 | tf_op jit(solution)/shard_map/attend/pallas_call | solution.py:287
  18.7 0.0 slice-start.2
  18.7 10.3 %all_to_all.16.heads_ref = bf16[32,16,128]{2,1,0:T(8,128)(2,1)S(1)} all-to-all(bf16[32,16,128]{2,1,0:T(8,128)(2,1)S(1)} %attend.1), channel_id=1, replica_groups=mesh['wide'=8,'narrow'=4] {'wide','narrow'}, dimensions={0} | all-to-all | bytes 262144 | tf_op jit(solution)/shard_map/all_to_all | solution.py:302
  29.0 0.0 copy-done.1
  29.0 0.0 copy-done.4
  29.0 1.2 %project.1 = bf16[16,1792]{1,0:T(8,128)(2,1)S(1)} custom-call(s32[16]{0:T(128)S(1)} %copy-done.6, s32[1]{0:T(128)} %bitcast.group_ref, bf16[32,16,128]{2,1,0:T(8,128)(2,1)S(1)} %all_to_all.16.heads_ref, bf16[2,1792]{1,0:T(2,128)(2,1)S(1)} %copy-done.4, bf16[1024,1792]{1,0:T(8,128)(2,1)S(1)} %copy-done.1), custom_call_target="tpu_custom_call" | custom-call | flops 12000000000 | tf_op jit(solution)/shard_map/project/pallas_call | solution.py:303
  30.2 0.7 %collective-permute-start = (bf16[16,1792]{1,0:T(8,128)(2,1)S(1)}, bf16[16,1792]{1,0:T(8,128)(2,1)S(1)}, u32[]{:S(2)}, u32[]{:S(2)}) collective-permute-start(bf16[16,1792]{1,0:T(8,128)(2,1)S(1)} %project.1), channel_id=1, source_target_pairs={{0,4},{4,0},{8,12},{12,8},{16,20},{20,16},{24,28},{28,24},{1,5},{5... | collective-permute-start | bytes 172040 | tf_op jit(solution)/shard_map/ppermute | solution.py:244
  30.9 3.5 %collective-permute-done = bf16[16,1792]{1,0:T(8,128)(2,1)S(1)} collective-permute-done((bf16[16,1792]{1,0:T(8,128)(2,1)S(1)}, bf16[16,1792]{1,0:T(8,128)(2,1)S(1)}, u32[]{:S(2)}, u32[]{:S(2)}) %collective-permute-start) | collective-permute-done | bytes 57376 | tf_op jit(solution)/shard_map/ppermute | solution.py:244
  34.5 0.7 %collective-permute-start.1 = (bf16[16,1792]{1,0:T(8,128)(2,1)S(1)}, bf16[16,1792]{1,0:T(8,128)(2,1)S(1)}, u32[]{:S(2)}, u32[]{:S(2)}) collective-permute-start(bf16[16,1792]{1,0:T(8,128)(2,1)S(1)} %add_convert_fusion.1), channel_id=1, source_target_pairs={{0,8},{4,12},{8,0},{12,4},{16,24},{20,28},{24,16},{28,20},{1,9},{5... | collective-permute-start | bytes 172040 | tf_op jit(solution)/shard_map/ppermute | solution.py:244
  35.2 3.5 %collective-permute-done.1 = bf16[16,1792]{1,0:T(8,128)(2,1)S(1)} collective-permute-done((bf16[16,1792]{1,0:T(8,128)(2,1)S(1)}, bf16[16,1792]{1,0:T(8,128)(2,1)S(1)}, u32[]{:S(2)}, u32[]{:S(2)}) %collective-permute-start.1) | collective-permute-done | bytes 57376 | tf_op jit(solution)/shard_map/ppermute | solution.py:244
  38.7 0.9 %collective-permute-start.2 = (bf16[16,1792]{1,0:T(8,128)(2,1)S(1)}, bf16[16,1792]{1,0:T(8,128)(2,1)S(1)}, u32[]{:S(2)}, u32[]{:S(2)}) collective-permute-start(bf16[16,1792]{1,0:T(8,128)(2,1)S(1)} %add_convert_fusion.first_ref), channel_id=1, source_target_pairs={{0,16},{4,20},{8,24},{12,28},{16,0},{20,4},{24,8},{28,12},{1,17},{... | collective-permute-start | bytes 172040 | tf_op jit(solution)/shard_map/ppermute | solution.py:244
  39.6 0.0 copy-done.7
  39.6 4.9 %collective-permute-done.2.second_ref = bf16[16,1792]{1,0:T(8,128)(2,1)S(1)} collective-permute-done((bf16[16,1792]{1,0:T(8,128)(2,1)S(1)}, bf16[16,1792]{1,0:T(8,128)(2,1)S(1)}, u32[]{:S(2)}, u32[]{:S(2)}) %collective-permute-start.2) | collective-permute-done | bytes 57376 | tf_op jit(solution)/shard_map/ppermute | solution.py:244
  44.5 0.0 slice-done
  44.5 0.0 slice-done.1
  44.5 1.2 %gate.1 = (f32[2,1792]{1,0:T(2,128)S(1)}, bf16[16,1792]{1,0:T(8,128)(2,1)S(1)}, bf16[16,2560]{1,0:T(8,128)(2,1)S(1)}) custom-call(s32[1]{0:T(128)} %bitcast.group_ref, bf16[16,1792]{1,0:T(8,128)(2,1)S(1)} %add_convert_fusion.first_ref, bf16[16,1792]{1,0:T(8,128)(2,1)S(1)} %collective-permute-done.2.second_ref, ...), custom_call_target="tpu_custom_call" | custom-call | flops 2000000000 | tf_op jit(solution)/shard_map/gate/pallas_call | solution.py:320
  45.7 0.0 collective-permute-start.3
  45.7 0.0 slice-start.4
  45.7 0.0 slice-done.2
  45.8 0.0 slice-done.3
  45.8 0.0 slice-start.5
  45.8 1.2 %up.1.first_ref = bf16[16,2304]{1,0:T(8,128)(2,1)S(1)} custom-call(bf16[16,1792]{1,0:T(8,128)(2,1)S(1)} %get-tuple-element.10.scaled_ref, bf16[1792,2304]{1,0:T(8,128)(2,1)S(1)} %bitcast.5), custom_call_target="tpu_custom_call" | custom-call | flops 2000000000 | tf_op jit(solution)/shard_map/up/pallas_call | solution.py:327
  47.0 0.5 collective-permute-start.5
  47.5 0.0 collective-permute-done.3.second_ref
  47.5 0.1 merge_gate.1.first_gate_ref
  47.5 0.3 collective-permute-start.4
  47.9 0.5 collective-permute-done.5.second_ref
  48.4 1.3 %collective-permute-start.6 = (bf16[16,2304]{1,0:T(8,128)(2,1)S(1)}, bf16[16,2304]{1,0:T(8,128)(2,1)S(1)}, u32[]{:S(2)}, u32[]{:S(2)}) collective-permute-start(bf16[16,2304]{1,0:T(8,128)(2,1)S(1)} %merge_up.1.first_up_ref), channel_id=1, source_target_pairs={{0,2},{1,3},{2,0},{3,1},{4,6},{5,7},{6,4},{7,5},{8,10},{9,11},{10,... | collective-permute-start | bytes 221192 | tf_op jit(solution)/shard_map/ppermute | solution.py:244
  49.7 3.9 %collective-permute-done.6.second_up_ref = bf16[16,2304]{1,0:T(8,128)(2,1)S(1)} collective-permute-done((bf16[16,2304]{1,0:T(8,128)(2,1)S(1)}, bf16[16,2304]{1,0:T(8,128)(2,1)S(1)}, u32[]{:S(2)}, u32[]{:S(2)}) %collective-permute-start.6) | collective-permute-done | bytes 73760 | tf_op jit(solution)/shard_map/ppermute | solution.py:244
  53.6 0.0 collective-permute-done.4.second_gate_ref
  53.6 0.0 slice-done.4
  53.6 0.0 slice-done.5
  53.6 1.3 %contract.1 = f32[8,2,1792]{2,1,0:T(2,128)S(1)} custom-call(bf16[16,2560]{1,0:T(8,128)(2,1)S(1)} %merge_gate.1.first_gate_ref, bf16[16,2560]{1,0:T(8,128)(2,1)S(1)} %collective-permute-done.4.second_gate_ref, bf16[16,2304]{1,0:T(8,128)(2,1)S(1)} %merge_up.1.first_up_ref, bf16[16,2304]{1,0:T(8,128)(2,1)S(1)} %collective-permute-done.6.second_up_ref, ...), custom_call_target="tpu_custom_call" | custom-call | flops 4000000000 | tf_op jit(solution)/shard_map/contract/pallas_call | solution.py:340
  54.9 9.7 %all_to_all.17 = f32[8,2,1792]{2,1,0:T(2,128)S(1)} all-to-all(f32[8,2,1792]{2,1,0:T(2,128)S(1)} %contract.1), channel_id=1, replica_groups=mesh['wide'=8,'narrow'=4] {'wide'}, dimensions={0} | all-to-all | bytes 229376 | tf_op jit(solution)/shard_map/all_to_all | solution.py:347
  64.6 0.6 add_convert_fusion.2
  (13 shorter events, 0.1 us)
Async XLA Ops:
  0.0 15.5 %copy-start = (bf16[2,2048,576]{1,2,0:T(8,128)(2,1)S(1)}, bf16[2,2048,576]{1,2,0:T(8,128)(2,1)}, u32[]{:S(2)}) copy-start(bf16[2,2048,576]{1,2,0:T(8,128)(2,1)} %param.18) | copy-start | bytes 14155780
  0.0 15.5 %copy-start.2 = (bf16[16,128,512]{2,1,0:T(8,128)(2,1)S(1)}, bf16[16,128,512]{2,1,0:T(8,128)(2,1)}, u32[]{:S(2)}) copy-start(bf16[16,128,512]{2,1,0:T(8,128)(2,1)} %key_ref.1) | copy-start | bytes 6291460
  0.0 15.5 %copy-start.3 = (bf16[16,512,128]{2,1,0:T(8,128)(2,1)S(1)}, bf16[16,512,128]{2,1,0:T(8,128)(2,1)}, u32[]{:S(2)}) copy-start(bf16[16,512,128]{2,1,0:T(8,128)(2,1)} %value_ref.1) | copy-start | bytes 6291460
  0.0 15.5 %copy-start.5 = (s32[2]{0:T(128)S(1)}, s32[2]{0:T(128)}, u32[]{:S(2)}) copy-start(s32[2]{0:T(128)} %lengths_ref.1) | copy-start | bytes 28
  0.0 15.5 %copy-start.6 = (s32[16]{0:T(128)S(1)}, s32[16]{0:T(128)}, u32[]{:S(2)}) copy-start(s32[16]{0:T(128)} %rows_ref.3) | copy-start | bytes 196
  0.0 44.5 %slice-start = ((s8[8257536]{0:T(1024)(128)(4,1)}), s8[4194304]{0:T(1024)(128)(4,1)S(1)}, s32[]{:S(2)}) async-start(s8[8257536]{0:T(1024)(128)(4,1)} %bitcast.2), calls=%async_computation.3 | async-start | bytes 8388608
  15.5 13.5 %copy-start.1 = (bf16[1024,1792]{1,0:T(8,128)(2,1)S(1)}, bf16[1024,1792]{1,0:T(8,128)(2,1)}, u32[]{:S(2)}) copy-start(bf16[1024,1792]{1,0:T(8,128)(2,1)} %weight_ref.4) | copy-start | bytes 11010052
  15.5 13.4 %copy-start.4 = (bf16[2,1792]{1,0:T(2,128)(2,1)S(1)}, bf16[2,1792]{1,0:T(2,128)(2,1)}, u32[]{:S(2)}) copy-start(bf16[2,1792]{1,0:T(2,128)(2,1)} %residual_ref.1) | copy-start | bytes 21508
  15.5 29.0 %slice-start.1 = ((s8[8257536]{0:T(1024)(128)(4,1)}), s8[4063232]{0:T(1024)(128)(4,1)S(1)}, s32[]{:S(2)}) async-start(s8[8257536]{0:T(1024)(128)(4,1)} %bitcast.2), calls=%async_computation.4 | async-start | bytes 8126464
  18.7 27.1 %slice-start.2 = ((s8[8257536]{0:T(1024)(128)(4,1)}), s8[4194304]{0:T(1024)(128)(4,1)S(1)}, s32[]{:S(2)}) async-start(s8[8257536]{0:T(1024)(128)(4,1)} %bitcast.4), calls=%async_computation.5 | async-start | bytes 8388608
  29.0 10.6 %copy-start.7 = (bf16[1792]{0:T(1024)(128)(2,1)S(1)}, bf16[1792]{0:T(1024)(128)(2,1)}, u32[]{:S(2)}) copy-start(bf16[1792]{0:T(1024)(128)(2,1)} %param.22) | copy-start | bytes 10756
  29.0 16.8 %slice-start.3 = ((s8[8257536]{0:T(1024)(128)(4,1)}), s8[4063232]{0:T(1024)(128)(4,1)S(1)}, s32[]{:S(2)}) async-start(s8[8257536]{0:T(1024)(128)(4,1)} %bitcast.4), calls=%async_computation.6 | async-start | bytes 8126464
  30.2 4.2 %collective-permute-start = (bf16[16,1792]{1,0:T(8,128)(2,1)S(1)}, bf16[16,1792]{1,0:T(8,128)(2,1)S(1)}, u32[]{:S(2)}, u32[]{:S(2)}) collective-permute-start(bf16[16,1792]{1,0:T(8,128)(2,1)S(1)} %project.1), channel_id=1, source_target_pairs={{0,4},{4,0},{8,12},{12,8},{16,20},{20,16},{24,28},{28,24},{1,5},{5... | collective-permute-start | bytes 172040 | tf_op jit(solution)/shard_map/ppermute | solution.py:244
  34.5 4.2 %collective-permute-start.1 = (bf16[16,1792]{1,0:T(8,128)(2,1)S(1)}, bf16[16,1792]{1,0:T(8,128)(2,1)S(1)}, u32[]{:S(2)}, u32[]{:S(2)}) collective-permute-start(bf16[16,1792]{1,0:T(8,128)(2,1)S(1)} %add_convert_fusion.1), channel_id=1, source_target_pairs={{0,8},{4,12},{8,0},{12,4},{16,24},{20,28},{24,16},{28,20},{1,9},{5... | collective-permute-start | bytes 172040 | tf_op jit(solution)/shard_map/ppermute | solution.py:244
  38.7 5.8 %collective-permute-start.2 = (bf16[16,1792]{1,0:T(8,128)(2,1)S(1)}, bf16[16,1792]{1,0:T(8,128)(2,1)S(1)}, u32[]{:S(2)}, u32[]{:S(2)}) collective-permute-start(bf16[16,1792]{1,0:T(8,128)(2,1)S(1)} %add_convert_fusion.first_ref), channel_id=1, source_target_pairs={{0,16},{4,20},{8,24},{12,28},{16,0},{20,4},{24,8},{28,12},{1,17},{... | collective-permute-start | bytes 172040 | tf_op jit(solution)/shard_map/ppermute | solution.py:244
  45.7 1.7 %collective-permute-start.3 = (bf16[16,2560]{1,0:T(8,128)(2,1)S(1)}, bf16[16,2560]{1,0:T(8,128)(2,1)S(1)}, u32[]{:S(2)}, u32[]{:S(2)}) collective-permute-start(bf16[16,2560]{1,0:T(8,128)(2,1)S(1)} %get-tuple-element.9.first_ref), channel_id=1, source_target_pairs={{0,1},{1,0},{2,3},{3,2},{4,5},{5,4},{6,7},{7,6},{8,9},{9,8},{10,11... | collective-permute-start | bytes 245768 | tf_op jit(solution)/shard_map/ppermute | solution.py:244
  45.7 7.9 %slice-start.4 = ((s8[8257536]{0:T(1024)(128)(4,1)}), s8[4194304]{0:T(1024)(128)(4,1)S(1)}, s32[]{:S(2)}) async-start(s8[8257536]{0:T(1024)(128)(4,1)} %bitcast.6), calls=%async_computation.7 | async-start | bytes 8388608
  45.8 7.8 %slice-start.5 = ((s8[8257536]{0:T(1024)(128)(4,1)}), s8[4063232]{0:T(1024)(128)(4,1)S(1)}, s32[]{:S(2)}) async-start(s8[8257536]{0:T(1024)(128)(4,1)} %bitcast.6), calls=%async_computation.8 | async-start | bytes 8126464
  47.0 1.4 %collective-permute-start.5 = (bf16[16,2304]{1,0:T(8,128)(2,1)S(1)}, bf16[16,2304]{1,0:T(8,128)(2,1)S(1)}, u32[]{:S(2)}, u32[]{:S(2)}) collective-permute-start(bf16[16,2304]{1,0:T(8,128)(2,1)S(1)} %up.1.first_ref), channel_id=1, source_target_pairs={{0,1},{1,0},{2,3},{3,2},{4,5},{5,4},{6,7},{7,6},{8,9},{9,8},{10,11... | collective-permute-start | bytes 221192 | tf_op jit(solution)/shard_map/ppermute | solution.py:244
  47.5 6.0 %collective-permute-start.4 = (bf16[16,2560]{1,0:T(8,128)(2,1)S(1)}, bf16[16,2560]{1,0:T(8,128)(2,1)S(1)}, u32[]{:S(2)}, u32[]{:S(2)}) collective-permute-start(bf16[16,2560]{1,0:T(8,128)(2,1)S(1)} %merge_gate.1.first_gate_ref), channel_id=1, source_target_pairs={{0,2},{1,3},{2,0},{3,1},{4,6},{5,7},{6,4},{7,5},{8,10},{9,11},{10,... | collective-permute-start | bytes 245768 | tf_op jit(solution)/shard_map/ppermute | solution.py:244
  48.4 5.2 %collective-permute-start.6 = (bf16[16,2304]{1,0:T(8,128)(2,1)S(1)}, bf16[16,2304]{1,0:T(8,128)(2,1)S(1)}, u32[]{:S(2)}, u32[]{:S(2)}) collective-permute-start(bf16[16,2304]{1,0:T(8,128)(2,1)S(1)} %merge_up.1.first_up_ref), channel_id=1, source_target_pairs={{0,2},{1,3},{2,0},{3,1},{4,6},{5,7},{6,4},{7,5},{8,10},{9,11},{10,... | collective-permute-start | bytes 221192 | tf_op jit(solution)/shard_map/ppermute | solution.py:244

commit v7 on v6

--- a/solution.py
+++ b/solution.py
@@ -189,10 +189,11 @@
     return ref[:, start : start + 1].astype(F32) + ref[:, start + 128 : start + 129].astype(F32)
 
 
-def gate_kernel(
-    group_ref, first_ref, second_ref, gain_ref, weight_ref, middle_ref, scaled_ref, out_ref
-):
-    middle = first_ref[...].astype(F32) + second_ref[...].astype(F32)
+def gate_kernel(group_ref, gain_ref, weight_ref, *refs):
+    parts, (middle_ref, scaled_ref, out_ref) = refs[:-3], refs[-3:]
+    middle = parts[0][...].astype(F32)
+    for part in parts[1:]:
+        middle = middle + part[...].astype(F32)
     slots = middle_ref.shape[0]
     row = lax.broadcasted_iota(jnp.int32, (middle.shape[0], 1), 0)
     for slot in range(slots):
@@ -238,6 +239,14 @@
     slots = out_ref.shape[1]
     for owner in range(out_ref.shape[0]):
         out_ref[owner] = total[owner * slots : (owner + 1) * slots]
+
+
+def exchange_groups(size):
+    bits = size.bit_length() - 1
+    groups = [[1]] if bits else []
+    for bit in range(1, bits, 2):
+        groups.append([part << bit for part in range(1, 4 if bit + 1 < bits else 2)])
+    return groups
 
 
 def swap(array, axis, distance, size):
@@ -307,12 +316,14 @@
         "project",
         flops=PROJECT,
     )(slot_rows, group[None], received, residual_in, out_proj)
-    distance = 1
-    while distance < wide:
-        other = swap(summed, "wide", distance, wide)
-        distance *= 2
-        if distance < wide:
-            summed = (summed.astype(F32) + other.astype(F32)).astype(BF16)
+    groups = exchange_groups(wide)
+    for index, group_bits in enumerate(groups):
+        others = [swap(summed, "wide", distance, wide) for distance in group_bits]
+        if index + 1 < len(groups):
+            total = summed.astype(F32)
+            for other in others:
+                total = total + other.astype(F32)
+            summed = total.astype(BF16)
     columns = gate_weight.shape[1]
     padded = -(-columns // 128) * 128
     gate_shape = pltpu.VMEM((rows, padded + 256), BF16)
@@ -320,10 +331,10 @@
     middle, scaled, gate = call(
         gate_kernel,
         (pltpu.VMEM((slots, features), F32), pltpu.VMEM((rows, features), BF16), gate_shape),
-        [SMEM] + [VMEM] * 4,
+        [SMEM] + [VMEM] * (3 + len(others)),
         "gate",
         flops=EXPAND // 2,
-    )(group[None], summed, other, norm_gain[None, :], gate_weight)
+    )(group[None], norm_gain[None, :], gate_weight, summed, *others)
     up = call(up_kernel, up_shape, [VMEM] * 2, "up", flops=EXPAND // 2)(scaled, up_weight)
     distance = 1
     while distance < narrow:

time: 65.5 us -> 63.4 us (0.968)
  waiting for transfers between devices: 16.3 us -> 10.2 us
  starting transfers between devices: 4.4 us -> 7.77 us
    ppermute x7 -> x8, waiting for transfers between devices: 16.3 us -> 10.2 us  [swap(): return lax.ppermute(array, axis, [(i, i ^ distance) for i in range(size)])]
    ppermute x7 -> x8, starting transfers between devices: 4.4 us -> 7.77 us  [swap(): return lax.ppermute(array, axis, [(i, i ^ distance) for i in range(size)])]
  transfers between devices with their start and end apart: 7 -> 8, of which waited for: 5 -> 4; matrix products, arithmetic and copies ran while one was open for 0% -> 0% of each run, Pallas kernels for 2% -> 2%
where the time goes in v7:
time: 63.4 us; the launch traced here: 63.1 us
  blocking collectives  35.1 us (55%)
  waiting for transfers between devices  10.2 us (16%)
  Pallas kernels  9.07 us (14%)
  starting transfers between devices  7.77 us (12%)
  other arithmetic  0.67 us (1%)
    all_to_all x1, blocking collectives, shards(): queries = lax.all_to_all(packed, 'wide', 0, 0, tiled=True)  14.5 us
    all_to_all x1, blocking collectives, shards(): total = jnp.sum(lax.all_to_all(down, 'wide', 0, 0, tiled=True), axis=0)  10.4 us
    all_to_all x1, blocking collectives, shards(): received = lax.all_to_all(heads_out, ('wide', 'narrow'), 0, 0, tiled=True)  10.3 us
    ppermute x8, waiting for transfers between devices, swap(): return lax.ppermute(array, axis, [(i, i ^ distance) for i in range(size)])  10.2 us
    ppermute x8, starting transfers between devices, swap(): return lax.ppermute(array, axis, [(i, i ^ distance) for i in range(size)])  7.77 us
    pallas_call x1, Pallas kernels, shards(): call(functools.partial(attend_kernel, narrow, blocks, scale), pltpu.VMEM(...  3.11 us
  transfers between devices with their start and end apart: 8, of which 4 were waited for; matrix products, arithmetic and copies ran while one was open for 0% of the time, Pallas kernels for 2%

profile of v7, /device:TPU:0, one launch (start us, length us, event | category | flops | bytes accessed | tf_op | source)
XLA Modules:
  0.0 63.1 jit_solution(14173228740654582145)
XLA Ops:
  0.0 0.0 slice-start
  0.0 1.0 %pack.1 = bf16[8,2,24,128]{3,2,1,0:T(8,128)(2,1)S(1)} custom-call(s32[1]{0:T(128)} %bitcast.group_ref, bf16[2,16,128]{2,1,0:T(8,128)(2,1)} %nope_hbm.1, bf16[2,16,64]{2,1,0:T(8,128)(2,1)} %rope_hbm.1), custom_call_target="tpu_custom_call" | custom-call | flops 10000000000 | tf_op jit(solution)/shard_map/pack/pallas_call | solution.py:282
  1.0 14.5 %all_to_all.15.query_ref = bf16[8,2,24,128]{3,2,1,0:T(8,128)(2,1)S(1)} all-to-all(bf16[8,2,24,128]{3,2,1,0:T(8,128)(2,1)S(1)} %pack.1), channel_id=1, replica_groups=mesh['wide'=8,'narrow'=4] {'wide'}, dimensions={0} | all-to-all | bytes 196608 | tf_op jit(solution)/shard_map/all_to_all | solution.py:294
  15.5 0.0 copy-done
  15.5 0.0 copy-done.2
  15.5 0.0 copy-done.3
  15.5 0.0 copy-done.5
  15.5 0.0 copy-done.6
  15.5 0.0 copy-start.1
  15.5 0.0 copy-start.4
  15.5 0.0 slice-start.1
  15.5 3.1 %attend.1 = bf16[32,16,128]{2,1,0:T(8,128)(2,1)S(1)} custom-call(s32[1]{0:T(128)} %bitcast.group_ref, s32[16]{0:T(128)S(1)} %copy-done.6, s32[2]{0:T(128)S(1)} %copy-done.5, bf16[8,2,24,128]{3,2,1,0:T(8,128)(2,1)S(1)} %all_to_all.15.query_ref, bf16[16,128,512]{2,1,0:T(8,128)(2,1)S(1)} %copy-done.2, bf16[2,576,2048]{2,1,0:T(8,128)(2,1)S(1)} %bitcast.8, ...), custom_call_target="tpu_custom_call" | custom-call | flops 15000000512 | tf_op jit(solution)/shard_map/attend/pallas_call | solution.py:296
  18.7 0.0 slice-start.2
  18.7 10.3 %all_to_all.16.heads_ref = bf16[32,16,128]{2,1,0:T(8,128)(2,1)S(1)} all-to-all(bf16[32,16,128]{2,1,0:T(8,128)(2,1)S(1)} %attend.1), channel_id=1, replica_groups=mesh['wide'=8,'narrow'=4] {'wide','narrow'}, dimensions={0} | all-to-all | bytes 262144 | tf_op jit(solution)/shard_map/all_to_all | solution.py:311
  29.0 0.0 copy-done.1
  29.0 0.0 copy-done.4
  29.0 1.2 %project.1 = bf16[16,1792]{1,0:T(8,128)(2,1)S(1)} custom-call(s32[16]{0:T(128)S(1)} %copy-done.6, s32[1]{0:T(128)} %bitcast.group_ref, bf16[32,16,128]{2,1,0:T(8,128)(2,1)S(1)} %all_to_all.16.heads_ref, bf16[2,1792]{1,0:T(2,128)(2,1)S(1)} %copy-done.4, bf16[1024,1792]{1,0:T(8,128)(2,1)S(1)} %copy-done.1), custom_call_target="tpu_custom_call" | custom-call | flops 12000000000 | tf_op jit(solution)/shard_map/project/pallas_call | solution.py:312
  30.2 0.7 %collective-permute-start = (bf16[16,1792]{1,0:T(8,128)(2,1)S(1)}, bf16[16,1792]{1,0:T(8,128)(2,1)S(1)}, u32[]{:S(2)}, u32[]{:S(2)}) collective-permute-start(bf16[16,1792]{1,0:T(8,128)(2,1)S(1)} %project.1), channel_id=1, source_target_pairs={{0,4},{4,0},{8,12},{12,8},{16,20},{20,16},{24,28},{28,24},{1,5},{5... | collective-permute-start | bytes 172040 | tf_op jit(solution)/shard_map/ppermute | solution.py:253
  30.9 3.5 %collective-permute-done = bf16[16,1792]{1,0:T(8,128)(2,1)S(1)} collective-permute-done((bf16[16,1792]{1,0:T(8,128)(2,1)S(1)}, bf16[16,1792]{1,0:T(8,128)(2,1)S(1)}, u32[]{:S(2)}, u32[]{:S(2)}) %collective-permute-start) | collective-permute-done | bytes 57376 | tf_op jit(solution)/shard_map/ppermute | solution.py:253
  34.5 1.4 %collective-permute-start.3 = (bf16[16,1792]{1,0:T(8,128)(2,1)S(1)}, bf16[16,1792]{1,0:T(8,128)(2,1)S(1)}, u32[]{:S(2)}, u32[]{:S(2)}) collective-permute-start(bf16[16,1792]{1,0:T(8,128)(2,1)S(1)} %add_convert_fusion.refs_0_), channel_id=1, source_target_pairs={{0,24},{4,28},{8,16},{12,20},{16,8},{20,12},{24,0},{28,4},{1,25},{... | collective-permute-start | bytes 172040 | tf_op jit(solution)/shard_map/ppermute | solution.py:253
  35.9 0.8 %collective-permute-start.2 = (bf16[16,1792]{1,0:T(8,128)(2,1)S(1)}, bf16[16,1792]{1,0:T(8,128)(2,1)S(1)}, u32[]{:S(2)}, u32[]{:S(2)}) collective-permute-start(bf16[16,1792]{1,0:T(8,128)(2,1)S(1)} %add_convert_fusion.refs_0_), channel_id=1, source_target_pairs={{0,16},{4,20},{8,24},{12,28},{16,0},{20,4},{24,8},{28,12},{1,17},{... | collective-permute-start | bytes 172040 | tf_op jit(solution)/shard_map/ppermute | solution.py:253
  36.7 2.3 %collective-permute-start.1 = (bf16[16,1792]{1,0:T(8,128)(2,1)S(1)}, bf16[16,1792]{1,0:T(8,128)(2,1)S(1)}, u32[]{:S(2)}, u32[]{:S(2)}) collective-permute-start(bf16[16,1792]{1,0:T(8,128)(2,1)S(1)} %add_convert_fusion.refs_0_), channel_id=1, source_target_pairs={{0,8},{4,12},{8,0},{12,4},{16,24},{20,28},{24,16},{28,20},{1,9},{5... | collective-permute-start | bytes 172040 | tf_op jit(solution)/shard_map/ppermute | solution.py:253
  38.9 0.0 copy-done.7
  38.9 1.6 %collective-permute-done.3.refs_3_ = bf16[16,1792]{1,0:T(8,128)(2,1)S(1)} collective-permute-done((bf16[16,1792]{1,0:T(8,128)(2,1)S(1)}, bf16[16,1792]{1,0:T(8,128)(2,1)S(1)}, u32[]{:S(2)}, u32[]{:S(2)}) %collective-permute-start.3) | collective-permute-done | bytes 57376 | tf_op jit(solution)/shard_map/ppermute | solution.py:253
  40.5 1.2 %collective-permute-done.2.refs_2_ = bf16[16,1792]{1,0:T(8,128)(2,1)S(1)} collective-permute-done((bf16[16,1792]{1,0:T(8,128)(2,1)S(1)}, bf16[16,1792]{1,0:T(8,128)(2,1)S(1)}, u32[]{:S(2)}, u32[]{:S(2)}) %collective-permute-start.2) | collective-permute-done | bytes 57376 | tf_op jit(solution)/shard_map/ppermute | solution.py:253
  41.8 0.0 collective-permute-done.1.refs_1_
  41.8 0.0 slice-done
  41.8 0.0 slice-done.1
  41.8 1.2 %gate.1 = (f32[2,1792]{1,0:T(2,128)S(1)}, bf16[16,1792]{1,0:T(8,128)(2,1)S(1)}, bf16[16,2560]{1,0:T(8,128)(2,1)S(1)}) custom-call(s32[1]{0:T(128)} %bitcast.group_ref, bf16[1,1792]{1,0:T(2,128)(2,1)S(1)} %broadcast_in_dim.10.gain_ref, bf16[1792,2304]{1,0:T(8,128)(2,1)S(1)} %bitcast.3, bf16[16,1792]{1,0:T(8,128)(2,1)S(1)} %add_convert_fusion.refs_0_, ...), custom_call_target="tpu_custom_call" | custom-call | flops 2000000000 | tf_op jit(solution)/shard_map/gate/pallas_call | solution.py:331
  43.0 0.0 collective-permute-start.4
  43.0 0.0 slice-start.4
  43.0 0.0 slice-done.2
  43.0 0.0 slice-done.3
  43.0 0.0 slice-start.5
  43.0 1.2 %up.1.first_ref = bf16[16,2304]{1,0:T(8,128)(2,1)S(1)} custom-call(bf16[16,1792]{1,0:T(8,128)(2,1)S(1)} %get-tuple-element.10.scaled_ref, bf16[1792,2304]{1,0:T(8,128)(2,1)S(1)} %bitcast.5), custom_call_target="tpu_custom_call" | custom-call | flops 2000000000 | tf_op jit(solution)/shard_map/up/pallas_call | solution.py:338
  44.2 0.5 collective-permute-start.6
  44.7 0.0 collective-permute-done.4.second_ref
  44.7 0.1 merge_gate.1.first_gate_ref
  44.8 0.9 %collective-permute-start.5 = (bf16[16,2560]{1,0:T(8,128)(2,1)S(1)}, bf16[16,2560]{1,0:T(8,128)(2,1)S(1)}, u32[]{:S(2)}, u32[]{:S(2)}) collective-permute-start(bf16[16,2560]{1,0:T(8,128)(2,1)S(1)} %merge_gate.1.first_gate_ref), channel_id=1, source_target_pairs={{0,2},{1,3},{2,0},{3,1},{4,6},{5,7},{6,4},{7,5},{8,10},{9,11},{10,... | collective-permute-start | bytes 245768 | tf_op jit(solution)/shard_map/ppermute | solution.py:253
  45.7 0.0 collective-permute-done.6.second_ref
  45.7 1.2 %collective-permute-start.7 = (bf16[16,2304]{1,0:T(8,128)(2,1)S(1)}, bf16[16,2304]{1,0:T(8,128)(2,1)S(1)}, u32[]{:S(2)}, u32[]{:S(2)}) collective-permute-start(bf16[16,2304]{1,0:T(8,128)(2,1)S(1)} %merge_up.1.first_up_ref), channel_id=1, source_target_pairs={{0,2},{1,3},{2,0},{3,1},{4,6},{5,7},{6,4},{7,5},{8,10},{9,11},{10,... | collective-permute-start | bytes 221192 | tf_op jit(solution)/shard_map/ppermute | solution.py:253
  46.9 3.9 %collective-permute-done.7.second_up_ref = bf16[16,2304]{1,0:T(8,128)(2,1)S(1)} collective-permute-done((bf16[16,2304]{1,0:T(8,128)(2,1)S(1)}, bf16[16,2304]{1,0:T(8,128)(2,1)S(1)}, u32[]{:S(2)}, u32[]{:S(2)}) %collective-permute-start.7) | collective-permute-done | bytes 73760 | tf_op jit(solution)/shard_map/ppermute | solution.py:253
  50.8 0.0 collective-permute-done.5.second_gate_ref
  50.8 0.0 slice-done.4
  50.8 0.0 slice-done.5
  50.9 1.3 %contract.1 = f32[8,2,1792]{2,1,0:T(2,128)S(1)} custom-call(bf16[16,2560]{1,0:T(8,128)(2,1)S(1)} %merge_gate.1.first_gate_ref, bf16[16,2560]{1,0:T(8,128)(2,1)S(1)} %collective-permute-done.5.second_gate_ref, bf16[16,2304]{1,0:T(8,128)(2,1)S(1)} %merge_up.1.first_up_ref, bf16[16,2304]{1,0:T(8,128)(2,1)S(1)} %collective-permute-done.7.second_up_ref, ...), custom_call_target="tpu_custom_call" | custom-call | flops 4000000000 | tf_op jit(solution)/shard_map/contract/pallas_call | solution.py:351
  52.1 10.4 %all_to_all.17 = f32[8,2,1792]{2,1,0:T(2,128)S(1)} all-to-all(f32[8,2,1792]{2,1,0:T(2,128)S(1)} %contract.1), channel_id=1, replica_groups=mesh['wide'=8,'narrow'=4] {'wide'}, dimensions={0} | all-to-all | bytes 229376 | tf_op jit(solution)/shard_map/all_to_all | solution.py:358
  62.5 0.6 add_convert_fusion.1
  (14 shorter events, 0.1 us)
Async XLA Ops:
  0.0 15.5 %copy-start = (bf16[2,2048,576]{1,2,0:T(8,128)(2,1)S(1)}, bf16[2,2048,576]{1,2,0:T(8,128)(2,1)}, u32[]{:S(2)}) copy-start(bf16[2,2048,576]{1,2,0:T(8,128)(2,1)} %param.18) | copy-start | bytes 14155780
  0.0 15.5 %copy-start.2 = (bf16[16,128,512]{2,1,0:T(8,128)(2,1)S(1)}, bf16[16,128,512]{2,1,0:T(8,128)(2,1)}, u32[]{:S(2)}) copy-start(bf16[16,128,512]{2,1,0:T(8,128)(2,1)} %key_ref.1) | copy-start | bytes 6291460
  0.0 15.5 %copy-start.3 = (bf16[16,512,128]{2,1,0:T(8,128)(2,1)S(1)}, bf16[16,512,128]{2,1,0:T(8,128)(2,1)}, u32[]{:S(2)}) copy-start(bf16[16,512,128]{2,1,0:T(8,128)(2,1)} %value_ref.1) | copy-start | bytes 6291460
  0.0 15.5 %copy-start.5 = (s32[2]{0:T(128)S(1)}, s32[2]{0:T(128)}, u32[]{:S(2)}) copy-start(s32[2]{0:T(128)} %lengths_ref.1) | copy-start | bytes 28
  0.0 15.5 %copy-start.6 = (s32[16]{0:T(128)S(1)}, s32[16]{0:T(128)}, u32[]{:S(2)}) copy-start(s32[16]{0:T(128)} %rows_ref.3) | copy-start | bytes 196
  0.0 41.7 %slice-start = ((s8[8257536]{0:T(1024)(128)(4,1)}), s8[4194304]{0:T(1024)(128)(4,1)S(1)}, s32[]{:S(2)}) async-start(s8[8257536]{0:T(1024)(128)(4,1)} %bitcast.2), calls=%async_computation.3 | async-start | bytes 8388608
  15.5 13.5 %copy-start.1 = (bf16[1024,1792]{1,0:T(8,128)(2,1)S(1)}, bf16[1024,1792]{1,0:T(8,128)(2,1)}, u32[]{:S(2)}) copy-start(bf16[1024,1792]{1,0:T(8,128)(2,1)} %weight_ref.4) | copy-start | bytes 11010052
  15.5 13.4 %copy-start.4 = (bf16[2,1792]{1,0:T(2,128)(2,1)S(1)}, bf16[2,1792]{1,0:T(2,128)(2,1)}, u32[]{:S(2)}) copy-start(bf16[2,1792]{1,0:T(2,128)(2,1)} %residual_ref.1) | copy-start | bytes 21508
  15.5 26.2 %slice-start.1 = ((s8[8257536]{0:T(1024)(128)(4,1)}), s8[4063232]{0:T(1024)(128)(4,1)S(1)}, s32[]{:S(2)}) async-start(s8[8257536]{0:T(1024)(128)(4,1)} %bitcast.2), calls=%async_computation.4 | async-start | bytes 8126464
  18.7 24.4 %slice-start.2 = ((s8[8257536]{0:T(1024)(128)(4,1)}), s8[4194304]{0:T(1024)(128)(4,1)S(1)}, s32[]{:S(2)}) async-start(s8[8257536]{0:T(1024)(128)(4,1)} %bitcast.4), calls=%async_computation.5 | async-start | bytes 8388608
  29.0 10.0 %copy-start.7 = (bf16[1792]{0:T(1024)(128)(2,1)S(1)}, bf16[1792]{0:T(1024)(128)(2,1)}, u32[]{:S(2)}) copy-start(bf16[1792]{0:T(1024)(128)(2,1)} %param.22) | copy-start | bytes 10756
  29.0 14.1 %slice-start.3 = ((s8[8257536]{0:T(1024)(128)(4,1)}), s8[4063232]{0:T(1024)(128)(4,1)S(1)}, s32[]{:S(2)}) async-start(s8[8257536]{0:T(1024)(128)(4,1)} %bitcast.4), calls=%async_computation.6 | async-start | bytes 8126464
  30.2 4.2 %collective-permute-start = (bf16[16,1792]{1,0:T(8,128)(2,1)S(1)}, bf16[16,1792]{1,0:T(8,128)(2,1)S(1)}, u32[]{:S(2)}, u32[]{:S(2)}) collective-permute-start(bf16[16,1792]{1,0:T(8,128)(2,1)S(1)} %project.1), channel_id=1, source_target_pairs={{0,4},{4,0},{8,12},{12,8},{16,20},{20,16},{24,28},{28,24},{1,5},{5... | collective-permute-start | bytes 172040 | tf_op jit(solution)/shard_map/ppermute | solution.py:253
  34.5 6.1 %collective-permute-start.3 = (bf16[16,1792]{1,0:T(8,128)(2,1)S(1)}, bf16[16,1792]{1,0:T(8,128)(2,1)S(1)}, u32[]{:S(2)}, u32[]{:S(2)}) collective-permute-start(bf16[16,1792]{1,0:T(8,128)(2,1)S(1)} %add_convert_fusion.refs_0_), channel_id=1, source_target_pairs={{0,24},{4,28},{8,16},{12,20},{16,8},{20,12},{24,0},{28,4},{1,25},{... | collective-permute-start | bytes 172040 | tf_op jit(solution)/shard_map/ppermute | solution.py:253
  35.9 5.9 %collective-permute-start.2 = (bf16[16,1792]{1,0:T(8,128)(2,1)S(1)}, bf16[16,1792]{1,0:T(8,128)(2,1)S(1)}, u32[]{:S(2)}, u32[]{:S(2)}) collective-permute-start(bf16[16,1792]{1,0:T(8,128)(2,1)S(1)} %add_convert_fusion.refs_0_), channel_id=1, source_target_pairs={{0,16},{4,20},{8,24},{12,28},{16,0},{20,4},{24,8},{28,12},{1,17},{... | collective-permute-start | bytes 172040 | tf_op jit(solution)/shard_map/ppermute | solution.py:253
  36.7 5.1 %collective-permute-start.1 = (bf16[16,1792]{1,0:T(8,128)(2,1)S(1)}, bf16[16,1792]{1,0:T(8,128)(2,1)S(1)}, u32[]{:S(2)}, u32[]{:S(2)}) collective-permute-start(bf16[16,1792]{1,0:T(8,128)(2,1)S(1)} %add_convert_fusion.refs_0_), channel_id=1, source_target_pairs={{0,8},{4,12},{8,0},{12,4},{16,24},{20,28},{24,16},{28,20},{1,9},{5... | collective-permute-start | bytes 172040 | tf_op jit(solution)/shard_map/ppermute | solution.py:253
  43.0 1.7 %collective-permute-start.4 = (bf16[16,2560]{1,0:T(8,128)(2,1)S(1)}, bf16[16,2560]{1,0:T(8,128)(2,1)S(1)}, u32[]{:S(2)}, u32[]{:S(2)}) collective-permute-start(bf16[16,2560]{1,0:T(8,128)(2,1)S(1)} %get-tuple-element.9.first_ref), channel_id=1, source_target_pairs={{0,1},{1,0},{2,3},{3,2},{4,5},{5,4},{6,7},{7,6},{8,9},{9,8},{10,11... | collective-permute-start | bytes 245768 | tf_op jit(solution)/shard_map/ppermute | solution.py:253
  43.0 7.9 %slice-start.4 = ((s8[8257536]{0:T(1024)(128)(4,1)}), s8[4194304]{0:T(1024)(128)(4,1)S(1)}, s32[]{:S(2)}) async-start(s8[8257536]{0:T(1024)(128)(4,1)} %bitcast.6), calls=%async_computation.7 | async-start | bytes 8388608
  43.0 7.8 %slice-start.5 = ((s8[8257536]{0:T(1024)(128)(4,1)}), s8[4063232]{0:T(1024)(128)(4,1)S(1)}, s32[]{:S(2)}) async-start(s8[8257536]{0:T(1024)(128)(4,1)} %bitcast.6), calls=%async_computation.8 | async-start | bytes 8126464
  44.2 1.5 %collective-permute-start.6 = (bf16[16,2304]{1,0:T(8,128)(2,1)S(1)}, bf16[16,2304]{1,0:T(8,128)(2,1)S(1)}, u32[]{:S(2)}, u32[]{:S(2)}) collective-permute-start(bf16[16,2304]{1,0:T(8,128)(2,1)S(1)} %up.1.first_ref), channel_id=1, source_target_pairs={{0,1},{1,0},{2,3},{3,2},{4,5},{5,4},{6,7},{7,6},{8,9},{9,8},{10,11... | collective-permute-start | bytes 221192 | tf_op jit(solution)/shard_map/ppermute | solution.py:253
  44.8 6.0 %collective-permute-start.5 = (bf16[16,2560]{1,0:T(8,128)(2,1)S(1)}, bf16[16,2560]{1,0:T(8,128)(2,1)S(1)}, u32[]{:S(2)}, u32[]{:S(2)}) collective-permute-start(bf16[16,2560]{1,0:T(8,128)(2,1)S(1)} %merge_gate.1.first_gate_ref), channel_id=1, source_target_pairs={{0,2},{1,3},{2,0},{3,1},{4,6},{5,7},{6,4},{7,5},{8,10},{9,11},{10,... | collective-permute-start | bytes 245768 | tf_op jit(solution)/shard_map/ppermute | solution.py:253
  45.7 5.1 %collective-permute-start.7 = (bf16[16,2304]{1,0:T(8,128)(2,1)S(1)}, bf16[16,2304]{1,0:T(8,128)(2,1)S(1)}, u32[]{:S(2)}, u32[]{:S(2)}) collective-permute-start(bf16[16,2304]{1,0:T(8,128)(2,1)S(1)} %merge_up.1.first_up_ref), channel_id=1, source_target_pairs={{0,2},{1,3},{2,0},{3,1},{4,6},{5,7},{6,4},{7,5},{8,10},{9,11},{10,... | collective-permute-start | bytes 221192 | tf_op jit(solution)/shard_map/ppermute | solution.py:253

commit v8 on v7

--- a/solution.py
+++ b/solution.py
@@ -141,7 +141,9 @@
         out_ref[target] = pieces[(target // narrow) % blocks]
 
 
-def project_kernel(narrow, blocks, rows_ref, group_ref, heads_ref, residual_ref, weight_ref, out_ref):
+def project_kernel(
+    narrow, blocks, rows_ref, group_ref, heads_ref, residual_ref, weight_ref, own_ref, out_ref
+):
     wide = heads_ref.shape[0] // narrow
     slots = residual_ref.shape[0]
     rows = wide * slots
@@ -169,6 +171,7 @@
     for slot in range(slots):
         own = residual_ref[slot : slot + 1, :].astype(F32)
         total = total + jnp.where(row == group * slots + slot, own, 0.0)
+    own_ref[...] = total
     out_ref[...] = total.astype(BF16)
 
 
@@ -190,7 +193,7 @@
 
 
 def gate_kernel(group_ref, gain_ref, weight_ref, *refs):
-    parts, (middle_ref, scaled_ref, out_ref) = refs[:-3], refs[-3:]
+    parts, (middle_ref, scaled_ref, own_ref, out_ref) = refs[:-4], refs[-4:]
     middle = parts[0][...].astype(F32)
     for part in parts[1:]:
         middle = middle + part[...].astype(F32)
@@ -201,44 +204,68 @@
         middle_ref[slot : slot + 1] = jnp.sum(own, axis=0, keepdims=True)
     scaled = (middle * gain_ref[...].astype(F32)).astype(BF16)
     scaled_ref[...] = scaled
-    columns = weight_ref.shape[1]
-    out_ref[:, :columns] = jnp.dot(scaled, weight_ref[...], preferred_element_type=F32).astype(BF16)
-    put_sums(out_ref, out_ref.shape[1] - 256, jnp.sum(middle * middle, axis=1, keepdims=True))
-
-
-def up_kernel(scaled_ref, weight_ref, out_ref):
-    out_ref[...] = jnp.dot(scaled_ref[...], weight_ref[...], preferred_element_type=F32).astype(
-        BF16
-    )
-
-
-def merge_kernel(first_ref, second_ref, out_ref):
-    out_ref[...] = (first_ref[...].astype(F32) + second_ref[...].astype(F32)).astype(BF16)
-
-
-def merge_sums_kernel(first_ref, second_ref, out_ref):
-    end = out_ref.shape[1] - 256
-    out_ref[:, :end] = (
-        first_ref[:, :end].astype(F32) + second_ref[:, :end].astype(F32)
-    ).astype(BF16)
-    put_sums(out_ref, end, get_sums(first_ref, end) + get_sums(second_ref, end))
+    put_gate(
+        own_ref,
+        out_ref,
+        jnp.dot(scaled, weight_ref[...], preferred_element_type=F32),
+        jnp.sum(middle * middle, axis=1, keepdims=True),
+    )
+
+
+def put_gate(own_ref, out_ref, gate, square):
+    columns, end = gate.shape[1], own_ref.shape[1] - 128
+    own_ref[:, :columns] = gate
+    own_ref[:, end:] = jnp.broadcast_to(square, (gate.shape[0], 128))
+    out_ref[:, :columns] = gate.astype(BF16)
+    put_sums(out_ref, end, square)
+
+
+def up_kernel(scaled_ref, weight_ref, own_ref, out_ref):
+    up = jnp.dot(scaled_ref[...], weight_ref[...], preferred_element_type=F32)
+    own_ref[...] = up
+    out_ref[...] = up.astype(BF16)
+
+
+def merge_kernel(first_ref, second_ref, own_ref, out_ref):
+    total = first_ref[...] + second_ref[...].astype(F32)
+    own_ref[...] = total
+    out_ref[...] = total.astype(BF16)
+
+
+def merge_sums_kernel(columns, first_ref, second_ref, own_ref, out_ref):
+    end = own_ref.shape[1] - 128
+    put_gate(
+        own_ref,
+        out_ref,
+        first_ref[:, :columns] + second_ref[:, :columns].astype(F32),
+        first_ref[:, end : end + 1] + get_sums(second_ref, end),
+    )
 
 
 def contract_kernel(
     first_gate_ref, second_gate_ref, first_up_ref, second_up_ref, weight_ref, out_ref
 ):
-    end = first_gate_ref.shape[1] - 256
+    end = first_gate_ref.shape[1] - 128
     columns = weight_ref.shape[0]
-    square = get_sums(first_gate_ref, end) + get_sums(second_gate_ref, end)
+    square = first_gate_ref[:, end : end + 1] + get_sums(second_gate_ref, end)
     factor = lax.rsqrt(square / D + 1e-06)
-    gate = first_gate_ref[:, :columns].astype(F32) + second_gate_ref[:, :columns].astype(F32)
+    gate = first_gate_ref[:, :columns] + second_gate_ref[:, :columns].astype(F32)
     gate = gate * factor
-    up = (first_up_ref[...].astype(F32) + second_up_ref[...].astype(F32)) * factor
+    up = (first_up_ref[...] + second_up_ref[...].astype(F32)) * factor
     hidden = (gate / (1.0 + jnp.exp(-gate)) * up).astype(BF16)
     total = jnp.dot(hidden, weight_ref[...], preferred_element_type=F32)
     slots = out_ref.shape[1]
     for owner in range(out_ref.shape[0]):
         out_ref[owner] = total[owner * slots : (owner + 1) * slots]
+
+
+def exchange(array, first, second, wide, narrow):
+    pairs = [
+        (w * narrow + n, (w ^ (second if n % 2 else first)) * narrow + n)
+        for w in range(wide)
+        for n in range(narrow)
+    ]
+    return lax.ppermute(array, ("wide", "narrow"), pairs)
 
 
 def exchange_groups(size):
@@ -309,45 +336,53 @@
         near(absorb_value),
     )
     received = lax.all_to_all(heads_out, ("wide", "narrow"), 0, 0, tiled=True)
-    summed = call(
+    total, summed = call(
         functools.partial(project_kernel, narrow, blocks),
-        pltpu.VMEM((rows, features), BF16),
+        (pltpu.VMEM((rows, features), F32), pltpu.VMEM((rows, features), BF16)),
         [SMEM, SMEM, VMEM, VMEM, VMEM],
         "project",
         flops=PROJECT,
     )(slot_rows, group[None], received, residual_in, out_proj)
     groups = exchange_groups(wide)
-    for index, group_bits in enumerate(groups):
-        others = [swap(summed, "wide", distance, wide) for distance in group_bits]
+    for index, distances in enumerate(groups):
+        others = [
+            exchange(summed, first, second, wide, narrow)
+            for first, second in zip(distances, distances[::-1])
+        ]
         if index + 1 < len(groups):
-            total = summed.astype(F32)
             for other in others:
                 total = total + other.astype(F32)
             summed = total.astype(BF16)
     columns = gate_weight.shape[1]
     padded = -(-columns // 128) * 128
-    gate_shape = pltpu.VMEM((rows, padded + 256), BF16)
-    up_shape = pltpu.VMEM((rows, columns), BF16)
-    middle, scaled, gate = call(
+    gate_shapes = (pltpu.VMEM((rows, padded + 128), F32), pltpu.VMEM((rows, padded + 256), BF16))
+    up_shapes = (pltpu.VMEM((rows, columns), F32), pltpu.VMEM((rows, columns), BF16))
+    middle, scaled, gate, gate_sent = call(
         gate_kernel,
-        (pltpu.VMEM((slots, features), F32), pltpu.VMEM((rows, features), BF16), gate_shape),
+        (pltpu.VMEM((slots, features), F32), pltpu.VMEM((rows, features), BF16)) + gate_shapes,
         [SMEM] + [VMEM] * (3 + len(others)),
         "gate",
         flops=EXPAND // 2,
-    )(group[None], norm_gain[None, :], gate_weight, summed, *others)
-    up = call(up_kernel, up_shape, [VMEM] * 2, "up", flops=EXPAND // 2)(scaled, up_weight)
-    distance = 1
-    while distance < narrow:
-        other_gate = swap(gate, "narrow", distance, narrow)
-        other_up = swap(up, "narrow", distance, narrow)
-        distance *= 2
-        if distance < narrow:
-            gate = call(
-                merge_sums_kernel, gate_shape, [VMEM] * 2, "merge_gate", flops=MERGE // 4
+    )(group[None], norm_gain[None, :], gate_weight, total, *others)
+    up, up_sent = call(up_kernel, up_shapes, [VMEM] * 2, "up", flops=EXPAND // 2)(
+        scaled, up_weight
+    )
+    distance = narrow // 2
+    while distance:
+        other_gate = swap(gate_sent, "narrow", distance, narrow)
+        other_up = swap(up_sent, "narrow", distance, narrow)
+        distance //= 2
+        if distance:
+            gate, gate_sent = call(
+                functools.partial(merge_sums_kernel, columns),
+                gate_shapes,
+                [VMEM] * 2,
+                "merge_gate",
+                flops=MERGE // 4,
             )(gate, other_gate)
-            up = call(merge_kernel, up_shape, [VMEM] * 2, "merge_up", flops=MERGE // 4)(
-                up, other_up
-            )
+            up, up_sent = call(
+                merge_kernel, up_shapes, [VMEM] * 2, "merge_up", flops=MERGE // 4
+            )(up, other_up)
     down = call(
         contract_kernel,
         pltpu.VMEM((wide, slots, features), F32),

time: 63.4 us -> 63.3 us (level)
  waiting for transfers between devices: 10.2 us -> 11.2 us
    ppermute x0 -> x4, waiting for transfers between devices: none -> 6.67 us  [exchange(): return lax.ppermute(array, ('wide', 'narrow'), pairs)]
    ppermute x8 -> x4, waiting for transfers between devices: 10.2 us -> 4.57 us  [swap(): return lax.ppermute(array, axis, [(i, i ^ distance) for i in range(size)])]
    ppermute x8 -> x4, starting transfers between devices: 7.77 us -> 2.13 us  [swap(): return lax.ppermute(array, axis, [(i, i ^ distance) for i in range(size)])]
    ppermute x0 -> x4, starting transfers between devices: none -> 5.18 us  [exchange(): return lax.ppermute(array, ('wide', 'narrow'), pairs)]
  transfers between devices with their start and end apart: 8 -> 8, of which waited for: 4 -> 6; matrix products, arithmetic and copies ran while one was open for 0% -> 0% of each run, Pallas kernels for 2% -> 2%
where the time goes in v8:
time: 63.3 us; the launch traced here: 63 us
  blocking collectives  34.5 us (55%)
  waiting for transfers between devices  11.2 us (18%)
  Pallas kernels  9.08 us (14%)
  starting transfers between devices  7.31 us (12%)
  other arithmetic  0.67 us (1%)
    all_to_all x1, blocking collectives, shards(): queries = lax.all_to_all(packed, 'wide', 0, 0, tiled=True)  14.5 us
    all_to_all x1, blocking collectives, shards(): received = lax.all_to_all(heads_out, ('wide', 'narrow'), 0, 0, tiled=True)  10.3 us
    all_to_all x1, blocking collectives, shards(): total = jnp.sum(lax.all_to_all(down, 'wide', 0, 0, tiled=True), axis=0)  9.73 us
    ppermute x4, waiting for transfers between devices, exchange(): return lax.ppermute(array, ('wide', 'narrow'), pairs)  6.67 us
    ppermute x4, starting transfers between devices, exchange(): return lax.ppermute(array, ('wide', 'narrow'), pairs)  5.18 us
    ppermute x4, waiting for transfers between devices, swap(): return lax.ppermute(array, axis, [(i, i ^ distance) for i in range(size)])  4.57 us
    pallas_call x1, Pallas kernels, shards(): call(functools.partial(attend_kernel, narrow, blocks, scale), pltpu.VMEM(...  3.11 us
    ppermute x4, starting transfers between devices, swap(): return lax.ppermute(array, axis, [(i, i ^ distance) for i in range(size)])  2.13 us
  transfers between devices with their start and end apart: 8, of which 6 were waited for; matrix products, arithmetic and copies ran while one was open for 0% of the time, Pallas kernels for 2%

profile of v8, /device:TPU:0, one launch (start us, length us, event | category | flops | bytes accessed | tf_op | source)
XLA Modules:
  0.0 63.0 jit_solution(14925966220099241841)
XLA Ops:
  0.0 0.0 copy-start
  0.0 0.0 slice-start.2
  0.0 1.0 %pack.1 = bf16[8,2,24,128]{3,2,1,0:T(8,128)(2,1)S(1)} custom-call(s32[1]{0:T(128)} %bitcast.group_ref, bf16[2,16,128]{2,1,0:T(8,128)(2,1)} %nope_hbm.1, bf16[2,16,64]{2,1,0:T(8,128)(2,1)} %rope_hbm.1), custom_call_target="tpu_custom_call" | custom-call | flops 10000000000 | tf_op jit(solution)/shard_map/pack/pallas_call | solution.py:309
  1.0 14.5 %all_to_all.15.query_ref = bf16[8,2,24,128]{3,2,1,0:T(8,128)(2,1)S(1)} all-to-all(bf16[8,2,24,128]{3,2,1,0:T(8,128)(2,1)S(1)} %pack.1), channel_id=1, replica_groups=mesh['wide'=8,'narrow'=4] {'wide'}, dimensions={0} | all-to-all | bytes 196608 | tf_op jit(solution)/shard_map/all_to_all | solution.py:321
  15.5 0.0 copy-done
  15.5 0.0 copy-done.2
  15.5 0.0 copy-done.3
  15.5 0.0 copy-done.5
  15.5 0.0 copy-done.6
  15.5 0.0 copy-start.1
  15.5 0.0 copy-start.4
  15.5 0.0 slice-start.3
  15.5 3.1 %attend.1 = bf16[32,16,128]{2,1,0:T(8,128)(2,1)S(1)} custom-call(s32[1]{0:T(128)} %bitcast.group_ref, s32[16]{0:T(128)S(1)} %copy-done.6, s32[2]{0:T(128)S(1)} %copy-done.5, bf16[8,2,24,128]{3,2,1,0:T(8,128)(2,1)S(1)} %all_to_all.15.query_ref, bf16[16,128,512]{2,1,0:T(8,128)(2,1)S(1)} %copy-done.2, bf16[2,576,2048]{2,1,0:T(8,128)(2,1)S(1)} %bitcast.8, ...), custom_call_target="tpu_custom_call" | custom-call | flops 15000000512 | tf_op jit(solution)/shard_map/attend/pallas_call | solution.py:323
  18.7 0.0 slice-start
  18.7 10.3 %all_to_all.16.heads_ref = bf16[32,16,128]{2,1,0:T(8,128)(2,1)S(1)} all-to-all(bf16[32,16,128]{2,1,0:T(8,128)(2,1)S(1)} %attend.1), channel_id=1, replica_groups=mesh['wide'=8,'narrow'=4] {'wide','narrow'}, dimensions={0} | all-to-all | bytes 262144 | tf_op jit(solution)/shard_map/all_to_all | solution.py:338
  29.0 0.0 copy-done.1
  29.0 0.0 copy-done.4
  29.0 1.2 %project.1 = (f32[16,1792]{1,0:T(8,128)S(1)}, bf16[16,1792]{1,0:T(8,128)(2,1)S(1)}) custom-call(s32[16]{0:T(128)S(1)} %copy-done.6, s32[1]{0:T(128)} %bitcast.group_ref, bf16[32,16,128]{2,1,0:T(8,128)(2,1)S(1)} %all_to_all.16.heads_ref, bf16[2,1792]{1,0:T(2,128)(2,1)S(1)} %copy-done.4, bf16[1024,1792]{1,0:T(8,128)(2,1)S(1)} %copy-done.1), custom_call_target="tpu_custom_call" | custom-call | flops 12000000000 | tf_op jit(solution)/shard_map/project/pallas_call | solution.py:339
  30.2 0.7 %collective-permute-start = (bf16[16,1792]{1,0:T(8,128)(2,1)S(1)}, bf16[16,1792]{1,0:T(8,128)(2,1)S(1)}, u32[]{:S(2)}, u32[]{:S(2)}) collective-permute-start(bf16[16,1792]{1,0:T(8,128)(2,1)S(1)} %get-tuple-element.18), channel_id=1, source_target_pairs={{0,4},{1,5},{2,6},{3,7},{4,0},{5,1},{6,2},{7,3},{8,12},{9,13},{10,... | collective-permute-start | bytes 172040 | tf_op jit(solution)/shard_map/ppermute | solution.py:268
  31.0 3.5 %collective-permute-done = bf16[16,1792]{1,0:T(8,128)(2,1)S(1)} collective-permute-done((bf16[16,1792]{1,0:T(8,128)(2,1)S(1)}, bf16[16,1792]{1,0:T(8,128)(2,1)S(1)}, u32[]{:S(2)}, u32[]{:S(2)}) %collective-permute-start) | collective-permute-done | bytes 57376 | tf_op jit(solution)/shard_map/ppermute | solution.py:268
  34.5 1.4 %collective-permute-start.3 = (bf16[16,1792]{1,0:T(8,128)(2,1)S(1)}, bf16[16,1792]{1,0:T(8,128)(2,1)S(1)}, u32[]{:S(2)}, u32[]{:S(2)}) collective-permute-start(bf16[16,1792]{1,0:T(8,128)(2,1)S(1)} %get-tuple-element.29), channel_id=1, source_target_pairs={{0,24},{1,9},{2,26},{3,11},{4,28},{5,13},{6,30},{7,15},{8,16},{9,1... | collective-permute-start | bytes 172040 | tf_op jit(solution)/shard_map/ppermute | solution.py:268
  35.9 0.8 %collective-permute-start.2 = (bf16[16,1792]{1,0:T(8,128)(2,1)S(1)}, bf16[16,1792]{1,0:T(8,128)(2,1)S(1)}, u32[]{:S(2)}, u32[]{:S(2)}) collective-permute-start(bf16[16,1792]{1,0:T(8,128)(2,1)S(1)} %get-tuple-element.29), channel_id=1, source_target_pairs={{0,16},{1,17},{2,18},{3,19},{4,20},{5,21},{6,22},{7,23},{8,24},{9,... | collective-permute-start | bytes 172040 | tf_op jit(solution)/shard_map/ppermute | solution.py:268
  36.7 2.3 %collective-permute-start.1 = (bf16[16,1792]{1,0:T(8,128)(2,1)S(1)}, bf16[16,1792]{1,0:T(8,128)(2,1)S(1)}, u32[]{:S(2)}, u32[]{:S(2)}) collective-permute-start(bf16[16,1792]{1,0:T(8,128)(2,1)S(1)} %get-tuple-element.29), channel_id=1, source_target_pairs={{0,8},{1,25},{2,10},{3,27},{4,12},{5,29},{6,14},{7,31},{8,0},{9,17... | collective-permute-start | bytes 172040 | tf_op jit(solution)/shard_map/ppermute | solution.py:268
  38.9 0.0 copy-done.7
  39.0 1.6 %collective-permute-done.3.refs_3_ = bf16[16,1792]{1,0:T(8,128)(2,1)S(1)} collective-permute-done((bf16[16,1792]{1,0:T(8,128)(2,1)S(1)}, bf16[16,1792]{1,0:T(8,128)(2,1)S(1)}, u32[]{:S(2)}, u32[]{:S(2)}) %collective-permute-start.3) | collective-permute-done | bytes 57376 | tf_op jit(solution)/shard_map/ppermute | solution.py:268
  40.6 1.5 %collective-permute-done.2.refs_2_ = bf16[16,1792]{1,0:T(8,128)(2,1)S(1)} collective-permute-done((bf16[16,1792]{1,0:T(8,128)(2,1)S(1)}, bf16[16,1792]{1,0:T(8,128)(2,1)S(1)}, u32[]{:S(2)}, u32[]{:S(2)}) %collective-permute-start.2) | collective-permute-done | bytes 57376 | tf_op jit(solution)/shard_map/ppermute | solution.py:268
  42.1 0.0 collective-permute-done.1.refs_1_
  42.1 0.0 slice-done.2
  42.1 0.0 slice-done.3
  42.1 1.2 %gate.1 = (f32[2,1792]{1,0:T(2,128)S(1)}, bf16[16,1792]{1,0:T(8,128)(2,1)S(1)}, f32[16,2432]{1,0:T(8,128)S(1)}, bf16[16,2560]{1,0:T(8,128)(2,1)S(1)}) custom-call(s32[1]{0:T(128)} %bitcast.group_ref, bf16[1,1792]{1,0:T(2,128)(2,1)S(1)} %broadcast_in_dim.10.gain_ref, bf16[1792,2304]{1,0:T(8,128)(2,1)S(1)} %bitcast.5, ...), custom_call_target="tpu_custom_call" | custom-call | flops 2000000000 | tf_op jit(solution)/shard_map/gate/pallas_call | solution.py:360
  43.3 1.1 %collective-permute-start.4 = (bf16[16,2560]{1,0:T(8,128)(2,1)S(1)}, bf16[16,2560]{1,0:T(8,128)(2,1)S(1)}, u32[]{:S(2)}, u32[]{:S(2)}) collective-permute-start(bf16[16,2560]{1,0:T(8,128)(2,1)S(1)} %get-tuple-element.21), channel_id=1, source_target_pairs={{0,2},{1,3},{2,0},{3,1},{4,6},{5,7},{6,4},{7,5},{8,10},{9,11},{10,... | collective-permute-start | bytes 245768 | tf_op jit(solution)/shard_map/ppermute | solution.py:280
  44.4 0.0 slice-done
  44.4 0.0 slice-done.1
  44.4 0.0 slice-start.5
  44.5 1.2 %up.1 = (f32[16,2304]{1,0:T(8,128)S(1)}, bf16[16,2304]{1,0:T(8,128)(2,1)S(1)}) custom-call(bf16[16,1792]{1,0:T(8,128)(2,1)S(1)} %get-tuple-element.24.scaled_ref, bf16[1792,2304]{1,0:T(8,128)(2,1)S(1)} %bitcast.3), custom_call_target="tpu_custom_call" | custom-call | flops 2000000000 | tf_op jit(solution)/shard_map/up/pallas_call | solution.py:367
  45.6 0.9 %collective-permute-start.6 = (bf16[16,2304]{1,0:T(8,128)(2,1)S(1)}, bf16[16,2304]{1,0:T(8,128)(2,1)S(1)}, u32[]{:S(2)}, u32[]{:S(2)}) collective-permute-start(bf16[16,2304]{1,0:T(8,128)(2,1)S(1)} %get-tuple-element.26), channel_id=1, source_target_pairs={{0,2},{1,3},{2,0},{3,1},{4,6},{5,7},{6,4},{7,5},{8,10},{9,11},{10,... | collective-permute-start | bytes 221192 | tf_op jit(solution)/shard_map/ppermute | solution.py:280
  46.6 1.5 %collective-permute-done.4.second_ref = bf16[16,2560]{1,0:T(8,128)(2,1)S(1)} collective-permute-done((bf16[16,2560]{1,0:T(8,128)(2,1)S(1)}, bf16[16,2560]{1,0:T(8,128)(2,1)S(1)}, u32[]{:S(2)}, u32[]{:S(2)}) %collective-permute-start.4) | collective-permute-done | bytes 81952 | tf_op jit(solution)/shard_map/ppermute | solution.py:280
  48.1 0.1 merge_gate.1
  48.2 0.0 collective-permute-start.5
  48.2 1.8 %collective-permute-done.6.second_ref = bf16[16,2304]{1,0:T(8,128)(2,1)S(1)} collective-permute-done((bf16[16,2304]{1,0:T(8,128)(2,1)S(1)}, bf16[16,2304]{1,0:T(8,128)(2,1)S(1)}, u32[]{:S(2)}, u32[]{:S(2)}) %collective-permute-start.6) | collective-permute-done | bytes 73760 | tf_op jit(solution)/shard_map/ppermute | solution.py:280
  50.0 0.1 collective-permute-start.7
  50.1 1.3 %collective-permute-done.7.second_up_ref = bf16[16,2304]{1,0:T(8,128)(2,1)S(1)} collective-permute-done((bf16[16,2304]{1,0:T(8,128)(2,1)S(1)}, bf16[16,2304]{1,0:T(8,128)(2,1)S(1)}, u32[]{:S(2)}, u32[]{:S(2)}) %collective-permute-start.7) | collective-permute-done | bytes 73760 | tf_op jit(solution)/shard_map/ppermute | solution.py:280
  51.4 0.0 collective-permute-done.5.second_gate_ref
  51.4 0.0 slice-done.4
  51.4 0.0 slice-done.5
  51.4 1.3 %contract.1 = f32[8,2,1792]{2,1,0:T(2,128)S(1)} custom-call(f32[16,2432]{1,0:T(8,128)S(1)} %get-tuple-element.22.first_gate_ref, bf16[16,2560]{1,0:T(8,128)(2,1)S(1)} %collective-permute-done.5.second_gate_ref, f32[16,2304]{1,0:T(8,128)S(1)} %get-tuple-element.27.first_up_ref, bf16[16,2304]{1,0:T(8,128)(2,1)S(1)} %collective-permute-done.7.second_up_ref, ...), custom_call_target="tpu_custom_call" | custom-call | flops 4000000000 | tf_op jit(solution)/shard_map/contract/pallas_call | solution.py:386
  52.7 9.7 %all_to_all.17 = f32[8,2,1792]{2,1,0:T(2,128)S(1)} all-to-all(f32[8,2,1792]{2,1,0:T(2,128)S(1)} %contract.1), channel_id=1, replica_groups=mesh['wide'=8,'narrow'=4] {'wide'}, dimensions={0} | all-to-all | bytes 229376 | tf_op jit(solution)/shard_map/all_to_all | solution.py:393
  62.4 0.6 add_convert_fusion
  (14 shorter events, 0.1 us)
Async XLA Ops:
  0.0 15.5 %copy-start = (bf16[2,2048,576]{1,2,0:T(8,128)(2,1)S(1)}, bf16[2,2048,576]{1,2,0:T(8,128)(2,1)}, u32[]{:S(2)}) copy-start(bf16[2,2048,576]{1,2,0:T(8,128)(2,1)} %param.18) | copy-start | bytes 14155780
  0.0 15.5 %copy-start.2 = (bf16[16,128,512]{2,1,0:T(8,128)(2,1)S(1)}, bf16[16,128,512]{2,1,0:T(8,128)(2,1)}, u32[]{:S(2)}) copy-start(bf16[16,128,512]{2,1,0:T(8,128)(2,1)} %key_ref.1) | copy-start | bytes 6291460
  0.0 15.5 %copy-start.3 = (bf16[16,512,128]{2,1,0:T(8,128)(2,1)S(1)}, bf16[16,512,128]{2,1,0:T(8,128)(2,1)}, u32[]{:S(2)}) copy-start(bf16[16,512,128]{2,1,0:T(8,128)(2,1)} %value_ref.1) | copy-start | bytes 6291460
  0.0 15.5 %copy-start.5 = (s32[2]{0:T(128)S(1)}, s32[2]{0:T(128)}, u32[]{:S(2)}) copy-start(s32[2]{0:T(128)} %lengths_ref.1) | copy-start | bytes 28
  0.0 15.5 %copy-start.6 = (s32[16]{0:T(128)S(1)}, s32[16]{0:T(128)}, u32[]{:S(2)}) copy-start(s32[16]{0:T(128)} %rows_ref.3) | copy-start | bytes 196
  0.0 42.1 %slice-start.2 = ((s8[8257536]{0:T(1024)(128)(4,1)}), s8[4194304]{0:T(1024)(128)(4,1)S(1)}, s32[]{:S(2)}) async-start(s8[8257536]{0:T(1024)(128)(4,1)} %bitcast.4), calls=%async_computation.5 | async-start | bytes 8388608
  15.5 13.5 %copy-start.1 = (bf16[1024,1792]{1,0:T(8,128)(2,1)S(1)}, bf16[1024,1792]{1,0:T(8,128)(2,1)}, u32[]{:S(2)}) copy-start(bf16[1024,1792]{1,0:T(8,128)(2,1)} %weight_ref.4) | copy-start | bytes 11010052
  15.5 13.4 %copy-start.4 = (bf16[2,1792]{1,0:T(2,128)(2,1)S(1)}, bf16[2,1792]{1,0:T(2,128)(2,1)}, u32[]{:S(2)}) copy-start(bf16[2,1792]{1,0:T(2,128)(2,1)} %residual_ref.1) | copy-start | bytes 21508
  15.5 26.6 %slice-start.3 = ((s8[8257536]{0:T(1024)(128)(4,1)}), s8[4063232]{0:T(1024)(128)(4,1)S(1)}, s32[]{:S(2)}) async-start(s8[8257536]{0:T(1024)(128)(4,1)} %bitcast.4), calls=%async_computation.6 | async-start | bytes 8126464
  18.7 25.8 %slice-start = ((s8[8257536]{0:T(1024)(128)(4,1)}), s8[4194304]{0:T(1024)(128)(4,1)S(1)}, s32[]{:S(2)}) async-start(s8[8257536]{0:T(1024)(128)(4,1)} %bitcast.2), calls=%async_computation.3 | async-start | bytes 8388608
  29.0 10.0 %copy-start.7 = (bf16[1792]{0:T(1024)(128)(2,1)S(1)}, bf16[1792]{0:T(1024)(128)(2,1)}, u32[]{:S(2)}) copy-start(bf16[1792]{0:T(1024)(128)(2,1)} %param.22) | copy-start | bytes 10756
  29.0 15.5 %slice-start.1 = ((s8[8257536]{0:T(1024)(128)(4,1)}), s8[4063232]{0:T(1024)(128)(4,1)S(1)}, s32[]{:S(2)}) async-start(s8[8257536]{0:T(1024)(128)(4,1)} %bitcast.2), calls=%async_computation.4 | async-start | bytes 8126464
  30.2 4.2 %collective-permute-start = (bf16[16,1792]{1,0:T(8,128)(2,1)S(1)}, bf16[16,1792]{1,0:T(8,128)(2,1)S(1)}, u32[]{:S(2)}, u32[]{:S(2)}) collective-permute-start(bf16[16,1792]{1,0:T(8,128)(2,1)S(1)} %get-tuple-element.18), channel_id=1, source_target_pairs={{0,4},{1,5},{2,6},{3,7},{4,0},{5,1},{6,2},{7,3},{8,12},{9,13},{10,... | collective-permute-start | bytes 172040 | tf_op jit(solution)/shard_map/ppermute | solution.py:268
  34.5 6.1 %collective-permute-start.3 = (bf16[16,1792]{1,0:T(8,128)(2,1)S(1)}, bf16[16,1792]{1,0:T(8,128)(2,1)S(1)}, u32[]{:S(2)}, u32[]{:S(2)}) collective-permute-start(bf16[16,1792]{1,0:T(8,128)(2,1)S(1)} %get-tuple-element.29), channel_id=1, source_target_pairs={{0,24},{1,9},{2,26},{3,11},{4,28},{5,13},{6,30},{7,15},{8,16},{9,1... | collective-permute-start | bytes 172040 | tf_op jit(solution)/shard_map/ppermute | solution.py:268
  35.9 6.2 %collective-permute-start.2 = (bf16[16,1792]{1,0:T(8,128)(2,1)S(1)}, bf16[16,1792]{1,0:T(8,128)(2,1)S(1)}, u32[]{:S(2)}, u32[]{:S(2)}) collective-permute-start(bf16[16,1792]{1,0:T(8,128)(2,1)S(1)} %get-tuple-element.29), channel_id=1, source_target_pairs={{0,16},{1,17},{2,18},{3,19},{4,20},{5,21},{6,22},{7,23},{8,24},{9,... | collective-permute-start | bytes 172040 | tf_op jit(solution)/shard_map/ppermute | solution.py:268
  36.7 5.4 %collective-permute-start.1 = (bf16[16,1792]{1,0:T(8,128)(2,1)S(1)}, bf16[16,1792]{1,0:T(8,128)(2,1)S(1)}, u32[]{:S(2)}, u32[]{:S(2)}) collective-permute-start(bf16[16,1792]{1,0:T(8,128)(2,1)S(1)} %get-tuple-element.29), channel_id=1, source_target_pairs={{0,8},{1,25},{2,10},{3,27},{4,12},{5,29},{6,14},{7,31},{8,0},{9,17... | collective-permute-start | bytes 172040 | tf_op jit(solution)/shard_map/ppermute | solution.py:268
  43.3 4.7 %collective-permute-start.4 = (bf16[16,2560]{1,0:T(8,128)(2,1)S(1)}, bf16[16,2560]{1,0:T(8,128)(2,1)S(1)}, u32[]{:S(2)}, u32[]{:S(2)}) collective-permute-start(bf16[16,2560]{1,0:T(8,128)(2,1)S(1)} %get-tuple-element.21), channel_id=1, source_target_pairs={{0,2},{1,3},{2,0},{3,1},{4,6},{5,7},{6,4},{7,5},{8,10},{9,11},{10,... | collective-permute-start | bytes 245768 | tf_op jit(solution)/shard_map/ppermute | solution.py:280
  44.4 6.9 %slice-start.4 = ((s8[8257536]{0:T(1024)(128)(4,1)}), s8[4194304]{0:T(1024)(128)(4,1)S(1)}, s32[]{:S(2)}) async-start(s8[8257536]{0:T(1024)(128)(4,1)} %bitcast.6), calls=%async_computation.7 | async-start | bytes 8388608
  44.4 6.9 %slice-start.5 = ((s8[8257536]{0:T(1024)(128)(4,1)}), s8[4063232]{0:T(1024)(128)(4,1)S(1)}, s32[]{:S(2)}) async-start(s8[8257536]{0:T(1024)(128)(4,1)} %bitcast.6), calls=%async_computation.8 | async-start | bytes 8126464
  45.6 4.4 %collective-permute-start.6 = (bf16[16,2304]{1,0:T(8,128)(2,1)S(1)}, bf16[16,2304]{1,0:T(8,128)(2,1)S(1)}, u32[]{:S(2)}, u32[]{:S(2)}) collective-permute-start(bf16[16,2304]{1,0:T(8,128)(2,1)S(1)} %get-tuple-element.26), channel_id=1, source_target_pairs={{0,2},{1,3},{2,0},{3,1},{4,6},{5,7},{6,4},{7,5},{8,10},{9,11},{10,... | collective-permute-start | bytes 221192 | tf_op jit(solution)/shard_map/ppermute | solution.py:280
  48.2 3.2 %collective-permute-start.5 = (bf16[16,2560]{1,0:T(8,128)(2,1)S(1)}, bf16[16,2560]{1,0:T(8,128)(2,1)S(1)}, u32[]{:S(2)}, u32[]{:S(2)}) collective-permute-start(bf16[16,2560]{1,0:T(8,128)(2,1)S(1)} %get-tuple-element.23), channel_id=1, source_target_pairs={{0,1},{1,0},{2,3},{3,2},{4,5},{5,4},{6,7},{7,6},{8,9},{9,8},{10,11... | collective-permute-start | bytes 245768 | tf_op jit(solution)/shard_map/ppermute | solution.py:280
  50.0 1.3 %collective-permute-start.7 = (bf16[16,2304]{1,0:T(8,128)(2,1)S(1)}, bf16[16,2304]{1,0:T(8,128)(2,1)S(1)}, u32[]{:S(2)}, u32[]{:S(2)}) collective-permute-start(bf16[16,2304]{1,0:T(8,128)(2,1)S(1)} %get-tuple-element.28), channel_id=1, source_target_pairs={{0,1},{1,0},{2,3},{3,2},{4,5},{5,4},{6,7},{7,6},{8,9},{9,8},{10,11... | collective-permute-start | bytes 221192 | tf_op jit(solution)/shard_map/ppermute | solution.py:280

commit v9 on v8

--- a/solution.py
+++ b/solution.py
@@ -41,7 +41,7 @@
         cost_estimate=pl.CostEstimate(flops=flops, transcendentals=0, bytes_accessed=0),
         in_specs=in_specs,
         out_specs=jax.tree.map(lambda _: VMEM, out_shape),
-        compiler_params=pltpu.CompilerParams(vmem_limit_bytes=16 * 1024 * 1024),
+        compiler_params=pltpu.CompilerParams(vmem_limit_bytes=8 * 1024 * 1024),
         name=name,
     )
 
@@ -192,7 +192,31 @@
     return ref[:, start : start + 1].astype(F32) + ref[:, start + 128 : start + 129].astype(F32)
 
 
-def gate_kernel(group_ref, gain_ref, weight_ref, *refs):
+def put_terms(own_ref, out_ref, gate, up, square):
+    columns = gate.shape[1]
+    padded = -(-columns // 128) * 128
+    for side, terms in enumerate((gate, up)):
+        place = slice(side * padded, side * padded + columns)
+        own_ref[:, place] = terms
+        out_ref[:, place] = terms.astype(BF16)
+    if square is not None:
+        own_ref[:, 2 * padded :] = jnp.broadcast_to(square, (gate.shape[0], 128))
+        put_sums(out_ref, 2 * padded, square)
+
+
+def get_terms(columns, own_ref, arrived_ref, with_square):
+    padded = -(-columns // 128) * 128
+    gate, up = (
+        own_ref[:, start : start + columns] + arrived_ref[:, start : start + columns].astype(F32)
+        for start in (0, padded)
+    )
+    square = None
+    if with_square:
+        square = own_ref[:, 2 * padded : 2 * padded + 1] + get_sums(arrived_ref, 2 * padded)
+    return gate, up, square
+
+
+def expand_first_kernel(cut, group_ref, gain_ref, gate_ref, up_ref, *refs):
     parts, (middle_ref, scaled_ref, own_ref, out_ref) = refs[:-4], refs[-4:]
     middle = parts[0][...].astype(F32)
     for part in parts[1:]:
@@ -204,56 +228,51 @@
         middle_ref[slot : slot + 1] = jnp.sum(own, axis=0, keepdims=True)
     scaled = (middle * gain_ref[...].astype(F32)).astype(BF16)
     scaled_ref[...] = scaled
-    put_gate(
+    put_terms(
         own_ref,
         out_ref,
-        jnp.dot(scaled, weight_ref[...], preferred_element_type=F32),
+        jnp.dot(scaled, gate_ref[:, :cut], preferred_element_type=F32),
+        jnp.dot(scaled, up_ref[:, :cut], preferred_element_type=F32),
         jnp.sum(middle * middle, axis=1, keepdims=True),
     )
 
 
-def put_gate(own_ref, out_ref, gate, square):
-    columns, end = gate.shape[1], own_ref.shape[1] - 128
-    own_ref[:, :columns] = gate
-    own_ref[:, end:] = jnp.broadcast_to(square, (gate.shape[0], 128))
-    out_ref[:, :columns] = gate.astype(BF16)
-    put_sums(out_ref, end, square)
-
-
-def up_kernel(scaled_ref, weight_ref, own_ref, out_ref):
-    up = jnp.dot(scaled_ref[...], weight_ref[...], preferred_element_type=F32)
-    own_ref[...] = up
-    out_ref[...] = up.astype(BF16)
-
-
-def merge_kernel(first_ref, second_ref, own_ref, out_ref):
-    total = first_ref[...] + second_ref[...].astype(F32)
-    own_ref[...] = total
-    out_ref[...] = total.astype(BF16)
-
-
-def merge_sums_kernel(columns, first_ref, second_ref, own_ref, out_ref):
-    end = own_ref.shape[1] - 128
-    put_gate(
+def expand_second_kernel(cut, scaled_ref, gate_ref, up_ref, own_ref, out_ref):
+    scaled = scaled_ref[...]
+    put_terms(
         own_ref,
         out_ref,
-        first_ref[:, :columns] + second_ref[:, :columns].astype(F32),
-        first_ref[:, end : end + 1] + get_sums(second_ref, end),
-    )
-
-
-def contract_kernel(
-    first_gate_ref, second_gate_ref, first_up_ref, second_up_ref, weight_ref, out_ref
+        jnp.dot(scaled, gate_ref[:, cut:], preferred_element_type=F32),
+        jnp.dot(scaled, up_ref[:, cut:], preferred_element_type=F32),
+        None,
+    )
+
+
+def merge_kernel(columns, with_square, first_ref, second_ref, own_ref, out_ref):
+    put_terms(own_ref, out_ref, *get_terms(columns, first_ref, second_ref, with_square))
+
+
+def activated(gate, up, factor):
+    gate = gate * factor
+    return (gate / (1.0 + jnp.exp(-gate)) * (up * factor)).astype(BF16)
+
+
+def contract_first_kernel(cut, own_ref, arrived_ref, weight_ref, factor_ref, out_ref):
+    gate, up, square = get_terms(cut, own_ref, arrived_ref, True)
+    factor = lax.rsqrt(square / D + 1e-06)
+    factor_ref[...] = jnp.broadcast_to(factor, factor_ref.shape)
+    out_ref[...] = jnp.dot(
+        activated(gate, up, factor), weight_ref[:cut, :], preferred_element_type=F32
+    )
+
+
+def contract_second_kernel(
+    cut, own_ref, arrived_ref, weight_ref, factor_ref, partial_ref, out_ref
 ):
-    end = first_gate_ref.shape[1] - 128
-    columns = weight_ref.shape[0]
-    square = first_gate_ref[:, end : end + 1] + get_sums(second_gate_ref, end)
-    factor = lax.rsqrt(square / D + 1e-06)
-    gate = first_gate_ref[:, :columns] + second_gate_ref[:, :columns].astype(F32)
-    gate = gate * factor
-    up = (first_up_ref[...] + second_up_ref[...].astype(F32)) * factor
-    hidden = (gate / (1.0 + jnp.exp(-gate)) * up).astype(BF16)
-    total = jnp.dot(hidden, weight_ref[...], preferred_element_type=F32)
+    gate, up, _ = get_terms(weight_ref.shape[0] - cut, own_ref, arrived_ref, False)
+    total = partial_ref[...] + jnp.dot(
+        activated(gate, up, factor_ref[:, :1]), weight_ref[cut:, :], preferred_element_type=F32
+    )
     slots = out_ref.shape[1]
     for owner in range(out_ref.shape[0]):
         out_ref[owner] = total[owner * slots : (owner + 1) * slots]
@@ -354,42 +373,58 @@
                 total = total + other.astype(F32)
             summed = total.astype(BF16)
     columns = gate_weight.shape[1]
-    padded = -(-columns // 128) * 128
-    gate_shapes = (pltpu.VMEM((rows, padded + 128), F32), pltpu.VMEM((rows, padded + 256), BF16))
-    up_shapes = (pltpu.VMEM((rows, columns), F32), pltpu.VMEM((rows, columns), BF16))
-    middle, scaled, gate, gate_sent = call(
-        gate_kernel,
-        (pltpu.VMEM((slots, features), F32), pltpu.VMEM((rows, features), BF16)) + gate_shapes,
-        [SMEM] + [VMEM] * (3 + len(others)),
-        "gate",
+    cut = -(-2 * columns // 768) * 256
+    halves = [(cut, 128, 256), (columns - cut, 0, 0)]
+    shapes = []
+    for size, kept, sent in halves:
+        width = -(-size // 128) * 256
+        shapes.append((pltpu.VMEM((rows, width + kept), F32), pltpu.VMEM((rows, width + sent), BF16)))
+    middle, scaled, own, terms = call(
+        functools.partial(expand_first_kernel, cut),
+        (pltpu.VMEM((slots, features), F32), pltpu.VMEM((rows, features), BF16)) + shapes[0],
+        [SMEM] + [VMEM] * (4 + len(others)),
+        "expand_first",
         flops=EXPAND // 2,
-    )(group[None], norm_gain[None, :], gate_weight, total, *others)
-    up, up_sent = call(up_kernel, up_shapes, [VMEM] * 2, "up", flops=EXPAND // 2)(
-        scaled, up_weight
-    )
+    )(group[None], norm_gain[None, :], gate_weight, up_weight, total, *others)
+    first = (own, terms)
+    second = call(
+        functools.partial(expand_second_kernel, cut),
+        shapes[1],
+        [VMEM] * 3,
+        "expand_second",
+        flops=EXPAND // 2,
+    )(scaled, gate_weight, up_weight)
     distance = narrow // 2
     while distance:
-        other_gate = swap(gate_sent, "narrow", distance, narrow)
-        other_up = swap(up_sent, "narrow", distance, narrow)
+        arrived = [swap(half[1], "narrow", distance, narrow) for half in (first, second)]
         distance //= 2
         if distance:
-            gate, gate_sent = call(
-                functools.partial(merge_sums_kernel, columns),
-                gate_shapes,
-                [VMEM] * 2,
-                "merge_gate",
-                flops=MERGE // 4,
-            )(gate, other_gate)
-            up, up_sent = call(
-                merge_kernel, up_shapes, [VMEM] * 2, "merge_up", flops=MERGE // 4
-            )(up, other_up)
+            first, second = (
+                call(
+                    functools.partial(merge_kernel, size, kept > 0),
+                    shape,
+                    [VMEM] * 2,
+                    "merge",
+                    flops=MERGE // 4,
+                )(half[0], other)
+                for (size, kept, _), shape, half, other in zip(
+                    halves, shapes, (first, second), arrived
+                )
+            )
+    factor, partial = call(
+        functools.partial(contract_first_kernel, cut),
+        (pltpu.VMEM((rows, 128), F32), pltpu.VMEM((rows, features), F32)),
+        [VMEM] * 3,
+        "contract_first",
+        flops=CONTRACT // 4,
+    )(first[0], arrived[0], down_weight)
     down = call(
-        contract_kernel,
+        functools.partial(contract_second_kernel, cut),
         pltpu.VMEM((wide, slots, features), F32),
         [VMEM] * 5,
-        "contract",
+        "contract_second",
         flops=CONTRACT,
-    )(gate, other_gate, up, other_up, down_weight)
+    )(second[0], arrived[1], down_weight, factor, partial)
     total = jnp.sum(lax.all_to_all(down, "wide", 0, 0, tiled=True), axis=0)
     return (middle + total).astype(BF16)
 

time: 63.3 us -> 62.3 us (0.984)
  waiting for transfers between devices: 11.2 us -> 10 us
    ppermute x4, waiting for transfers between devices: 4.57 us -> 3.33 us  [swap(): return lax.ppermute(array, axis, [(i, i ^ distance) for i in range(size)])]
    pallas_call x5 -> x6, Pallas kernels: 3.77 us -> 3.91 us  [the longest x1 1.55 us: shards(): call(functools.partial(expand_first_kernel, cut), (pltpu.VMEM((slots, fea...]
  transfers between devices with their start and end apart: 8 -> 8, of which waited for: 6 -> 6; matrix products, arithmetic and copies ran while one was open for 0% -> 0% of each run, Pallas kernels for 2% -> 3%
where the time goes in v9:
time: 62.3 us; the launch traced here: 62 us
  blocking collectives  34.5 us (55%)
  waiting for transfers between devices  10 us (16%)
  Pallas kernels  9.22 us (15%)
  starting transfers between devices  7.3 us (12%)
  other arithmetic  0.67 us (1%)
    all_to_all x1, blocking collectives, shards(): queries = lax.all_to_all(packed, 'wide', 0, 0, tiled=True)  14.5 us
    all_to_all x1, blocking collectives, shards(): received = lax.all_to_all(heads_out, ('wide', 'narrow'), 0, 0, tiled=True)  10.3 us
    all_to_all x1, blocking collectives, shards(): total = jnp.sum(lax.all_to_all(down, 'wide', 0, 0, tiled=True), axis=0)  9.78 us
    ppermute x4, waiting for transfers between devices, exchange(): return lax.ppermute(array, ('wide', 'narrow'), pairs)  6.67 us
    ppermute x4, starting transfers between devices, exchange(): return lax.ppermute(array, ('wide', 'narrow'), pairs)  5.18 us
    ppermute x4, waiting for transfers between devices, swap(): return lax.ppermute(array, axis, [(i, i ^ distance) for i in range(size)])  3.33 us
    pallas_call x1, Pallas kernels, shards(): call(functools.partial(attend_kernel, narrow, blocks, scale), pltpu.VMEM(...  3.11 us
    ppermute x4, starting transfers between devices, swap(): return lax.ppermute(array, axis, [(i, i ^ distance) for i in range(size)])  2.12 us
  transfers between devices with their start and end apart: 8, of which 6 were waited for; matrix products, arithmetic and copies ran while one was open for 0% of the time, Pallas kernels for 3%

profile of v9, /device:TPU:0, one launch (start us, length us, event | category | flops | bytes accessed | tf_op | source)
XLA Modules:
  0.0 62.0 jit_solution(2544536939821055364)
XLA Ops:
  0.0 0.0 copy-start
  0.0 1.0 %pack.1 = bf16[8,2,24,128]{3,2,1,0:T(8,128)(2,1)S(1)} custom-call(s32[1]{0:T(128)} %bitcast.group_ref, bf16[2,16,128]{2,1,0:T(8,128)(2,1)} %nope_hbm.1, bf16[2,16,64]{2,1,0:T(8,128)(2,1)} %rope_hbm.1), custom_call_target="tpu_custom_call" | custom-call | flops 10000000000 | tf_op jit(solution)/shard_map/pack/pallas_call | solution.py:328
  1.0 14.5 %all_to_all.15.query_ref = bf16[8,2,24,128]{3,2,1,0:T(8,128)(2,1)S(1)} all-to-all(bf16[8,2,24,128]{3,2,1,0:T(8,128)(2,1)S(1)} %pack.1), channel_id=1, replica_groups=mesh['wide'=8,'narrow'=4] {'wide'}, dimensions={0} | all-to-all | bytes 196608 | tf_op jit(solution)/shard_map/all_to_all | solution.py:340
  15.5 0.0 copy-done
  15.5 0.0 copy-done.2
  15.5 0.0 copy-done.3
  15.5 0.0 copy-done.5
  15.5 0.0 copy-done.6
  15.5 0.0 copy-start.1
  15.5 0.0 copy-start.4
  15.5 3.1 %attend.1 = bf16[32,16,128]{2,1,0:T(8,128)(2,1)S(1)} custom-call(s32[1]{0:T(128)} %bitcast.group_ref, s32[16]{0:T(128)S(1)} %copy-done.6, s32[2]{0:T(128)S(1)} %copy-done.5, bf16[8,2,24,128]{3,2,1,0:T(8,128)(2,1)S(1)} %all_to_all.15.query_ref, bf16[16,128,512]{2,1,0:T(8,128)(2,1)S(1)} %copy-done.2, bf16[2,576,2048]{2,1,0:T(8,128)(2,1)S(1)} %bitcast.8, ...), custom_call_target="tpu_custom_call" | custom-call | flops 15000000512 | tf_op jit(solution)/shard_map/attend/pallas_call | solution.py:342
  18.6 0.0 slice-start
  18.6 0.0 slice-start.2
  18.7 10.3 %all_to_all.16.heads_ref = bf16[32,16,128]{2,1,0:T(8,128)(2,1)S(1)} all-to-all(bf16[32,16,128]{2,1,0:T(8,128)(2,1)S(1)} %attend.1), channel_id=1, replica_groups=mesh['wide'=8,'narrow'=4] {'wide','narrow'}, dimensions={0} | all-to-all | bytes 262144 | tf_op jit(solution)/shard_map/all_to_all | solution.py:357
  28.9 0.0 copy-done.1
  28.9 0.0 copy-done.4
  29.0 0.0 slice-start.3
  29.0 1.2 %project.1 = (f32[16,1792]{1,0:T(8,128)S(1)}, bf16[16,1792]{1,0:T(8,128)(2,1)S(1)}) custom-call(s32[16]{0:T(128)S(1)} %copy-done.6, s32[1]{0:T(128)} %bitcast.group_ref, bf16[32,16,128]{2,1,0:T(8,128)(2,1)S(1)} %all_to_all.16.heads_ref, bf16[2,1792]{1,0:T(2,128)(2,1)S(1)} %copy-done.4, bf16[1024,1792]{1,0:T(8,128)(2,1)S(1)} %copy-done.1), custom_call_target="tpu_custom_call" | custom-call | flops 12000000000 | tf_op jit(solution)/shard_map/project/pallas_call | solution.py:358
  30.2 0.7 %collective-permute-start = (bf16[16,1792]{1,0:T(8,128)(2,1)S(1)}, bf16[16,1792]{1,0:T(8,128)(2,1)S(1)}, u32[]{:S(2)}, u32[]{:S(2)}) collective-permute-start(bf16[16,1792]{1,0:T(8,128)(2,1)S(1)} %get-tuple-element.20), channel_id=1, source_target_pairs={{0,4},{1,5},{2,6},{3,7},{4,0},{5,1},{6,2},{7,3},{8,12},{9,13},{10,... | collective-permute-start | bytes 172040 | tf_op jit(solution)/shard_map/ppermute | solution.py:287
  30.9 3.5 %collective-permute-done = bf16[16,1792]{1,0:T(8,128)(2,1)S(1)} collective-permute-done((bf16[16,1792]{1,0:T(8,128)(2,1)S(1)}, bf16[16,1792]{1,0:T(8,128)(2,1)S(1)}, u32[]{:S(2)}, u32[]{:S(2)}) %collective-permute-start) | collective-permute-done | bytes 57376 | tf_op jit(solution)/shard_map/ppermute | solution.py:287
  34.5 1.4 %collective-permute-start.3 = (bf16[16,1792]{1,0:T(8,128)(2,1)S(1)}, bf16[16,1792]{1,0:T(8,128)(2,1)S(1)}, u32[]{:S(2)}, u32[]{:S(2)}) collective-permute-start(bf16[16,1792]{1,0:T(8,128)(2,1)S(1)} %get-tuple-element.33), channel_id=1, source_target_pairs={{0,24},{1,9},{2,26},{3,11},{4,28},{5,13},{6,30},{7,15},{8,16},{9,1... | collective-permute-start | bytes 172040 | tf_op jit(solution)/shard_map/ppermute | solution.py:287
  35.9 0.8 %collective-permute-start.2 = (bf16[16,1792]{1,0:T(8,128)(2,1)S(1)}, bf16[16,1792]{1,0:T(8,128)(2,1)S(1)}, u32[]{:S(2)}, u32[]{:S(2)}) collective-permute-start(bf16[16,1792]{1,0:T(8,128)(2,1)S(1)} %get-tuple-element.33), channel_id=1, source_target_pairs={{0,16},{1,17},{2,18},{3,19},{4,20},{5,21},{6,22},{7,23},{8,24},{9,... | collective-permute-start | bytes 172040 | tf_op jit(solution)/shard_map/ppermute | solution.py:287
  36.7 2.3 %collective-permute-start.1 = (bf16[16,1792]{1,0:T(8,128)(2,1)S(1)}, bf16[16,1792]{1,0:T(8,128)(2,1)S(1)}, u32[]{:S(2)}, u32[]{:S(2)}) collective-permute-start(bf16[16,1792]{1,0:T(8,128)(2,1)S(1)} %get-tuple-element.33), channel_id=1, source_target_pairs={{0,8},{1,25},{2,10},{3,27},{4,12},{5,29},{6,14},{7,31},{8,0},{9,17... | collective-permute-start | bytes 172040 | tf_op jit(solution)/shard_map/ppermute | solution.py:287
  38.9 0.0 copy-done.7
  39.0 1.6 %collective-permute-done.3.refs_3_ = bf16[16,1792]{1,0:T(8,128)(2,1)S(1)} collective-permute-done((bf16[16,1792]{1,0:T(8,128)(2,1)S(1)}, bf16[16,1792]{1,0:T(8,128)(2,1)S(1)}, u32[]{:S(2)}, u32[]{:S(2)}) %collective-permute-start.3) | collective-permute-done | bytes 57376 | tf_op jit(solution)/shard_map/ppermute | solution.py:287
  40.6 1.5 %collective-permute-done.2.refs_2_ = bf16[16,1792]{1,0:T(8,128)(2,1)S(1)} collective-permute-done((bf16[16,1792]{1,0:T(8,128)(2,1)S(1)}, bf16[16,1792]{1,0:T(8,128)(2,1)S(1)}, u32[]{:S(2)}, u32[]{:S(2)}) %collective-permute-start.2) | collective-permute-done | bytes 57376 | tf_op jit(solution)/shard_map/ppermute | solution.py:287
  42.1 0.0 collective-permute-done.1.refs_1_
  42.1 0.0 slice-done
  42.1 0.0 slice-done.2
  42.1 0.0 slice-done.1
  42.1 0.0 slice-done.3
  42.2 1.5 %expand_first.1 = (f32[2,1792]{1,0:T(2,128)S(1)}, bf16[16,1792]{1,0:T(8,128)(2,1)S(1)}, f32[16,3200]{1,0:T(8,128)S(1)}, bf16[16,3328]{1,0:T(8,128)(2,1)S(1)}) custom-call(s32[1]{0:T(128)} %bitcast.group_ref, bf16[1,1792]{1,0:T(2,128)(2,1)S(1)} %broadcast_in_dim.10.gain_ref, bf16[1792,2304]{1,0:T(8,128)(2,1)S(1)} %bitcast.3, bf16[1792,2304]{1,0:T(8,128)(2,1)S(1)} %bitcast.5, ...), custom_call_target="tpu_custom_call" | custom-call | flops 2000000000 | tf_op jit(solution)/shard_map/expand_first/pallas_call | solution.py:382
  43.7 1.1 %collective-permute-start.6 = (bf16[16,3328]{1,0:T(8,128)(2,1)S(1)}, bf16[16,3328]{1,0:T(8,128)(2,1)S(1)}, u32[]{:S(2)}, u32[]{:S(2)}) collective-permute-start(bf16[16,3328]{1,0:T(8,128)(2,1)S(1)} %get-tuple-element.28), channel_id=1, source_target_pairs={{0,2},{1,3},{2,0},{3,1},{4,6},{5,7},{6,4},{7,5},{8,10},{9,11},{10,... | collective-permute-start | bytes 319496 | tf_op jit(solution)/shard_map/ppermute | solution.py:299
  44.8 0.8 %expand_second.1 = (f32[16,1536]{1,0:T(8,128)S(1)}, bf16[16,1536]{1,0:T(8,128)(2,1)S(1)}) custom-call(bf16[16,1792]{1,0:T(8,128)(2,1)S(1)} %get-tuple-element.22.scaled_ref, bf16[1792,2304]{1,0:T(8,128)(2,1)S(1)} %bitcast.3, bf16[1792,2304]{1,0:T(8,128)(2,1)S(1)} %bitcast.5), custom_call_target="tpu_custom_call" | custom-call | flops 2000000000 | tf_op jit(solution)/shard_map/expand_second/pallas_call | solution.py:390
  45.6 0.9 %collective-permute-start.4 = (bf16[16,1536]{1,0:T(8,128)(2,1)S(1)}, bf16[16,1536]{1,0:T(8,128)(2,1)S(1)}, u32[]{:S(2)}, u32[]{:S(2)}) collective-permute-start(bf16[16,1536]{1,0:T(8,128)(2,1)S(1)} %get-tuple-element.24), channel_id=1, source_target_pairs={{0,2},{1,3},{2,0},{3,1},{4,6},{5,7},{6,4},{7,5},{8,10},{9,11},{10,... | collective-permute-start | bytes 147464 | tf_op jit(solution)/shard_map/ppermute | solution.py:299
  46.6 1.8 %collective-permute-done.6.second_ref = bf16[16,3328]{1,0:T(8,128)(2,1)S(1)} collective-permute-done((bf16[16,3328]{1,0:T(8,128)(2,1)S(1)}, bf16[16,3328]{1,0:T(8,128)(2,1)S(1)}, u32[]{:S(2)}, u32[]{:S(2)}) %collective-permute-start.6) | collective-permute-done | bytes 106528 | tf_op jit(solution)/shard_map/ppermute | solution.py:299
  48.4 0.1 merge.3
  48.5 0.0 collective-permute-start.7
  48.5 1.2 %collective-permute-done.4.second_ref = bf16[16,1536]{1,0:T(8,128)(2,1)S(1)} collective-permute-done((bf16[16,1536]{1,0:T(8,128)(2,1)S(1)}, bf16[16,1536]{1,0:T(8,128)(2,1)S(1)}, u32[]{:S(2)}, u32[]{:S(2)}) %collective-permute-start.4) | collective-permute-done | bytes 49184 | tf_op jit(solution)/shard_map/ppermute | solution.py:299
  49.7 0.1 collective-permute-start.5
  49.8 0.0 collective-permute-done.7.arrived_ref
  49.8 0.0 slice-done.4
  49.8 0.0 slice-done.5
  49.9 0.9 %contract_first.1 = (f32[16,128]{1,0:T(8,128)S(1)}, f32[16,1792]{1,0:T(8,128)S(1)}) custom-call(f32[16,3200]{1,0:T(8,128)S(1)} %get-tuple-element.29.own_ref, bf16[16,3328]{1,0:T(8,128)(2,1)S(1)} %collective-permute-done.7.arrived_ref, bf16[2304,1792]{1,0:T(8,128)(2,1)S(1)} %bitcast.7), custom_call_target="tpu_custom_call" | custom-call | flops 1000000000 | tf_op jit(solution)/shard_map/contract_first/pallas_call | solution.py:414
  50.8 0.3 collective-permute-done.5.arrived_ref
  51.0 0.5 contract_second.1
  51.6 9.8 %all_to_all.17 = f32[8,2,1792]{2,1,0:T(2,128)S(1)} all-to-all(f32[8,2,1792]{2,1,0:T(2,128)S(1)} %contract_second.1), channel_id=1, replica_groups=mesh['wide'=8,'narrow'=4] {'wide'}, dimensions={0} | all-to-all | bytes 229376 | tf_op jit(solution)/shard_map/all_to_all | solution.py:428
  61.4 0.6 add_convert_fusion
  (15 shorter events, 0.1 us)
Async XLA Ops:
  0.0 15.5 %copy-start = (bf16[2,2048,576]{1,2,0:T(8,128)(2,1)S(1)}, bf16[2,2048,576]{1,2,0:T(8,128)(2,1)}, u32[]{:S(2)}) copy-start(bf16[2,2048,576]{1,2,0:T(8,128)(2,1)} %param.18) | copy-start | bytes 14155780
  0.0 15.5 %copy-start.2 = (bf16[16,128,512]{2,1,0:T(8,128)(2,1)S(1)}, bf16[16,128,512]{2,1,0:T(8,128)(2,1)}, u32[]{:S(2)}) copy-start(bf16[16,128,512]{2,1,0:T(8,128)(2,1)} %key_ref.1) | copy-start | bytes 6291460
  0.0 15.5 %copy-start.3 = (bf16[16,512,128]{2,1,0:T(8,128)(2,1)S(1)}, bf16[16,512,128]{2,1,0:T(8,128)(2,1)}, u32[]{:S(2)}) copy-start(bf16[16,512,128]{2,1,0:T(8,128)(2,1)} %value_ref.1) | copy-start | bytes 6291460
  0.0 15.5 %copy-start.5 = (s32[2]{0:T(128)S(1)}, s32[2]{0:T(128)}, u32[]{:S(2)}) copy-start(s32[2]{0:T(128)} %lengths_ref.1) | copy-start | bytes 28
  0.0 15.5 %copy-start.6 = (s32[16]{0:T(128)S(1)}, s32[16]{0:T(128)}, u32[]{:S(2)}) copy-start(s32[16]{0:T(128)} %rows_ref.3) | copy-start | bytes 196
  15.5 13.5 %copy-start.1 = (bf16[1024,1792]{1,0:T(8,128)(2,1)S(1)}, bf16[1024,1792]{1,0:T(8,128)(2,1)}, u32[]{:S(2)}) copy-start(bf16[1024,1792]{1,0:T(8,128)(2,1)} %weight_ref.3) | copy-start | bytes 11010052
  15.5 13.4 %copy-start.4 = (bf16[2,1792]{1,0:T(2,128)(2,1)S(1)}, bf16[2,1792]{1,0:T(2,128)(2,1)}, u32[]{:S(2)}) copy-start(bf16[2,1792]{1,0:T(2,128)(2,1)} %residual_ref.1) | copy-start | bytes 21508
  18.6 23.5 %slice-start = ((s8[8257536]{0:T(1024)(128)(4,1)}), s8[4194304]{0:T(1024)(128)(4,1)S(1)}, s32[]{:S(2)}) async-start(s8[8257536]{0:T(1024)(128)(4,1)} %bitcast.2), calls=%async_computation.3 | async-start | bytes 8388608
  18.6 23.5 %slice-start.2 = ((s8[8257536]{0:T(1024)(128)(4,1)}), s8[4194304]{0:T(1024)(128)(4,1)S(1)}, s32[]{:S(2)}) async-start(s8[8257536]{0:T(1024)(128)(4,1)} %bitcast.4), calls=%async_computation.5 | async-start | bytes 8388608
  28.9 10.0 %copy-start.7 = (bf16[1792]{0:T(1024)(128)(2,1)S(1)}, bf16[1792]{0:T(1024)(128)(2,1)}, u32[]{:S(2)}) copy-start(bf16[1792]{0:T(1024)(128)(2,1)} %param.22) | copy-start | bytes 10756
  28.9 13.2 %slice-start.1 = ((s8[8257536]{0:T(1024)(128)(4,1)}), s8[4063232]{0:T(1024)(128)(4,1)S(1)}, s32[]{:S(2)}) async-start(s8[8257536]{0:T(1024)(128)(4,1)} %bitcast.2), calls=%async_computation.4 | async-start | bytes 8126464
  29.0 13.2 %slice-start.3 = ((s8[8257536]{0:T(1024)(128)(4,1)}), s8[4063232]{0:T(1024)(128)(4,1)S(1)}, s32[]{:S(2)}) async-start(s8[8257536]{0:T(1024)(128)(4,1)} %bitcast.4), calls=%async_computation.6 | async-start | bytes 8126464
  30.2 4.2 %collective-permute-start = (bf16[16,1792]{1,0:T(8,128)(2,1)S(1)}, bf16[16,1792]{1,0:T(8,128)(2,1)S(1)}, u32[]{:S(2)}, u32[]{:S(2)}) collective-permute-start(bf16[16,1792]{1,0:T(8,128)(2,1)S(1)} %get-tuple-element.20), channel_id=1, source_target_pairs={{0,4},{1,5},{2,6},{3,7},{4,0},{5,1},{6,2},{7,3},{8,12},{9,13},{10,... | collective-permute-start | bytes 172040 | tf_op jit(solution)/shard_map/ppermute | solution.py:287
  34.5 6.1 %collective-permute-start.3 = (bf16[16,1792]{1,0:T(8,128)(2,1)S(1)}, bf16[16,1792]{1,0:T(8,128)(2,1)S(1)}, u32[]{:S(2)}, u32[]{:S(2)}) collective-permute-start(bf16[16,1792]{1,0:T(8,128)(2,1)S(1)} %get-tuple-element.33), channel_id=1, source_target_pairs={{0,24},{1,9},{2,26},{3,11},{4,28},{5,13},{6,30},{7,15},{8,16},{9,1... | collective-permute-start | bytes 172040 | tf_op jit(solution)/shard_map/ppermute | solution.py:287
  35.9 6.2 %collective-permute-start.2 = (bf16[16,1792]{1,0:T(8,128)(2,1)S(1)}, bf16[16,1792]{1,0:T(8,128)(2,1)S(1)}, u32[]{:S(2)}, u32[]{:S(2)}) collective-permute-start(bf16[16,1792]{1,0:T(8,128)(2,1)S(1)} %get-tuple-element.33), channel_id=1, source_target_pairs={{0,16},{1,17},{2,18},{3,19},{4,20},{5,21},{6,22},{7,23},{8,24},{9,... | collective-permute-start | bytes 172040 | tf_op jit(solution)/shard_map/ppermute | solution.py:287
  36.7 5.4 %collective-permute-start.1 = (bf16[16,1792]{1,0:T(8,128)(2,1)S(1)}, bf16[16,1792]{1,0:T(8,128)(2,1)S(1)}, u32[]{:S(2)}, u32[]{:S(2)}) collective-permute-start(bf16[16,1792]{1,0:T(8,128)(2,1)S(1)} %get-tuple-element.33), channel_id=1, source_target_pairs={{0,8},{1,25},{2,10},{3,27},{4,12},{5,29},{6,14},{7,31},{8,0},{9,17... | collective-permute-start | bytes 172040 | tf_op jit(solution)/shard_map/ppermute | solution.py:287
  43.7 4.7 %collective-permute-start.6 = (bf16[16,3328]{1,0:T(8,128)(2,1)S(1)}, bf16[16,3328]{1,0:T(8,128)(2,1)S(1)}, u32[]{:S(2)}, u32[]{:S(2)}) collective-permute-start(bf16[16,3328]{1,0:T(8,128)(2,1)S(1)} %get-tuple-element.28), channel_id=1, source_target_pairs={{0,2},{1,3},{2,0},{3,1},{4,6},{5,7},{6,4},{7,5},{8,10},{9,11},{10,... | collective-permute-start | bytes 319496 | tf_op jit(solution)/shard_map/ppermute | solution.py:299
  44.8 5.0 %slice-start.4 = ((s8[8257536]{0:T(1024)(128)(4,1)}), s8[4194304]{0:T(1024)(128)(4,1)S(1)}, s32[]{:S(2)}) async-start(s8[8257536]{0:T(1024)(128)(4,1)} %bitcast.6), calls=%async_computation.7 | async-start | bytes 8388608
  44.8 5.0 %slice-start.5 = ((s8[8257536]{0:T(1024)(128)(4,1)}), s8[4063232]{0:T(1024)(128)(4,1)S(1)}, s32[]{:S(2)}) async-start(s8[8257536]{0:T(1024)(128)(4,1)} %bitcast.6), calls=%async_computation.8 | async-start | bytes 8126464
  45.6 4.1 %collective-permute-start.4 = (bf16[16,1536]{1,0:T(8,128)(2,1)S(1)}, bf16[16,1536]{1,0:T(8,128)(2,1)S(1)}, u32[]{:S(2)}, u32[]{:S(2)}) collective-permute-start(bf16[16,1536]{1,0:T(8,128)(2,1)S(1)} %get-tuple-element.24), channel_id=1, source_target_pairs={{0,2},{1,3},{2,0},{3,1},{4,6},{5,7},{6,4},{7,5},{8,10},{9,11},{10,... | collective-permute-start | bytes 147464 | tf_op jit(solution)/shard_map/ppermute | solution.py:299
  48.5 1.3 %collective-permute-start.7 = (bf16[16,3328]{1,0:T(8,128)(2,1)S(1)}, bf16[16,3328]{1,0:T(8,128)(2,1)S(1)}, u32[]{:S(2)}, u32[]{:S(2)}) collective-permute-start(bf16[16,3328]{1,0:T(8,128)(2,1)S(1)} %get-tuple-element.30), channel_id=1, source_target_pairs={{0,1},{1,0},{2,3},{3,2},{4,5},{5,4},{6,7},{7,6},{8,9},{9,8},{10,11... | collective-permute-start | bytes 319496 | tf_op jit(solution)/shard_map/ppermute | solution.py:299
  49.7 1.3 %collective-permute-start.5 = (bf16[16,1536]{1,0:T(8,128)(2,1)S(1)}, bf16[16,1536]{1,0:T(8,128)(2,1)S(1)}, u32[]{:S(2)}, u32[]{:S(2)}) collective-permute-start(bf16[16,1536]{1,0:T(8,128)(2,1)S(1)} %get-tuple-element.26), channel_id=1, source_target_pairs={{0,1},{1,0},{2,3},{3,2},{4,5},{5,4},{6,7},{7,6},{8,9},{9,8},{10,11... | collective-permute-start | bytes 147464 | tf_op jit(solution)/shard_map/ppermute | solution.py:299

commit v10 on v9

--- a/solution.py
+++ b/solution.py
@@ -275,7 +275,7 @@
     )
     slots = out_ref.shape[1]
     for owner in range(out_ref.shape[0]):
-        out_ref[owner] = total[owner * slots : (owner + 1) * slots]
+        out_ref[owner] = total[owner * slots : (owner + 1) * slots].astype(out_ref.dtype)
 
 
 def exchange(array, first, second, wide, narrow):
@@ -420,12 +420,12 @@
     )(first[0], arrived[0], down_weight)
     down = call(
         functools.partial(contract_second_kernel, cut),
-        pltpu.VMEM((wide, slots, features), F32),
+        pltpu.VMEM((wide, slots, features), BF16),
         [VMEM] * 5,
         "contract_second",
         flops=CONTRACT,
     )(second[0], arrived[1], down_weight, factor, partial)
-    total = jnp.sum(lax.all_to_all(down, "wide", 0, 0, tiled=True), axis=0)
+    total = jnp.sum(lax.all_to_all(down, "wide", 0, 0, tiled=True).astype(F32), axis=0)
     return (middle + total).astype(BF16)
 
 

time: 62.3 us -> 61.8 us (level)
  no operation moved by 1% of the time
where the time goes in v10:
time: 61.8 us; the launch traced here: 61.6 us
  blocking collectives  34.1 us (55%)
  waiting for transfers between devices  10 us (16%)
  Pallas kernels  9.22 us (15%)
  starting transfers between devices  7.3 us (12%)
  other arithmetic  0.68 us (1%)
    all_to_all x1, blocking collectives, shards(): queries = lax.all_to_all(packed, 'wide', 0, 0, tiled=True)  14.5 us
    all_to_all x1, blocking collectives, shards(): received = lax.all_to_all(heads_out, ('wide', 'narrow'), 0, 0, tiled=True)  10.3 us
    all_to_all x1, blocking collectives, shards(): lax.all_to_all(down, 'wide', 0, 0, tiled=True).astype(F32)  9.32 us
    ppermute x4, waiting for transfers between devices, exchange(): return lax.ppermute(array, ('wide', 'narrow'), pairs)  6.67 us
    ppermute x4, starting transfers between devices, exchange(): return lax.ppermute(array, ('wide', 'narrow'), pairs)  5.18 us
    ppermute x4, waiting for transfers between devices, swap(): return lax.ppermute(array, axis, [(i, i ^ distance) for i in range(size)])  3.33 us
    pallas_call x1, Pallas kernels, shards(): call(functools.partial(attend_kernel, narrow, blocks, scale), pltpu.VMEM(...  3.11 us
    ppermute x4, starting transfers between devices, swap(): return lax.ppermute(array, axis, [(i, i ^ distance) for i in range(size)])  2.12 us
  transfers between devices with their start and end apart: 8, of which 6 were waited for; matrix products, arithmetic and copies ran while one was open for 0% of the time, Pallas kernels for 3%

profile of v10, /device:TPU:0, one launch (start us, length us, event | category | flops | bytes accessed | tf_op | source)
XLA Modules:
  0.0 61.6 jit_solution(15586193110685389105)
XLA Ops:
  0.0 1.0 %pack.1 = bf16[8,2,24,128]{3,2,1,0:T(8,128)(2,1)S(1)} custom-call(s32[1]{0:T(128)} %bitcast.group_ref, bf16[2,16,128]{2,1,0:T(8,128)(2,1)} %nope_hbm.1, bf16[2,16,64]{2,1,0:T(8,128)(2,1)} %rope_hbm.1), custom_call_target="tpu_custom_call" | custom-call | flops 10000000000 | tf_op jit(solution)/shard_map/pack/pallas_call | solution.py:328
  1.0 14.5 %all_to_all.15.query_ref = bf16[8,2,24,128]{3,2,1,0:T(8,128)(2,1)S(1)} all-to-all(bf16[8,2,24,128]{3,2,1,0:T(8,128)(2,1)S(1)} %pack.1), channel_id=1, replica_groups=mesh['wide'=8,'narrow'=4] {'wide'}, dimensions={0} | all-to-all | bytes 196608 | tf_op jit(solution)/shard_map/all_to_all | solution.py:340
  15.5 0.0 copy-done
  15.5 0.0 copy-done.2
  15.5 0.0 copy-done.3
  15.5 0.0 copy-done.5
  15.5 0.0 copy-done.6
  15.5 0.0 copy-start.1
  15.5 0.0 copy-start.4
  15.5 3.1 %attend.1 = bf16[32,16,128]{2,1,0:T(8,128)(2,1)S(1)} custom-call(s32[1]{0:T(128)} %bitcast.group_ref, s32[16]{0:T(128)S(1)} %copy-done.6, s32[2]{0:T(128)S(1)} %copy-done.5, bf16[8,2,24,128]{3,2,1,0:T(8,128)(2,1)S(1)} %all_to_all.15.query_ref, bf16[16,128,512]{2,1,0:T(8,128)(2,1)S(1)} %copy-done.2, bf16[2,576,2048]{2,1,0:T(8,128)(2,1)S(1)} %bitcast.8, ...), custom_call_target="tpu_custom_call" | custom-call | flops 15000000512 | tf_op jit(solution)/shard_map/attend/pallas_call | solution.py:342
  18.6 0.0 slice-start
  18.6 0.0 slice-start.2
  18.7 10.3 %all_to_all.16.heads_ref = bf16[32,16,128]{2,1,0:T(8,128)(2,1)S(1)} all-to-all(bf16[32,16,128]{2,1,0:T(8,128)(2,1)S(1)} %attend.1), channel_id=1, replica_groups=mesh['wide'=8,'narrow'=4] {'wide','narrow'}, dimensions={0} | all-to-all | bytes 262144 | tf_op jit(solution)/shard_map/all_to_all | solution.py:357
  28.9 0.0 copy-done.1
  28.9 0.0 copy-done.4
  29.0 0.0 slice-start.3
  29.0 1.2 %project.1 = (f32[16,1792]{1,0:T(8,128)S(1)}, bf16[16,1792]{1,0:T(8,128)(2,1)S(1)}) custom-call(s32[16]{0:T(128)S(1)} %copy-done.6, s32[1]{0:T(128)} %bitcast.group_ref, bf16[32,16,128]{2,1,0:T(8,128)(2,1)S(1)} %all_to_all.16.heads_ref, bf16[2,1792]{1,0:T(2,128)(2,1)S(1)} %copy-done.4, bf16[1024,1792]{1,0:T(8,128)(2,1)S(1)} %copy-done.1), custom_call_target="tpu_custom_call" | custom-call | flops 12000000000 | tf_op jit(solution)/shard_map/project/pallas_call | solution.py:358
  30.2 0.7 %collective-permute-start = (bf16[16,1792]{1,0:T(8,128)(2,1)S(1)}, bf16[16,1792]{1,0:T(8,128)(2,1)S(1)}, u32[]{:S(2)}, u32[]{:S(2)}) collective-permute-start(bf16[16,1792]{1,0:T(8,128)(2,1)S(1)} %get-tuple-element.20), channel_id=1, source_target_pairs={{0,4},{1,5},{2,6},{3,7},{4,0},{5,1},{6,2},{7,3},{8,12},{9,13},{10,... | collective-permute-start | bytes 172040 | tf_op jit(solution)/shard_map/ppermute | solution.py:287
  31.0 3.5 %collective-permute-done = bf16[16,1792]{1,0:T(8,128)(2,1)S(1)} collective-permute-done((bf16[16,1792]{1,0:T(8,128)(2,1)S(1)}, bf16[16,1792]{1,0:T(8,128)(2,1)S(1)}, u32[]{:S(2)}, u32[]{:S(2)}) %collective-permute-start) | collective-permute-done | bytes 57376 | tf_op jit(solution)/shard_map/ppermute | solution.py:287
  34.5 1.4 %collective-permute-start.3 = (bf16[16,1792]{1,0:T(8,128)(2,1)S(1)}, bf16[16,1792]{1,0:T(8,128)(2,1)S(1)}, u32[]{:S(2)}, u32[]{:S(2)}) collective-permute-start(bf16[16,1792]{1,0:T(8,128)(2,1)S(1)} %get-tuple-element.33), channel_id=1, source_target_pairs={{0,24},{1,9},{2,26},{3,11},{4,28},{5,13},{6,30},{7,15},{8,16},{9,1... | collective-permute-start | bytes 172040 | tf_op jit(solution)/shard_map/ppermute | solution.py:287
  35.9 0.8 %collective-permute-start.2 = (bf16[16,1792]{1,0:T(8,128)(2,1)S(1)}, bf16[16,1792]{1,0:T(8,128)(2,1)S(1)}, u32[]{:S(2)}, u32[]{:S(2)}) collective-permute-start(bf16[16,1792]{1,0:T(8,128)(2,1)S(1)} %get-tuple-element.33), channel_id=1, source_target_pairs={{0,16},{1,17},{2,18},{3,19},{4,20},{5,21},{6,22},{7,23},{8,24},{9,... | collective-permute-start | bytes 172040 | tf_op jit(solution)/shard_map/ppermute | solution.py:287
  36.7 2.3 %collective-permute-start.1 = (bf16[16,1792]{1,0:T(8,128)(2,1)S(1)}, bf16[16,1792]{1,0:T(8,128)(2,1)S(1)}, u32[]{:S(2)}, u32[]{:S(2)}) collective-permute-start(bf16[16,1792]{1,0:T(8,128)(2,1)S(1)} %get-tuple-element.33), channel_id=1, source_target_pairs={{0,8},{1,25},{2,10},{3,27},{4,12},{5,29},{6,14},{7,31},{8,0},{9,17... | collective-permute-start | bytes 172040 | tf_op jit(solution)/shard_map/ppermute | solution.py:287
  38.9 0.0 copy-done.7
  39.0 1.6 %collective-permute-done.3.refs_3_ = bf16[16,1792]{1,0:T(8,128)(2,1)S(1)} collective-permute-done((bf16[16,1792]{1,0:T(8,128)(2,1)S(1)}, bf16[16,1792]{1,0:T(8,128)(2,1)S(1)}, u32[]{:S(2)}, u32[]{:S(2)}) %collective-permute-start.3) | collective-permute-done | bytes 57376 | tf_op jit(solution)/shard_map/ppermute | solution.py:287
  40.6 1.5 %collective-permute-done.2.refs_2_ = bf16[16,1792]{1,0:T(8,128)(2,1)S(1)} collective-permute-done((bf16[16,1792]{1,0:T(8,128)(2,1)S(1)}, bf16[16,1792]{1,0:T(8,128)(2,1)S(1)}, u32[]{:S(2)}, u32[]{:S(2)}) %collective-permute-start.2) | collective-permute-done | bytes 57376 | tf_op jit(solution)/shard_map/ppermute | solution.py:287
  42.1 0.0 collective-permute-done.1.refs_1_
  42.1 0.0 slice-done
  42.1 0.0 slice-done.2
  42.1 0.0 slice-done.1
  42.1 0.0 slice-done.3
  42.2 1.5 %expand_first.1 = (f32[2,1792]{1,0:T(2,128)S(1)}, bf16[16,1792]{1,0:T(8,128)(2,1)S(1)}, f32[16,3200]{1,0:T(8,128)S(1)}, bf16[16,3328]{1,0:T(8,128)(2,1)S(1)}) custom-call(s32[1]{0:T(128)} %bitcast.group_ref, bf16[1,1792]{1,0:T(2,128)(2,1)S(1)} %broadcast_in_dim.10.gain_ref, bf16[1792,2304]{1,0:T(8,128)(2,1)S(1)} %bitcast.3, bf16[1792,2304]{1,0:T(8,128)(2,1)S(1)} %bitcast.5, ...), custom_call_target="tpu_custom_call" | custom-call | flops 2000000000 | tf_op jit(solution)/shard_map/expand_first/pallas_call | solution.py:382
  43.7 1.1 %collective-permute-start.6 = (bf16[16,3328]{1,0:T(8,128)(2,1)S(1)}, bf16[16,3328]{1,0:T(8,128)(2,1)S(1)}, u32[]{:S(2)}, u32[]{:S(2)}) collective-permute-start(bf16[16,3328]{1,0:T(8,128)(2,1)S(1)} %get-tuple-element.28), channel_id=1, source_target_pairs={{0,2},{1,3},{2,0},{3,1},{4,6},{5,7},{6,4},{7,5},{8,10},{9,11},{10,... | collective-permute-start | bytes 319496 | tf_op jit(solution)/shard_map/ppermute | solution.py:299
  44.8 0.8 %expand_second.1 = (f32[16,1536]{1,0:T(8,128)S(1)}, bf16[16,1536]{1,0:T(8,128)(2,1)S(1)}) custom-call(bf16[16,1792]{1,0:T(8,128)(2,1)S(1)} %get-tuple-element.22.scaled_ref, bf16[1792,2304]{1,0:T(8,128)(2,1)S(1)} %bitcast.3, bf16[1792,2304]{1,0:T(8,128)(2,1)S(1)} %bitcast.5), custom_call_target="tpu_custom_call" | custom-call | flops 2000000000 | tf_op jit(solution)/shard_map/expand_second/pallas_call | solution.py:390
  45.6 0.9 %collective-permute-start.4 = (bf16[16,1536]{1,0:T(8,128)(2,1)S(1)}, bf16[16,1536]{1,0:T(8,128)(2,1)S(1)}, u32[]{:S(2)}, u32[]{:S(2)}) collective-permute-start(bf16[16,1536]{1,0:T(8,128)(2,1)S(1)} %get-tuple-element.24), channel_id=1, source_target_pairs={{0,2},{1,3},{2,0},{3,1},{4,6},{5,7},{6,4},{7,5},{8,10},{9,11},{10,... | collective-permute-start | bytes 147464 | tf_op jit(solution)/shard_map/ppermute | solution.py:299
  46.6 1.8 %collective-permute-done.6.second_ref = bf16[16,3328]{1,0:T(8,128)(2,1)S(1)} collective-permute-done((bf16[16,3328]{1,0:T(8,128)(2,1)S(1)}, bf16[16,3328]{1,0:T(8,128)(2,1)S(1)}, u32[]{:S(2)}, u32[]{:S(2)}) %collective-permute-start.6) | collective-permute-done | bytes 106528 | tf_op jit(solution)/shard_map/ppermute | solution.py:299
  48.4 0.1 merge.3
  48.5 0.0 collective-permute-start.7
  48.5 1.2 %collective-permute-done.4.second_ref = bf16[16,1536]{1,0:T(8,128)(2,1)S(1)} collective-permute-done((bf16[16,1536]{1,0:T(8,128)(2,1)S(1)}, bf16[16,1536]{1,0:T(8,128)(2,1)S(1)}, u32[]{:S(2)}, u32[]{:S(2)}) %collective-permute-start.4) | collective-permute-done | bytes 49184 | tf_op jit(solution)/shard_map/ppermute | solution.py:299
  49.7 0.1 collective-permute-start.5
  49.8 0.0 collective-permute-done.7.arrived_ref
  49.8 0.0 slice-done.4
  49.8 0.0 slice-done.5
  49.9 0.9 %contract_first.1 = (f32[16,128]{1,0:T(8,128)S(1)}, f32[16,1792]{1,0:T(8,128)S(1)}) custom-call(f32[16,3200]{1,0:T(8,128)S(1)} %get-tuple-element.29.own_ref, bf16[16,3328]{1,0:T(8,128)(2,1)S(1)} %collective-permute-done.7.arrived_ref, bf16[2304,1792]{1,0:T(8,128)(2,1)S(1)} %bitcast.7), custom_call_target="tpu_custom_call" | custom-call | flops 1000000000 | tf_op jit(solution)/shard_map/contract_first/pallas_call | solution.py:414
  50.8 0.3 collective-permute-done.5.arrived_ref
  51.0 0.5 contract_second.1
  51.6 9.3 %all_to_all.17 = bf16[8,2,1792]{2,1,0:T(2,128)(2,1)S(1)} all-to-all(bf16[8,2,1792]{2,1,0:T(2,128)(2,1)S(1)} %contract_second.1), channel_id=1, replica_groups=mesh['wide'=8,'narrow'=4] {'wide'}, dimensions={0} | all-to-all | bytes 114688 | tf_op jit(solution)/shard_map/all_to_all | solution.py:428
  60.9 0.1 convert_reduce_fusion
  61.0 0.6 add_convert_fusion
  (15 shorter events, 0.1 us)
Async XLA Ops:
  0.0 15.5 %copy-start = (bf16[2,2048,576]{1,2,0:T(8,128)(2,1)S(1)}, bf16[2,2048,576]{1,2,0:T(8,128)(2,1)}, u32[]{:S(2)}) copy-start(bf16[2,2048,576]{1,2,0:T(8,128)(2,1)} %param.18) | copy-start | bytes 14155780
  0.0 15.5 %copy-start.2 = (bf16[16,128,512]{2,1,0:T(8,128)(2,1)S(1)}, bf16[16,128,512]{2,1,0:T(8,128)(2,1)}, u32[]{:S(2)}) copy-start(bf16[16,128,512]{2,1,0:T(8,128)(2,1)} %key_ref.1) | copy-start | bytes 6291460
  0.0 15.5 %copy-start.3 = (bf16[16,512,128]{2,1,0:T(8,128)(2,1)S(1)}, bf16[16,512,128]{2,1,0:T(8,128)(2,1)}, u32[]{:S(2)}) copy-start(bf16[16,512,128]{2,1,0:T(8,128)(2,1)} %value_ref.1) | copy-start | bytes 6291460
  0.0 15.5 %copy-start.5 = (s32[2]{0:T(128)S(1)}, s32[2]{0:T(128)}, u32[]{:S(2)}) copy-start(s32[2]{0:T(128)} %lengths_ref.1) | copy-start | bytes 28
  0.0 15.5 %copy-start.6 = (s32[16]{0:T(128)S(1)}, s32[16]{0:T(128)}, u32[]{:S(2)}) copy-start(s32[16]{0:T(128)} %rows_ref.3) | copy-start | bytes 196
  15.5 13.5 %copy-start.1 = (bf16[1024,1792]{1,0:T(8,128)(2,1)S(1)}, bf16[1024,1792]{1,0:T(8,128)(2,1)}, u32[]{:S(2)}) copy-start(bf16[1024,1792]{1,0:T(8,128)(2,1)} %weight_ref.3) | copy-start | bytes 11010052
  15.5 13.4 %copy-start.4 = (bf16[2,1792]{1,0:T(2,128)(2,1)S(1)}, bf16[2,1792]{1,0:T(2,128)(2,1)}, u32[]{:S(2)}) copy-start(bf16[2,1792]{1,0:T(2,128)(2,1)} %residual_ref.1) | copy-start | bytes 21508
  18.6 23.5 %slice-start = ((s8[8257536]{0:T(1024)(128)(4,1)}), s8[4194304]{0:T(1024)(128)(4,1)S(1)}, s32[]{:S(2)}) async-start(s8[8257536]{0:T(1024)(128)(4,1)} %bitcast.2), calls=%async_computation.3 | async-start | bytes 8388608
  18.6 23.5 %slice-start.2 = ((s8[8257536]{0:T(1024)(128)(4,1)}), s8[4194304]{0:T(1024)(128)(4,1)S(1)}, s32[]{:S(2)}) async-start(s8[8257536]{0:T(1024)(128)(4,1)} %bitcast.4), calls=%async_computation.5 | async-start | bytes 8388608
  28.9 10.0 %copy-start.7 = (bf16[1792]{0:T(1024)(128)(2,1)S(1)}, bf16[1792]{0:T(1024)(128)(2,1)}, u32[]{:S(2)}) copy-start(bf16[1792]{0:T(1024)(128)(2,1)} %param.22) | copy-start | bytes 10756
  28.9 13.2 %slice-start.1 = ((s8[8257536]{0:T(1024)(128)(4,1)}), s8[4063232]{0:T(1024)(128)(4,1)S(1)}, s32[]{:S(2)}) async-start(s8[8257536]{0:T(1024)(128)(4,1)} %bitcast.2), calls=%async_computation.4 | async-start | bytes 8126464
  29.0 13.2 %slice-start.3 = ((s8[8257536]{0:T(1024)(128)(4,1)}), s8[4063232]{0:T(1024)(128)(4,1)S(1)}, s32[]{:S(2)}) async-start(s8[8257536]{0:T(1024)(128)(4,1)} %bitcast.4), calls=%async_computation.6 | async-start | bytes 8126464
  30.2 4.2 %collective-permute-start = (bf16[16,1792]{1,0:T(8,128)(2,1)S(1)}, bf16[16,1792]{1,0:T(8,128)(2,1)S(1)}, u32[]{:S(2)}, u32[]{:S(2)}) collective-permute-start(bf16[16,1792]{1,0:T(8,128)(2,1)S(1)} %get-tuple-element.20), channel_id=1, source_target_pairs={{0,4},{1,5},{2,6},{3,7},{4,0},{5,1},{6,2},{7,3},{8,12},{9,13},{10,... | collective-permute-start | bytes 172040 | tf_op jit(solution)/shard_map/ppermute | solution.py:287
  34.5 6.1 %collective-permute-start.3 = (bf16[16,1792]{1,0:T(8,128)(2,1)S(1)}, bf16[16,1792]{1,0:T(8,128)(2,1)S(1)}, u32[]{:S(2)}, u32[]{:S(2)}) collective-permute-start(bf16[16,1792]{1,0:T(8,128)(2,1)S(1)} %get-tuple-element.33), channel_id=1, source_target_pairs={{0,24},{1,9},{2,26},{3,11},{4,28},{5,13},{6,30},{7,15},{8,16},{9,1... | collective-permute-start | bytes 172040 | tf_op jit(solution)/shard_map/ppermute | solution.py:287
  35.9 6.2 %collective-permute-start.2 = (bf16[16,1792]{1,0:T(8,128)(2,1)S(1)}, bf16[16,1792]{1,0:T(8,128)(2,1)S(1)}, u32[]{:S(2)}, u32[]{:S(2)}) collective-permute-start(bf16[16,1792]{1,0:T(8,128)(2,1)S(1)} %get-tuple-element.33), channel_id=1, source_target_pairs={{0,16},{1,17},{2,18},{3,19},{4,20},{5,21},{6,22},{7,23},{8,24},{9,... | collective-permute-start | bytes 172040 | tf_op jit(solution)/shard_map/ppermute | solution.py:287
  36.7 5.4 %collective-permute-start.1 = (bf16[16,1792]{1,0:T(8,128)(2,1)S(1)}, bf16[16,1792]{1,0:T(8,128)(2,1)S(1)}, u32[]{:S(2)}, u32[]{:S(2)}) collective-permute-start(bf16[16,1792]{1,0:T(8,128)(2,1)S(1)} %get-tuple-element.33), channel_id=1, source_target_pairs={{0,8},{1,25},{2,10},{3,27},{4,12},{5,29},{6,14},{7,31},{8,0},{9,17... | collective-permute-start | bytes 172040 | tf_op jit(solution)/shard_map/ppermute | solution.py:287
  43.7 4.7 %collective-permute-start.6 = (bf16[16,3328]{1,0:T(8,128)(2,1)S(1)}, bf16[16,3328]{1,0:T(8,128)(2,1)S(1)}, u32[]{:S(2)}, u32[]{:S(2)}) collective-permute-start(bf16[16,3328]{1,0:T(8,128)(2,1)S(1)} %get-tuple-element.28), channel_id=1, source_target_pairs={{0,2},{1,3},{2,0},{3,1},{4,6},{5,7},{6,4},{7,5},{8,10},{9,11},{10,... | collective-permute-start | bytes 319496 | tf_op jit(solution)/shard_map/ppermute | solution.py:299
  44.8 5.0 %slice-start.4 = ((s8[8257536]{0:T(1024)(128)(4,1)}), s8[4194304]{0:T(1024)(128)(4,1)S(1)}, s32[]{:S(2)}) async-start(s8[8257536]{0:T(1024)(128)(4,1)} %bitcast.6), calls=%async_computation.7 | async-start | bytes 8388608
  44.8 5.0 %slice-start.5 = ((s8[8257536]{0:T(1024)(128)(4,1)}), s8[4063232]{0:T(1024)(128)(4,1)S(1)}, s32[]{:S(2)}) async-start(s8[8257536]{0:T(1024)(128)(4,1)} %bitcast.6), calls=%async_computation.8 | async-start | bytes 8126464
  45.6 4.1 %collective-permute-start.4 = (bf16[16,1536]{1,0:T(8,128)(2,1)S(1)}, bf16[16,1536]{1,0:T(8,128)(2,1)S(1)}, u32[]{:S(2)}, u32[]{:S(2)}) collective-permute-start(bf16[16,1536]{1,0:T(8,128)(2,1)S(1)} %get-tuple-element.24), channel_id=1, source_target_pairs={{0,2},{1,3},{2,0},{3,1},{4,6},{5,7},{6,4},{7,5},{8,10},{9,11},{10,... | collective-permute-start | bytes 147464 | tf_op jit(solution)/shard_map/ppermute | solution.py:299
  48.5 1.3 %collective-permute-start.7 = (bf16[16,3328]{1,0:T(8,128)(2,1)S(1)}, bf16[16,3328]{1,0:T(8,128)(2,1)S(1)}, u32[]{:S(2)}, u32[]{:S(2)}) collective-permute-start(bf16[16,3328]{1,0:T(8,128)(2,1)S(1)} %get-tuple-element.30), channel_id=1, source_target_pairs={{0,1},{1,0},{2,3},{3,2},{4,5},{5,4},{6,7},{7,6},{8,9},{9,8},{10,11... | collective-permute-start | bytes 319496 | tf_op jit(solution)/shard_map/ppermute | solution.py:299
  49.7 1.3 %collective-permute-start.5 = (bf16[16,1536]{1,0:T(8,128)(2,1)S(1)}, bf16[16,1536]{1,0:T(8,128)(2,1)S(1)}, u32[]{:S(2)}, u32[]{:S(2)}) collective-permute-start(bf16[16,1536]{1,0:T(8,128)(2,1)S(1)} %get-tuple-element.26), channel_id=1, source_target_pairs={{0,1},{1,0},{2,3},{3,2},{4,5},{5,4},{6,7},{7,6},{8,9},{9,8},{10,11... | collective-permute-start | bytes 147464 | tf_op jit(solution)/shard_map/ppermute | solution.py:299

commit v11 on v10

--- a/solution.py
+++ b/solution.py
@@ -62,6 +62,24 @@
         out_ref[target] = row
 
 
+def place_rows(group, per_block, rows_ref, residual_ref, select_ref, spread_ref):
+    rows, slots = spread_ref.shape[0], residual_ref.shape[0]
+    count = select_ref.shape[0]
+    column = lax.broadcasted_iota(jnp.int32, (1, count), 1)
+    column_row = jnp.zeros((1, count), jnp.int32)
+    for slot in range(rows):
+        column_row = jnp.where(column // per_block == slot, rows_ref[slot], column_row)
+    wanted = column_row + rows * (column % per_block)
+    position = lax.broadcasted_iota(jnp.int32, (count, count), 0)
+    select_ref[...] = jnp.where(position == wanted, 1.0, 0.0).astype(BF16)
+    row = lax.broadcasted_iota(jnp.int32, (rows, 1), 0)
+    spread = jnp.zeros(spread_ref.shape, F32)
+    for slot in range(slots):
+        own = residual_ref[slot : slot + 1, :].astype(F32)
+        spread = jnp.where(row == group * slots + slot, own, spread)
+    spread_ref[...] = spread
+
+
 def attend_kernel(
     narrow,
     blocks,
@@ -73,13 +91,17 @@
     key_ref,
     cache_ref,
     value_ref,
+    residual_ref,
     out_ref,
+    select_ref,
+    spread_ref,
 ):
     slots, latent = cache_ref.shape[0], value_ref.shape[1]
     heads, head_size = key_ref.shape[0], key_ref.shape[1]
     rope = cache_ref.shape[1] - latent
     span = cache_ref.shape[2]
     group = group_ref[0]
+    place_rows(group, heads // blocks, rows_ref, residual_ref, select_ref, spread_ref)
     queries = []
     for slot in range(slots):
         row = rows_ref[group * slots + slot]
@@ -142,35 +164,19 @@
 
 
 def project_kernel(
-    narrow, blocks, rows_ref, group_ref, heads_ref, residual_ref, weight_ref, own_ref, out_ref
+    narrow, blocks, group_ref, heads_ref, select_ref, residual_ref, weight_ref, own_ref, out_ref
 ):
     wide = heads_ref.shape[0] // narrow
-    slots = residual_ref.shape[0]
-    rows = wide * slots
-    per_block = heads_ref.shape[1] // slots
-    head_size = heads_ref.shape[2]
-    group = group_ref[0]
-    holder = group // blocks
+    rows = own_ref.shape[0]
+    holder = group_ref[0] // blocks
     received = jnp.concatenate(
         [heads_ref[source * narrow + holder] for source in range(wide)], axis=0
     )
-    count = rows * per_block
-    column = lax.broadcasted_iota(jnp.int32, (1, count), 1)
-    column_row = jnp.zeros((1, count), jnp.int32)
-    for slot in range(rows):
-        column_row = jnp.where(column // per_block == slot, rows_ref[slot], column_row)
-    wanted = column_row + rows * (column % per_block)
-    position = lax.broadcasted_iota(jnp.int32, (count, count), 0)
-    select = jnp.where(position == wanted, 1.0, 0.0).astype(BF16)
-    ordered = jnp.dot(select, received, preferred_element_type=F32).astype(BF16)
+    ordered = jnp.dot(select_ref[...], received, preferred_element_type=F32).astype(BF16)
     flat = jnp.concatenate(
-        [ordered[head * rows : (head + 1) * rows] for head in range(per_block)], axis=1
-    )
-    total = jnp.dot(flat, weight_ref[...], preferred_element_type=F32)
-    row = lax.broadcasted_iota(jnp.int32, (rows, 1), 0)
-    for slot in range(slots):
-        own = residual_ref[slot : slot + 1, :].astype(F32)
-        total = total + jnp.where(row == group * slots + slot, own, 0.0)
+        [ordered[first : first + rows] for first in range(0, ordered.shape[0], rows)], axis=1
+    )
+    total = residual_ref[...] + jnp.dot(flat, weight_ref[...], preferred_element_type=F32)
     own_ref[...] = total
     out_ref[...] = total.astype(BF16)
 
@@ -339,10 +345,14 @@
     )(group[None], far(query_nope), far(query_rope))
     queries = lax.all_to_all(packed, "wide", 0, 0, tiled=True)
     cache = jnp.swapaxes(latent_cache, 1, 2)
-    heads_out = call(
+    heads_out, select, spread = call(
         functools.partial(attend_kernel, narrow, blocks, scale),
-        pltpu.VMEM((wide * narrow, slots * per_block, head_size), BF16),
-        [SMEM, SMEM, SMEM, VMEM, VMEM, VMEM, VMEM],
+        (
+            pltpu.VMEM((wide * narrow, slots * per_block, head_size), BF16),
+            pltpu.VMEM((rows * per_block, rows * per_block), BF16),
+            pltpu.VMEM((rows, features), F32),
+        ),
+        [SMEM, SMEM, SMEM] + [VMEM] * 5,
         "attend",
         flops=ATTEND,
     )(
@@ -353,15 +363,16 @@
         near(absorb_key),
         near(cache),
         near(absorb_value),
+        residual_in,
     )
     received = lax.all_to_all(heads_out, ("wide", "narrow"), 0, 0, tiled=True)
     total, summed = call(
         functools.partial(project_kernel, narrow, blocks),
         (pltpu.VMEM((rows, features), F32), pltpu.VMEM((rows, features), BF16)),
-        [SMEM, SMEM, VMEM, VMEM, VMEM],
+        [SMEM] + [VMEM] * 4,
         "project",
         flops=PROJECT,
-    )(slot_rows, group[None], received, residual_in, out_proj)
+    )(group[None], received, select, spread, out_proj)
     groups = exchange_groups(wide)
     for index, distances in enumerate(groups):
         others = [

time: 61.8 us -> 61.2 us (level)
  no operation moved by 1% of the time
where the time goes in v11:
time: 61.2 us; the launch traced here: 61 us
  blocking collectives  34.1 us (56%)
  waiting for transfers between devices  10 us (16%)
  Pallas kernels  8.69 us (14%)
  starting transfers between devices  7.25 us (12%)
  other arithmetic  0.68 us (1%)
    all_to_all x1, blocking collectives, shards(): queries = lax.all_to_all(packed, 'wide', 0, 0, tiled=True)  14.5 us
    all_to_all x1, blocking collectives, shards(): received = lax.all_to_all(heads_out, ('wide', 'narrow'), 0, 0, tiled=True)  10.3 us
    all_to_all x1, blocking collectives, shards(): lax.all_to_all(down, 'wide', 0, 0, tiled=True).astype(F32)  9.32 us
    ppermute x4, waiting for transfers between devices, exchange(): return lax.ppermute(array, ('wide', 'narrow'), pairs)  6.67 us
    ppermute x4, starting transfers between devices, exchange(): return lax.ppermute(array, ('wide', 'narrow'), pairs)  5.13 us
    ppermute x4, waiting for transfers between devices, swap(): return lax.ppermute(array, axis, [(i, i ^ distance) for i in range(size)])  3.33 us
    pallas_call x1, Pallas kernels, shards(): call(functools.partial(attend_kernel, narrow, blocks, scale), (pltpu.VMEM...  3.11 us
    ppermute x4, starting transfers between devices, swap(): return lax.ppermute(array, axis, [(i, i ^ distance) for i in range(size)])  2.12 us
  transfers between devices with their start and end apart: 8, of which 6 were waited for; matrix products, arithmetic and copies ran while one was open for 0% of the time, Pallas kernels for 3%

profile of v11, /device:TPU:0, one launch (start us, length us, event | category | flops | bytes accessed | tf_op | source)
XLA Modules:
  0.0 61.0 jit_solution(16432204523910691318)
XLA Ops:
  0.0 0.0 copy-start
  0.0 0.0 copy-start.6
  0.0 1.0 %pack.1 = bf16[8,2,24,128]{3,2,1,0:T(8,128)(2,1)S(1)} custom-call(s32[1]{0:T(128)} %bitcast.group_ref, bf16[2,16,128]{2,1,0:T(8,128)(2,1)} %nope_hbm.1, bf16[2,16,64]{2,1,0:T(8,128)(2,1)} %rope_hbm.1), custom_call_target="tpu_custom_call" | custom-call | flops 10000000000 | tf_op jit(solution)/shard_map/pack/pallas_call | solution.py:334
  1.0 14.5 %all_to_all.15.query_ref = bf16[8,2,24,128]{3,2,1,0:T(8,128)(2,1)S(1)} all-to-all(bf16[8,2,24,128]{3,2,1,0:T(8,128)(2,1)S(1)} %pack.1), channel_id=1, replica_groups=mesh['wide'=8,'narrow'=4] {'wide'}, dimensions={0} | all-to-all | bytes 196608 | tf_op jit(solution)/shard_map/all_to_all | solution.py:346
  15.5 0.0 copy-done
  15.5 0.0 copy-done.2
  15.5 0.0 copy-done.3
  15.5 0.0 copy-done.4
  15.5 0.0 copy-done.5
  15.5 0.0 copy-done.6
  15.5 0.0 copy-start.1
  15.5 3.1 %attend.1 = (bf16[32,16,128]{2,1,0:T(8,128)(2,1)S(1)}, bf16[128,128]{1,0:T(8,128)(2,1)S(1)}, f32[16,1792]{1,0:T(8,128)S(1)}) custom-call(s32[1]{0:T(128)} %bitcast.group_ref, s32[16]{0:T(128)S(1)} %copy-done.5, s32[2]{0:T(128)S(1)} %copy-done.6, bf16[8,2,24,128]{3,2,1,0:T(8,128)(2,1)S(1)} %all_to_all.15.query_ref, bf16[16,128,512]{2,1,0:T(8,128)(2,1)S(1)} %copy-done.2, ...), custom_call_target="tpu_custom_call" | custom-call | flops 15000000512 | tf_op jit(solution)/shard_map/attend/pallas_call | solution.py:348
  18.6 10.3 %all_to_all.16.heads_ref = bf16[32,16,128]{2,1,0:T(8,128)(2,1)S(1)} all-to-all(bf16[32,16,128]{2,1,0:T(8,128)(2,1)S(1)} %get-tuple-element.22), channel_id=1, replica_groups=mesh['wide'=8,'narrow'=4] {'wide','narrow'}, dimensions={0} | all-to-all | bytes 262144 | tf_op jit(solution)/shard_map/all_to_all | solution.py:368
  28.9 0.0 copy-done.1
  28.9 0.0 slice-start.1
  28.9 0.0 slice-start.3
  29.0 0.7 %project.1 = (f32[16,1792]{1,0:T(8,128)S(1)}, bf16[16,1792]{1,0:T(8,128)(2,1)S(1)}) custom-call(s32[1]{0:T(128)} %bitcast.group_ref, bf16[32,16,128]{2,1,0:T(8,128)(2,1)S(1)} %all_to_all.16.heads_ref, bf16[128,128]{1,0:T(8,128)(2,1)S(1)} %get-tuple-element.23.select_ref, f32[16,1792]{1,0:T(8,128)S(1)} %get-tuple-element.24.residual_ref, ...), custom_call_target="tpu_custom_call" | custom-call | flops 12000000000 | tf_op jit(solution)/shard_map/project/pallas_call | solution.py:369
  29.7 0.7 %collective-permute-start = (bf16[16,1792]{1,0:T(8,128)(2,1)S(1)}, bf16[16,1792]{1,0:T(8,128)(2,1)S(1)}, u32[]{:S(2)}, u32[]{:S(2)}) collective-permute-start(bf16[16,1792]{1,0:T(8,128)(2,1)S(1)} %get-tuple-element.26), channel_id=1, source_target_pairs={{0,4},{1,5},{2,6},{3,7},{4,0},{5,1},{6,2},{7,3},{8,12},{9,13},{10,... | collective-permute-start | bytes 172040 | tf_op jit(solution)/shard_map/ppermute | solution.py:293
  30.3 3.5 %collective-permute-done = bf16[16,1792]{1,0:T(8,128)(2,1)S(1)} collective-permute-done((bf16[16,1792]{1,0:T(8,128)(2,1)S(1)}, bf16[16,1792]{1,0:T(8,128)(2,1)S(1)}, u32[]{:S(2)}, u32[]{:S(2)}) %collective-permute-start) | collective-permute-done | bytes 57376 | tf_op jit(solution)/shard_map/ppermute | solution.py:293
  33.9 1.4 %collective-permute-start.3 = (bf16[16,1792]{1,0:T(8,128)(2,1)S(1)}, bf16[16,1792]{1,0:T(8,128)(2,1)S(1)}, u32[]{:S(2)}, u32[]{:S(2)}) collective-permute-start(bf16[16,1792]{1,0:T(8,128)(2,1)S(1)} %get-tuple-element.39), channel_id=1, source_target_pairs={{0,24},{1,9},{2,26},{3,11},{4,28},{5,13},{6,30},{7,15},{8,16},{9,1... | collective-permute-start | bytes 172040 | tf_op jit(solution)/shard_map/ppermute | solution.py:293
  35.3 0.8 %collective-permute-start.2 = (bf16[16,1792]{1,0:T(8,128)(2,1)S(1)}, bf16[16,1792]{1,0:T(8,128)(2,1)S(1)}, u32[]{:S(2)}, u32[]{:S(2)}) collective-permute-start(bf16[16,1792]{1,0:T(8,128)(2,1)S(1)} %get-tuple-element.39), channel_id=1, source_target_pairs={{0,16},{1,17},{2,18},{3,19},{4,20},{5,21},{6,22},{7,23},{8,24},{9,... | collective-permute-start | bytes 172040 | tf_op jit(solution)/shard_map/ppermute | solution.py:293
  36.1 2.3 %collective-permute-start.1 = (bf16[16,1792]{1,0:T(8,128)(2,1)S(1)}, bf16[16,1792]{1,0:T(8,128)(2,1)S(1)}, u32[]{:S(2)}, u32[]{:S(2)}) collective-permute-start(bf16[16,1792]{1,0:T(8,128)(2,1)S(1)} %get-tuple-element.39), channel_id=1, source_target_pairs={{0,8},{1,25},{2,10},{3,27},{4,12},{5,29},{6,14},{7,31},{8,0},{9,17... | collective-permute-start | bytes 172040 | tf_op jit(solution)/shard_map/ppermute | solution.py:293
  38.3 0.0 copy-done.7
  38.3 1.6 %collective-permute-done.3.refs_3_ = bf16[16,1792]{1,0:T(8,128)(2,1)S(1)} collective-permute-done((bf16[16,1792]{1,0:T(8,128)(2,1)S(1)}, bf16[16,1792]{1,0:T(8,128)(2,1)S(1)}, u32[]{:S(2)}, u32[]{:S(2)}) %collective-permute-start.3) | collective-permute-done | bytes 57376 | tf_op jit(solution)/shard_map/ppermute | solution.py:293
  40.0 1.5 %collective-permute-done.2.refs_2_ = bf16[16,1792]{1,0:T(8,128)(2,1)S(1)} collective-permute-done((bf16[16,1792]{1,0:T(8,128)(2,1)S(1)}, bf16[16,1792]{1,0:T(8,128)(2,1)S(1)}, u32[]{:S(2)}, u32[]{:S(2)}) %collective-permute-start.2) | collective-permute-done | bytes 57376 | tf_op jit(solution)/shard_map/ppermute | solution.py:293
  41.5 0.0 collective-permute-done.1.refs_1_
  41.5 0.0 slice-done
  41.5 0.0 slice-done.2
  41.5 0.0 slice-done.1
  41.5 0.0 slice-done.3
  41.5 1.5 %expand_first.1 = (f32[2,1792]{1,0:T(2,128)S(1)}, bf16[16,1792]{1,0:T(8,128)(2,1)S(1)}, f32[16,3200]{1,0:T(8,128)S(1)}, bf16[16,3328]{1,0:T(8,128)(2,1)S(1)}) custom-call(s32[1]{0:T(128)} %bitcast.group_ref, bf16[1,1792]{1,0:T(2,128)(2,1)S(1)} %broadcast_in_dim.10.gain_ref, bf16[1792,2304]{1,0:T(8,128)(2,1)S(1)} %bitcast.3, bf16[1792,2304]{1,0:T(8,128)(2,1)S(1)} %bitcast.5, ...), custom_call_target="tpu_custom_call" | custom-call | flops 2000000000 | tf_op jit(solution)/shard_map/expand_first/pallas_call | solution.py:393
  43.1 1.1 %collective-permute-start.6 = (bf16[16,3328]{1,0:T(8,128)(2,1)S(1)}, bf16[16,3328]{1,0:T(8,128)(2,1)S(1)}, u32[]{:S(2)}, u32[]{:S(2)}) collective-permute-start(bf16[16,3328]{1,0:T(8,128)(2,1)S(1)} %get-tuple-element.34), channel_id=1, source_target_pairs={{0,2},{1,3},{2,0},{3,1},{4,6},{5,7},{6,4},{7,5},{8,10},{9,11},{10,... | collective-permute-start | bytes 319496 | tf_op jit(solution)/shard_map/ppermute | solution.py:305
  44.2 0.8 %expand_second.1 = (f32[16,1536]{1,0:T(8,128)S(1)}, bf16[16,1536]{1,0:T(8,128)(2,1)S(1)}) custom-call(bf16[16,1792]{1,0:T(8,128)(2,1)S(1)} %get-tuple-element.28.scaled_ref, bf16[1792,2304]{1,0:T(8,128)(2,1)S(1)} %bitcast.3, bf16[1792,2304]{1,0:T(8,128)(2,1)S(1)} %bitcast.5), custom_call_target="tpu_custom_call" | custom-call | flops 2000000000 | tf_op jit(solution)/shard_map/expand_second/pallas_call | solution.py:401
  45.0 0.9 %collective-permute-start.4 = (bf16[16,1536]{1,0:T(8,128)(2,1)S(1)}, bf16[16,1536]{1,0:T(8,128)(2,1)S(1)}, u32[]{:S(2)}, u32[]{:S(2)}) collective-permute-start(bf16[16,1536]{1,0:T(8,128)(2,1)S(1)} %get-tuple-element.30), channel_id=1, source_target_pairs={{0,2},{1,3},{2,0},{3,1},{4,6},{5,7},{6,4},{7,5},{8,10},{9,11},{10,... | collective-permute-start | bytes 147464 | tf_op jit(solution)/shard_map/ppermute | solution.py:305
  46.0 1.8 %collective-permute-done.6.second_ref = bf16[16,3328]{1,0:T(8,128)(2,1)S(1)} collective-permute-done((bf16[16,3328]{1,0:T(8,128)(2,1)S(1)}, bf16[16,3328]{1,0:T(8,128)(2,1)S(1)}, u32[]{:S(2)}, u32[]{:S(2)}) %collective-permute-start.6) | collective-permute-done | bytes 106528 | tf_op jit(solution)/shard_map/ppermute | solution.py:305
  47.8 0.1 merge.3
  47.9 0.0 collective-permute-start.7
  47.9 1.2 %collective-permute-done.4.second_ref = bf16[16,1536]{1,0:T(8,128)(2,1)S(1)} collective-permute-done((bf16[16,1536]{1,0:T(8,128)(2,1)S(1)}, bf16[16,1536]{1,0:T(8,128)(2,1)S(1)}, u32[]{:S(2)}, u32[]{:S(2)}) %collective-permute-start.4) | collective-permute-done | bytes 49184 | tf_op jit(solution)/shard_map/ppermute | solution.py:305
  49.1 0.1 collective-permute-start.5
  49.2 0.0 collective-permute-done.7.arrived_ref
  49.2 0.0 slice-done.4
  49.2 0.0 slice-done.5
  49.3 0.9 %contract_first.1 = (f32[16,128]{1,0:T(8,128)S(1)}, f32[16,1792]{1,0:T(8,128)S(1)}) custom-call(f32[16,3200]{1,0:T(8,128)S(1)} %get-tuple-element.35.own_ref, bf16[16,3328]{1,0:T(8,128)(2,1)S(1)} %collective-permute-done.7.arrived_ref, bf16[2304,1792]{1,0:T(8,128)(2,1)S(1)} %bitcast.7), custom_call_target="tpu_custom_call" | custom-call | flops 1000000000 | tf_op jit(solution)/shard_map/contract_first/pallas_call | solution.py:425
  50.2 0.3 collective-permute-done.5.arrived_ref
  50.4 0.5 contract_second.1
  51.0 9.3 %all_to_all.17 = bf16[8,2,1792]{2,1,0:T(2,128)(2,1)S(1)} all-to-all(bf16[8,2,1792]{2,1,0:T(2,128)(2,1)S(1)} %contract_second.1), channel_id=1, replica_groups=mesh['wide'=8,'narrow'=4] {'wide'}, dimensions={0} | all-to-all | bytes 114688 | tf_op jit(solution)/shard_map/all_to_all | solution.py:439
  60.3 0.1 convert_reduce_fusion
  60.4 0.6 add_convert_fusion
  (15 shorter events, 0.1 us)
Async XLA Ops:
  0.0 15.5 %copy-start = (bf16[2,2048,576]{1,2,0:T(8,128)(2,1)S(1)}, bf16[2,2048,576]{1,2,0:T(8,128)(2,1)}, u32[]{:S(2)}) copy-start(bf16[2,2048,576]{1,2,0:T(8,128)(2,1)} %param.18) | copy-start | bytes 14155780
  0.0 15.5 %copy-start.2 = (bf16[16,128,512]{2,1,0:T(8,128)(2,1)S(1)}, bf16[16,128,512]{2,1,0:T(8,128)(2,1)}, u32[]{:S(2)}) copy-start(bf16[16,128,512]{2,1,0:T(8,128)(2,1)} %key_ref.1) | copy-start | bytes 6291460
  0.0 15.5 %copy-start.3 = (bf16[16,512,128]{2,1,0:T(8,128)(2,1)S(1)}, bf16[16,512,128]{2,1,0:T(8,128)(2,1)}, u32[]{:S(2)}) copy-start(bf16[16,512,128]{2,1,0:T(8,128)(2,1)} %value_ref.1) | copy-start | bytes 6291460
  0.0 15.5 %copy-start.4 = (bf16[2,1792]{1,0:T(2,128)(2,1)S(1)}, bf16[2,1792]{1,0:T(2,128)(2,1)}, u32[]{:S(2)}) copy-start(bf16[2,1792]{1,0:T(2,128)(2,1)} %residual_ref.1) | copy-start | bytes 21508
  0.0 15.5 %copy-start.5 = (s32[16]{0:T(128)S(1)}, s32[16]{0:T(128)}, u32[]{:S(2)}) copy-start(s32[16]{0:T(128)} %rows_ref.1) | copy-start | bytes 196
  0.0 15.5 %copy-start.6 = (s32[2]{0:T(128)S(1)}, s32[2]{0:T(128)}, u32[]{:S(2)}) copy-start(s32[2]{0:T(128)} %lengths_ref.1) | copy-start | bytes 28
  15.5 13.4 %copy-start.1 = (bf16[1024,1792]{1,0:T(8,128)(2,1)S(1)}, bf16[1024,1792]{1,0:T(8,128)(2,1)}, u32[]{:S(2)}) copy-start(bf16[1024,1792]{1,0:T(8,128)(2,1)} %weight_ref.3) | copy-start | bytes 11010052
  28.9 12.6 %slice-start = ((s8[8257536]{0:T(1024)(128)(4,1)}), s8[4194304]{0:T(1024)(128)(4,1)S(1)}, s32[]{:S(2)}) async-start(s8[8257536]{0:T(1024)(128)(4,1)} %bitcast.2), calls=%async_computation.3 | async-start | bytes 8388608
  28.9 12.6 %slice-start.2 = ((s8[8257536]{0:T(1024)(128)(4,1)}), s8[4194304]{0:T(1024)(128)(4,1)S(1)}, s32[]{:S(2)}) async-start(s8[8257536]{0:T(1024)(128)(4,1)} %bitcast.4), calls=%async_computation.5 | async-start | bytes 8388608
  28.9 9.4 %copy-start.7 = (bf16[1792]{0:T(1024)(128)(2,1)S(1)}, bf16[1792]{0:T(1024)(128)(2,1)}, u32[]{:S(2)}) copy-start(bf16[1792]{0:T(1024)(128)(2,1)} %param.22) | copy-start | bytes 10756
  28.9 12.6 %slice-start.1 = ((s8[8257536]{0:T(1024)(128)(4,1)}), s8[4063232]{0:T(1024)(128)(4,1)S(1)}, s32[]{:S(2)}) async-start(s8[8257536]{0:T(1024)(128)(4,1)} %bitcast.2), calls=%async_computation.4 | async-start | bytes 8126464
  28.9 12.6 %slice-start.3 = ((s8[8257536]{0:T(1024)(128)(4,1)}), s8[4063232]{0:T(1024)(128)(4,1)S(1)}, s32[]{:S(2)}) async-start(s8[8257536]{0:T(1024)(128)(4,1)} %bitcast.4), calls=%async_computation.6 | async-start | bytes 8126464
  29.7 4.2 %collective-permute-start = (bf16[16,1792]{1,0:T(8,128)(2,1)S(1)}, bf16[16,1792]{1,0:T(8,128)(2,1)S(1)}, u32[]{:S(2)}, u32[]{:S(2)}) collective-permute-start(bf16[16,1792]{1,0:T(8,128)(2,1)S(1)} %get-tuple-element.26), channel_id=1, source_target_pairs={{0,4},{1,5},{2,6},{3,7},{4,0},{5,1},{6,2},{7,3},{8,12},{9,13},{10,... | collective-permute-start | bytes 172040 | tf_op jit(solution)/shard_map/ppermute | solution.py:293
  33.9 6.1 %collective-permute-start.3 = (bf16[16,1792]{1,0:T(8,128)(2,1)S(1)}, bf16[16,1792]{1,0:T(8,128)(2,1)S(1)}, u32[]{:S(2)}, u32[]{:S(2)}) collective-permute-start(bf16[16,1792]{1,0:T(8,128)(2,1)S(1)} %get-tuple-element.39), channel_id=1, source_target_pairs={{0,24},{1,9},{2,26},{3,11},{4,28},{5,13},{6,30},{7,15},{8,16},{9,1... | collective-permute-start | bytes 172040 | tf_op jit(solution)/shard_map/ppermute | solution.py:293
  35.3 6.2 %collective-permute-start.2 = (bf16[16,1792]{1,0:T(8,128)(2,1)S(1)}, bf16[16,1792]{1,0:T(8,128)(2,1)S(1)}, u32[]{:S(2)}, u32[]{:S(2)}) collective-permute-start(bf16[16,1792]{1,0:T(8,128)(2,1)S(1)} %get-tuple-element.39), channel_id=1, source_target_pairs={{0,16},{1,17},{2,18},{3,19},{4,20},{5,21},{6,22},{7,23},{8,24},{9,... | collective-permute-start | bytes 172040 | tf_op jit(solution)/shard_map/ppermute | solution.py:293
  36.1 5.4 %collective-permute-start.1 = (bf16[16,1792]{1,0:T(8,128)(2,1)S(1)}, bf16[16,1792]{1,0:T(8,128)(2,1)S(1)}, u32[]{:S(2)}, u32[]{:S(2)}) collective-permute-start(bf16[16,1792]{1,0:T(8,128)(2,1)S(1)} %get-tuple-element.39), channel_id=1, source_target_pairs={{0,8},{1,25},{2,10},{3,27},{4,12},{5,29},{6,14},{7,31},{8,0},{9,17... | collective-permute-start | bytes 172040 | tf_op jit(solution)/shard_map/ppermute | solution.py:293
  43.1 4.7 %collective-permute-start.6 = (bf16[16,3328]{1,0:T(8,128)(2,1)S(1)}, bf16[16,3328]{1,0:T(8,128)(2,1)S(1)}, u32[]{:S(2)}, u32[]{:S(2)}) collective-permute-start(bf16[16,3328]{1,0:T(8,128)(2,1)S(1)} %get-tuple-element.34), channel_id=1, source_target_pairs={{0,2},{1,3},{2,0},{3,1},{4,6},{5,7},{6,4},{7,5},{8,10},{9,11},{10,... | collective-permute-start | bytes 319496 | tf_op jit(solution)/shard_map/ppermute | solution.py:305
  44.2 5.0 %slice-start.4 = ((s8[8257536]{0:T(1024)(128)(4,1)}), s8[4194304]{0:T(1024)(128)(4,1)S(1)}, s32[]{:S(2)}) async-start(s8[8257536]{0:T(1024)(128)(4,1)} %bitcast.6), calls=%async_computation.7 | async-start | bytes 8388608
  44.2 5.0 %slice-start.5 = ((s8[8257536]{0:T(1024)(128)(4,1)}), s8[4063232]{0:T(1024)(128)(4,1)S(1)}, s32[]{:S(2)}) async-start(s8[8257536]{0:T(1024)(128)(4,1)} %bitcast.6), calls=%async_computation.8 | async-start | bytes 8126464
  45.0 4.1 %collective-permute-start.4 = (bf16[16,1536]{1,0:T(8,128)(2,1)S(1)}, bf16[16,1536]{1,0:T(8,128)(2,1)S(1)}, u32[]{:S(2)}, u32[]{:S(2)}) collective-permute-start(bf16[16,1536]{1,0:T(8,128)(2,1)S(1)} %get-tuple-element.30), channel_id=1, source_target_pairs={{0,2},{1,3},{2,0},{3,1},{4,6},{5,7},{6,4},{7,5},{8,10},{9,11},{10,... | collective-permute-start | bytes 147464 | tf_op jit(solution)/shard_map/ppermute | solution.py:305
  47.9 1.3 %collective-permute-start.7 = (bf16[16,3328]{1,0:T(8,128)(2,1)S(1)}, bf16[16,3328]{1,0:T(8,128)(2,1)S(1)}, u32[]{:S(2)}, u32[]{:S(2)}) collective-permute-start(bf16[16,3328]{1,0:T(8,128)(2,1)S(1)} %get-tuple-element.36), channel_id=1, source_target_pairs={{0,1},{1,0},{2,3},{3,2},{4,5},{5,4},{6,7},{7,6},{8,9},{9,8},{10,11... | collective-permute-start | bytes 319496 | tf_op jit(solution)/shard_map/ppermute | solution.py:305
  49.1 1.3 %collective-permute-start.5 = (bf16[16,1536]{1,0:T(8,128)(2,1)S(1)}, bf16[16,1536]{1,0:T(8,128)(2,1)S(1)}, u32[]{:S(2)}, u32[]{:S(2)}) collective-permute-start(bf16[16,1536]{1,0:T(8,128)(2,1)S(1)} %get-tuple-element.32), channel_id=1, source_target_pairs={{0,1},{1,0},{2,3},{3,2},{4,5},{5,4},{6,7},{7,6},{8,9},{9,8},{10,11... | collective-permute-start | bytes 147464 | tf_op jit(solution)/shard_map/ppermute | solution.py:305

commit v12 on v11

--- a/solution.py
+++ b/solution.py
@@ -9,6 +9,7 @@
 from jax.sharding import PartitionSpec as P
 
 D = 7168
+CHUNK = 512
 BF16 = jnp.bfloat16
 F32 = jnp.float32
 VMEM = pl.BlockSpec(memory_space=pltpu.VMEM)
@@ -263,22 +264,30 @@
     return (gate / (1.0 + jnp.exp(-gate)) * (up * factor)).astype(BF16)
 
 
+def contracted(gate, up, factor, weight_ref, first):
+    total = 0.0
+    for start in range(0, gate.shape[1], CHUNK):
+        part = slice(start, min(start + CHUNK, gate.shape[1]))
+        total = total + jnp.dot(
+            activated(gate[:, part], up[:, part], factor),
+            weight_ref[first + part.start : first + part.stop, :],
+            preferred_element_type=F32,
+        )
+    return total
+
+
 def contract_first_kernel(cut, own_ref, arrived_ref, weight_ref, factor_ref, out_ref):
     gate, up, square = get_terms(cut, own_ref, arrived_ref, True)
     factor = lax.rsqrt(square / D + 1e-06)
     factor_ref[...] = jnp.broadcast_to(factor, factor_ref.shape)
-    out_ref[...] = jnp.dot(
-        activated(gate, up, factor), weight_ref[:cut, :], preferred_element_type=F32
-    )
+    out_ref[...] = contracted(gate, up, factor, weight_ref, 0)
 
 
 def contract_second_kernel(
     cut, own_ref, arrived_ref, weight_ref, factor_ref, partial_ref, out_ref
 ):
     gate, up, _ = get_terms(weight_ref.shape[0] - cut, own_ref, arrived_ref, False)
-    total = partial_ref[...] + jnp.dot(
-        activated(gate, up, factor_ref[:, :1]), weight_ref[cut:, :], preferred_element_type=F32
-    )
+    total = partial_ref[...] + contracted(gate, up, factor_ref[:, :1], weight_ref, cut)
     slots = out_ref.shape[1]
     for owner in range(out_ref.shape[0]):
         out_ref[owner] = total[owner * slots : (owner + 1) * slots].astype(out_ref.dtype)

time: 61.2 us -> 61.2 us (level)
  no operation moved by 1% of the time
where the time goes in v12:
time: 61.2 us; the launch traced here: 61 us
  blocking collectives  34.1 us (56%)
  waiting for transfers between devices  10 us (16%)
  Pallas kernels  8.68 us (14%)
  starting transfers between devices  7.25 us (12%)
  other arithmetic  0.68 us (1%)
    all_to_all x1, blocking collectives, shards(): queries = lax.all_to_all(packed, 'wide', 0, 0, tiled=True)  14.5 us
    all_to_all x1, blocking collectives, shards(): received = lax.all_to_all(heads_out, ('wide', 'narrow'), 0, 0, tiled=True)  10.3 us
    all_to_all x1, blocking collectives, shards(): lax.all_to_all(down, 'wide', 0, 0, tiled=True).astype(F32)  9.32 us
    ppermute x4, waiting for transfers between devices, exchange(): return lax.ppermute(array, ('wide', 'narrow'), pairs)  6.67 us
    ppermute x4, starting transfers between devices, exchange(): return lax.ppermute(array, ('wide', 'narrow'), pairs)  5.13 us
    ppermute x4, waiting for transfers between devices, swap(): return lax.ppermute(array, axis, [(i, i ^ distance) for i in range(size)])  3.34 us
    pallas_call x1, Pallas kernels, shards(): call(functools.partial(attend_kernel, narrow, blocks, scale), (pltpu.VMEM...  3.11 us
    ppermute x4, starting transfers between devices, swap(): return lax.ppermute(array, axis, [(i, i ^ distance) for i in range(size)])  2.12 us
  transfers between devices with their start and end apart: 8, of which 6 were waited for; matrix products, arithmetic and copies ran while one was open for 0% of the time, Pallas kernels for 3%

profile of v12, /device:TPU:0, one launch (start us, length us, event | category | flops | bytes accessed | tf_op | source)
XLA Modules:
  0.0 61.0 jit_solution(6639837601904252619)
XLA Ops:
  0.0 0.0 copy-start.2
  0.0 0.0 copy-start.6
  0.0 1.0 %pack.1 = bf16[8,2,24,128]{3,2,1,0:T(8,128)(2,1)S(1)} custom-call(s32[1]{0:T(128)} %bitcast.group_ref, bf16[2,16,128]{2,1,0:T(8,128)(2,1)} %nope_hbm.1, bf16[2,16,64]{2,1,0:T(8,128)(2,1)} %rope_hbm.1), custom_call_target="tpu_custom_call" | custom-call | flops 10000000000 | tf_op jit(solution)/shard_map/pack/pallas_call | solution.py:343
  1.0 14.5 %all_to_all.15.query_ref = bf16[8,2,24,128]{3,2,1,0:T(8,128)(2,1)S(1)} all-to-all(bf16[8,2,24,128]{3,2,1,0:T(8,128)(2,1)S(1)} %pack.1), channel_id=1, replica_groups=mesh['wide'=8,'narrow'=4] {'wide'}, dimensions={0} | all-to-all | bytes 196608 | tf_op jit(solution)/shard_map/all_to_all | solution.py:355
  15.5 0.0 copy-done
  15.5 0.0 copy-done.2
  15.5 0.0 copy-done.3
  15.5 0.0 copy-done.4
  15.5 0.0 copy-done.5
  15.5 0.0 copy-done.6
  15.5 0.0 copy-start.1
  15.5 3.1 %attend.1 = (bf16[32,16,128]{2,1,0:T(8,128)(2,1)S(1)}, bf16[128,128]{1,0:T(8,128)(2,1)S(1)}, f32[16,1792]{1,0:T(8,128)S(1)}) custom-call(s32[1]{0:T(128)} %bitcast.group_ref, s32[16]{0:T(128)S(1)} %copy-done.5, s32[2]{0:T(128)S(1)} %copy-done.6, bf16[8,2,24,128]{3,2,1,0:T(8,128)(2,1)S(1)} %all_to_all.15.query_ref, bf16[16,128,512]{2,1,0:T(8,128)(2,1)S(1)} %copy-done.2, ...), custom_call_target="tpu_custom_call" | custom-call | flops 15000000512 | tf_op jit(solution)/shard_map/attend/pallas_call | solution.py:357
  18.6 10.3 %all_to_all.16.heads_ref = bf16[32,16,128]{2,1,0:T(8,128)(2,1)S(1)} all-to-all(bf16[32,16,128]{2,1,0:T(8,128)(2,1)S(1)} %get-tuple-element.22), channel_id=1, replica_groups=mesh['wide'=8,'narrow'=4] {'wide','narrow'}, dimensions={0} | all-to-all | bytes 262144 | tf_op jit(solution)/shard_map/all_to_all | solution.py:377
  28.9 0.0 copy-done.1
  28.9 0.0 slice-start.1
  28.9 0.0 slice-start.3
  29.0 0.7 %project.1 = (f32[16,1792]{1,0:T(8,128)S(1)}, bf16[16,1792]{1,0:T(8,128)(2,1)S(1)}) custom-call(s32[1]{0:T(128)} %bitcast.group_ref, bf16[32,16,128]{2,1,0:T(8,128)(2,1)S(1)} %all_to_all.16.heads_ref, bf16[128,128]{1,0:T(8,128)(2,1)S(1)} %get-tuple-element.23.select_ref, f32[16,1792]{1,0:T(8,128)S(1)} %get-tuple-element.24.residual_ref, ...), custom_call_target="tpu_custom_call" | custom-call | flops 12000000000 | tf_op jit(solution)/shard_map/project/pallas_call | solution.py:378
  29.7 0.7 %collective-permute-start = (bf16[16,1792]{1,0:T(8,128)(2,1)S(1)}, bf16[16,1792]{1,0:T(8,128)(2,1)S(1)}, u32[]{:S(2)}, u32[]{:S(2)}) collective-permute-start(bf16[16,1792]{1,0:T(8,128)(2,1)S(1)} %get-tuple-element.26), channel_id=1, source_target_pairs={{0,4},{1,5},{2,6},{3,7},{4,0},{5,1},{6,2},{7,3},{8,12},{9,13},{10,... | collective-permute-start | bytes 172040 | tf_op jit(solution)/shard_map/ppermute | solution.py:302
  30.3 3.5 %collective-permute-done = bf16[16,1792]{1,0:T(8,128)(2,1)S(1)} collective-permute-done((bf16[16,1792]{1,0:T(8,128)(2,1)S(1)}, bf16[16,1792]{1,0:T(8,128)(2,1)S(1)}, u32[]{:S(2)}, u32[]{:S(2)}) %collective-permute-start) | collective-permute-done | bytes 57376 | tf_op jit(solution)/shard_map/ppermute | solution.py:302
  33.9 1.4 %collective-permute-start.3 = (bf16[16,1792]{1,0:T(8,128)(2,1)S(1)}, bf16[16,1792]{1,0:T(8,128)(2,1)S(1)}, u32[]{:S(2)}, u32[]{:S(2)}) collective-permute-start(bf16[16,1792]{1,0:T(8,128)(2,1)S(1)} %get-tuple-element.39), channel_id=1, source_target_pairs={{0,24},{1,9},{2,26},{3,11},{4,28},{5,13},{6,30},{7,15},{8,16},{9,1... | collective-permute-start | bytes 172040 | tf_op jit(solution)/shard_map/ppermute | solution.py:302
  35.3 0.8 %collective-permute-start.2 = (bf16[16,1792]{1,0:T(8,128)(2,1)S(1)}, bf16[16,1792]{1,0:T(8,128)(2,1)S(1)}, u32[]{:S(2)}, u32[]{:S(2)}) collective-permute-start(bf16[16,1792]{1,0:T(8,128)(2,1)S(1)} %get-tuple-element.39), channel_id=1, source_target_pairs={{0,16},{1,17},{2,18},{3,19},{4,20},{5,21},{6,22},{7,23},{8,24},{9,... | collective-permute-start | bytes 172040 | tf_op jit(solution)/shard_map/ppermute | solution.py:302
  36.1 2.3 %collective-permute-start.1 = (bf16[16,1792]{1,0:T(8,128)(2,1)S(1)}, bf16[16,1792]{1,0:T(8,128)(2,1)S(1)}, u32[]{:S(2)}, u32[]{:S(2)}) collective-permute-start(bf16[16,1792]{1,0:T(8,128)(2,1)S(1)} %get-tuple-element.39), channel_id=1, source_target_pairs={{0,8},{1,25},{2,10},{3,27},{4,12},{5,29},{6,14},{7,31},{8,0},{9,17... | collective-permute-start | bytes 172040 | tf_op jit(solution)/shard_map/ppermute | solution.py:302
  38.3 0.0 copy-done.7
  38.3 1.6 %collective-permute-done.3.refs_3_ = bf16[16,1792]{1,0:T(8,128)(2,1)S(1)} collective-permute-done((bf16[16,1792]{1,0:T(8,128)(2,1)S(1)}, bf16[16,1792]{1,0:T(8,128)(2,1)S(1)}, u32[]{:S(2)}, u32[]{:S(2)}) %collective-permute-start.3) | collective-permute-done | bytes 57376 | tf_op jit(solution)/shard_map/ppermute | solution.py:302
  40.0 1.5 %collective-permute-done.2.refs_2_ = bf16[16,1792]{1,0:T(8,128)(2,1)S(1)} collective-permute-done((bf16[16,1792]{1,0:T(8,128)(2,1)S(1)}, bf16[16,1792]{1,0:T(8,128)(2,1)S(1)}, u32[]{:S(2)}, u32[]{:S(2)}) %collective-permute-start.2) | collective-permute-done | bytes 57376 | tf_op jit(solution)/shard_map/ppermute | solution.py:302
  41.5 0.0 collective-permute-done.1.refs_1_
  41.5 0.0 slice-done
  41.5 0.0 slice-done.2
  41.5 0.0 slice-done.1
  41.5 0.0 slice-done.3
  41.5 1.5 %expand_first.1 = (f32[2,1792]{1,0:T(2,128)S(1)}, bf16[16,1792]{1,0:T(8,128)(2,1)S(1)}, f32[16,3200]{1,0:T(8,128)S(1)}, bf16[16,3328]{1,0:T(8,128)(2,1)S(1)}) custom-call(s32[1]{0:T(128)} %bitcast.group_ref, bf16[1,1792]{1,0:T(2,128)(2,1)S(1)} %broadcast_in_dim.10.gain_ref, bf16[1792,2304]{1,0:T(8,128)(2,1)S(1)} %bitcast.3, bf16[1792,2304]{1,0:T(8,128)(2,1)S(1)} %bitcast.5, ...), custom_call_target="tpu_custom_call" | custom-call | flops 2000000000 | tf_op jit(solution)/shard_map/expand_first/pallas_call | solution.py:402
  43.1 1.1 %collective-permute-start.6 = (bf16[16,3328]{1,0:T(8,128)(2,1)S(1)}, bf16[16,3328]{1,0:T(8,128)(2,1)S(1)}, u32[]{:S(2)}, u32[]{:S(2)}) collective-permute-start(bf16[16,3328]{1,0:T(8,128)(2,1)S(1)} %get-tuple-element.34), channel_id=1, source_target_pairs={{0,2},{1,3},{2,0},{3,1},{4,6},{5,7},{6,4},{7,5},{8,10},{9,11},{10,... | collective-permute-start | bytes 319496 | tf_op jit(solution)/shard_map/ppermute | solution.py:314
  44.2 0.8 %expand_second.1 = (f32[16,1536]{1,0:T(8,128)S(1)}, bf16[16,1536]{1,0:T(8,128)(2,1)S(1)}) custom-call(bf16[16,1792]{1,0:T(8,128)(2,1)S(1)} %get-tuple-element.28.scaled_ref, bf16[1792,2304]{1,0:T(8,128)(2,1)S(1)} %bitcast.3, bf16[1792,2304]{1,0:T(8,128)(2,1)S(1)} %bitcast.5), custom_call_target="tpu_custom_call" | custom-call | flops 2000000000 | tf_op jit(solution)/shard_map/expand_second/pallas_call | solution.py:410
  45.0 0.9 %collective-permute-start.4 = (bf16[16,1536]{1,0:T(8,128)(2,1)S(1)}, bf16[16,1536]{1,0:T(8,128)(2,1)S(1)}, u32[]{:S(2)}, u32[]{:S(2)}) collective-permute-start(bf16[16,1536]{1,0:T(8,128)(2,1)S(1)} %get-tuple-element.30), channel_id=1, source_target_pairs={{0,2},{1,3},{2,0},{3,1},{4,6},{5,7},{6,4},{7,5},{8,10},{9,11},{10,... | collective-permute-start | bytes 147464 | tf_op jit(solution)/shard_map/ppermute | solution.py:314
  46.0 1.8 %collective-permute-done.6.second_ref = bf16[16,3328]{1,0:T(8,128)(2,1)S(1)} collective-permute-done((bf16[16,3328]{1,0:T(8,128)(2,1)S(1)}, bf16[16,3328]{1,0:T(8,128)(2,1)S(1)}, u32[]{:S(2)}, u32[]{:S(2)}) %collective-permute-start.6) | collective-permute-done | bytes 106528 | tf_op jit(solution)/shard_map/ppermute | solution.py:314
  47.8 0.1 merge.3
  47.9 0.0 collective-permute-start.7
  47.9 1.2 %collective-permute-done.4.second_ref = bf16[16,1536]{1,0:T(8,128)(2,1)S(1)} collective-permute-done((bf16[16,1536]{1,0:T(8,128)(2,1)S(1)}, bf16[16,1536]{1,0:T(8,128)(2,1)S(1)}, u32[]{:S(2)}, u32[]{:S(2)}) %collective-permute-start.4) | collective-permute-done | bytes 49184 | tf_op jit(solution)/shard_map/ppermute | solution.py:314
  49.1 0.1 collective-permute-start.5
  49.2 0.0 collective-permute-done.7.arrived_ref
  49.2 0.0 slice-done.4
  49.2 0.0 slice-done.5
  49.3 0.9 %contract_first.1 = (f32[16,128]{1,0:T(8,128)S(1)}, f32[16,1792]{1,0:T(8,128)S(1)}) custom-call(f32[16,3200]{1,0:T(8,128)S(1)} %get-tuple-element.35.own_ref, bf16[16,3328]{1,0:T(8,128)(2,1)S(1)} %collective-permute-done.7.arrived_ref, bf16[2304,1792]{1,0:T(8,128)(2,1)S(1)} %bitcast.7), custom_call_target="tpu_custom_call" | custom-call | flops 1000000000 | tf_op jit(solution)/shard_map/contract_first/pallas_call | solution.py:434
  50.2 0.3 collective-permute-done.5.arrived_ref
  50.4 0.5 contract_second.1
  51.0 9.3 %all_to_all.17 = bf16[8,2,1792]{2,1,0:T(2,128)(2,1)S(1)} all-to-all(bf16[8,2,1792]{2,1,0:T(2,128)(2,1)S(1)} %contract_second.1), channel_id=1, replica_groups=mesh['wide'=8,'narrow'=4] {'wide'}, dimensions={0} | all-to-all | bytes 114688 | tf_op jit(solution)/shard_map/all_to_all | solution.py:448
  60.3 0.1 convert_reduce_fusion
  60.4 0.6 add_convert_fusion
  (15 shorter events, 0.1 us)
Async XLA Ops:
  0.0 15.5 %copy-start = (bf16[2,2048,576]{1,2,0:T(8,128)(2,1)S(1)}, bf16[2,2048,576]{1,2,0:T(8,128)(2,1)}, u32[]{:S(2)}) copy-start(bf16[2,2048,576]{1,2,0:T(8,128)(2,1)} %param.18) | copy-start | bytes 14155780
  0.0 15.5 %copy-start.2 = (bf16[16,128,512]{2,1,0:T(8,128)(2,1)S(1)}, bf16[16,128,512]{2,1,0:T(8,128)(2,1)}, u32[]{:S(2)}) copy-start(bf16[16,128,512]{2,1,0:T(8,128)(2,1)} %key_ref.1) | copy-start | bytes 6291460
  0.0 15.5 %copy-start.3 = (bf16[16,512,128]{2,1,0:T(8,128)(2,1)S(1)}, bf16[16,512,128]{2,1,0:T(8,128)(2,1)}, u32[]{:S(2)}) copy-start(bf16[16,512,128]{2,1,0:T(8,128)(2,1)} %value_ref.1) | copy-start | bytes 6291460
  0.0 15.5 %copy-start.4 = (bf16[2,1792]{1,0:T(2,128)(2,1)S(1)}, bf16[2,1792]{1,0:T(2,128)(2,1)}, u32[]{:S(2)}) copy-start(bf16[2,1792]{1,0:T(2,128)(2,1)} %residual_ref.1) | copy-start | bytes 21508
  0.0 15.5 %copy-start.5 = (s32[16]{0:T(128)S(1)}, s32[16]{0:T(128)}, u32[]{:S(2)}) copy-start(s32[16]{0:T(128)} %rows_ref.1) | copy-start | bytes 196
  0.0 15.5 %copy-start.6 = (s32[2]{0:T(128)S(1)}, s32[2]{0:T(128)}, u32[]{:S(2)}) copy-start(s32[2]{0:T(128)} %lengths_ref.1) | copy-start | bytes 28
  15.5 13.4 %copy-start.1 = (bf16[1024,1792]{1,0:T(8,128)(2,1)S(1)}, bf16[1024,1792]{1,0:T(8,128)(2,1)}, u32[]{:S(2)}) copy-start(bf16[1024,1792]{1,0:T(8,128)(2,1)} %weight_ref.3) | copy-start | bytes 11010052
  28.9 12.6 %slice-start = ((s8[8257536]{0:T(1024)(128)(4,1)}), s8[4194304]{0:T(1024)(128)(4,1)S(1)}, s32[]{:S(2)}) async-start(s8[8257536]{0:T(1024)(128)(4,1)} %bitcast.2), calls=%async_computation.3 | async-start | bytes 8388608
  28.9 12.6 %slice-start.2 = ((s8[8257536]{0:T(1024)(128)(4,1)}), s8[4194304]{0:T(1024)(128)(4,1)S(1)}, s32[]{:S(2)}) async-start(s8[8257536]{0:T(1024)(128)(4,1)} %bitcast.4), calls=%async_computation.5 | async-start | bytes 8388608
  28.9 9.4 %copy-start.7 = (bf16[1792]{0:T(1024)(128)(2,1)S(1)}, bf16[1792]{0:T(1024)(128)(2,1)}, u32[]{:S(2)}) copy-start(bf16[1792]{0:T(1024)(128)(2,1)} %param.22) | copy-start | bytes 10756
  28.9 12.6 %slice-start.1 = ((s8[8257536]{0:T(1024)(128)(4,1)}), s8[4063232]{0:T(1024)(128)(4,1)S(1)}, s32[]{:S(2)}) async-start(s8[8257536]{0:T(1024)(128)(4,1)} %bitcast.2), calls=%async_computation.4 | async-start | bytes 8126464
  28.9 12.6 %slice-start.3 = ((s8[8257536]{0:T(1024)(128)(4,1)}), s8[4063232]{0:T(1024)(128)(4,1)S(1)}, s32[]{:S(2)}) async-start(s8[8257536]{0:T(1024)(128)(4,1)} %bitcast.4), calls=%async_computation.6 | async-start | bytes 8126464
  29.7 4.2 %collective-permute-start = (bf16[16,1792]{1,0:T(8,128)(2,1)S(1)}, bf16[16,1792]{1,0:T(8,128)(2,1)S(1)}, u32[]{:S(2)}, u32[]{:S(2)}) collective-permute-start(bf16[16,1792]{1,0:T(8,128)(2,1)S(1)} %get-tuple-element.26), channel_id=1, source_target_pairs={{0,4},{1,5},{2,6},{3,7},{4,0},{5,1},{6,2},{7,3},{8,12},{9,13},{10,... | collective-permute-start | bytes 172040 | tf_op jit(solution)/shard_map/ppermute | solution.py:302
  33.9 6.1 %collective-permute-start.3 = (bf16[16,1792]{1,0:T(8,128)(2,1)S(1)}, bf16[16,1792]{1,0:T(8,128)(2,1)S(1)}, u32[]{:S(2)}, u32[]{:S(2)}) collective-permute-start(bf16[16,1792]{1,0:T(8,128)(2,1)S(1)} %get-tuple-element.39), channel_id=1, source_target_pairs={{0,24},{1,9},{2,26},{3,11},{4,28},{5,13},{6,30},{7,15},{8,16},{9,1... | collective-permute-start | bytes 172040 | tf_op jit(solution)/shard_map/ppermute | solution.py:302
  35.3 6.2 %collective-permute-start.2 = (bf16[16,1792]{1,0:T(8,128)(2,1)S(1)}, bf16[16,1792]{1,0:T(8,128)(2,1)S(1)}, u32[]{:S(2)}, u32[]{:S(2)}) collective-permute-start(bf16[16,1792]{1,0:T(8,128)(2,1)S(1)} %get-tuple-element.39), channel_id=1, source_target_pairs={{0,16},{1,17},{2,18},{3,19},{4,20},{5,21},{6,22},{7,23},{8,24},{9,... | collective-permute-start | bytes 172040 | tf_op jit(solution)/shard_map/ppermute | solution.py:302
  36.1 5.4 %collective-permute-start.1 = (bf16[16,1792]{1,0:T(8,128)(2,1)S(1)}, bf16[16,1792]{1,0:T(8,128)(2,1)S(1)}, u32[]{:S(2)}, u32[]{:S(2)}) collective-permute-start(bf16[16,1792]{1,0:T(8,128)(2,1)S(1)} %get-tuple-element.39), channel_id=1, source_target_pairs={{0,8},{1,25},{2,10},{3,27},{4,12},{5,29},{6,14},{7,31},{8,0},{9,17... | collective-permute-start | bytes 172040 | tf_op jit(solution)/shard_map/ppermute | solution.py:302
  43.1 4.7 %collective-permute-start.6 = (bf16[16,3328]{1,0:T(8,128)(2,1)S(1)}, bf16[16,3328]{1,0:T(8,128)(2,1)S(1)}, u32[]{:S(2)}, u32[]{:S(2)}) collective-permute-start(bf16[16,3328]{1,0:T(8,128)(2,1)S(1)} %get-tuple-element.34), channel_id=1, source_target_pairs={{0,2},{1,3},{2,0},{3,1},{4,6},{5,7},{6,4},{7,5},{8,10},{9,11},{10,... | collective-permute-start | bytes 319496 | tf_op jit(solution)/shard_map/ppermute | solution.py:314
  44.2 5.0 %slice-start.4 = ((s8[8257536]{0:T(1024)(128)(4,1)}), s8[4194304]{0:T(1024)(128)(4,1)S(1)}, s32[]{:S(2)}) async-start(s8[8257536]{0:T(1024)(128)(4,1)} %bitcast.6), calls=%async_computation.7 | async-start | bytes 8388608
  44.2 5.0 %slice-start.5 = ((s8[8257536]{0:T(1024)(128)(4,1)}), s8[4063232]{0:T(1024)(128)(4,1)S(1)}, s32[]{:S(2)}) async-start(s8[8257536]{0:T(1024)(128)(4,1)} %bitcast.6), calls=%async_computation.8 | async-start | bytes 8126464
  45.0 4.1 %collective-permute-start.4 = (bf16[16,1536]{1,0:T(8,128)(2,1)S(1)}, bf16[16,1536]{1,0:T(8,128)(2,1)S(1)}, u32[]{:S(2)}, u32[]{:S(2)}) collective-permute-start(bf16[16,1536]{1,0:T(8,128)(2,1)S(1)} %get-tuple-element.30), channel_id=1, source_target_pairs={{0,2},{1,3},{2,0},{3,1},{4,6},{5,7},{6,4},{7,5},{8,10},{9,11},{10,... | collective-permute-start | bytes 147464 | tf_op jit(solution)/shard_map/ppermute | solution.py:314
  47.9 1.3 %collective-permute-start.7 = (bf16[16,3328]{1,0:T(8,128)(2,1)S(1)}, bf16[16,3328]{1,0:T(8,128)(2,1)S(1)}, u32[]{:S(2)}, u32[]{:S(2)}) collective-permute-start(bf16[16,3328]{1,0:T(8,128)(2,1)S(1)} %get-tuple-element.36), channel_id=1, source_target_pairs={{0,1},{1,0},{2,3},{3,2},{4,5},{5,4},{6,7},{7,6},{8,9},{9,8},{10,11... | collective-permute-start | bytes 319496 | tf_op jit(solution)/shard_map/ppermute | solution.py:314
  49.1 1.3 %collective-permute-start.5 = (bf16[16,1536]{1,0:T(8,128)(2,1)S(1)}, bf16[16,1536]{1,0:T(8,128)(2,1)S(1)}, u32[]{:S(2)}, u32[]{:S(2)}) collective-permute-start(bf16[16,1536]{1,0:T(8,128)(2,1)S(1)} %get-tuple-element.32), channel_id=1, source_target_pairs={{0,1},{1,0},{2,3},{3,2},{4,5},{5,4},{6,7},{7,6},{8,9},{9,8},{10,11... | collective-permute-start | bytes 147464 | tf_op jit(solution)/shard_map/ppermute | solution.py:314
